TPU v7x, 128 devices: a whole 4x4x4 slice. The times are simulated.
128 devices in a mesh: gx: 16 (over z, y), gy: 8 (over x, core).
Axes of the slice: x: 4, y: 4, z: 4, core: 2. Of those that a mesh axis runs over, the one named last changes fastest.
Arguments:
- enthalpy: float32 [1024, 1024, 128], P('gx', 'gy'), may hold values from 0 to 2.5
- conductivity: float32 [1024, 1024, 128], P('gx', 'gy'), may hold values from 0.5 to 1.5
- bead_enthalpy: float32 [1024, 1024, 128], P('gx', 'gy'), may hold values from 2 to 3
- birth_time: int32 [1024, 1024, 128], P('gx', 'gy'), may hold values from -2000 to 7999
- send_rows: int32 [16, 8, 128, 32], P('gx', 'gy'), may hold values from 0 to 8191
- send_counts: int32 [16, 8, 128], P('gx', 'gy'), may hold values from 0 to 32, as said below
Outputs:
- enthalpy_end: float32 [1024, 1024, 128], P('gx', 'gy')
- owner_rows: float32 [524288, 128], P(('gx', 'gy'))
Inputs may be any that keep to these rules, and one draw needn't show every extreme that they name: `send_counts`: in every draw one owner receives 32 rows from every tile.
All inputs are finite; a program needn't handle non-finite values.
Results may differ from a plain program's by a relative error of at most 0.0003.
Values sent between devices are 32-bit elements; how exact they have to be, the bound alone decides.
No kernel may reach another device: no remote copies, remote signals or barrier semaphores. Data moves between devices by JAX's collectives and lax.ppermute only.
A program may use at most 192 MiB of HBM per device.

v0:
```python
import jax
import jax.numpy as jnp
from jax import lax
from jax.sharding import PartitionSpec as P

STEPS = 3
TICKS = 2000


LATENT = 0.5
RATE = 0.08


def padded(block, sides, width):
    for axis, dim in sides:
        count = lax.axis_size(axis)
        forward = [(i, i + 1) for i in range(count - 1)]
        backward = [(target, source) for source, target in forward]
        low = lax.ppermute(
            lax.slice_in_dim(block, block.shape[dim] - width, None, axis=dim), axis, forward
        )
        high = lax.ppermute(lax.slice_in_dim(block, 0, width, axis=dim), axis, backward)
        block = jnp.concatenate([low, block, high], axis=dim)
    return block


def heat_content_into_kelvin(heat_content_latest):
    return jnp.minimum(heat_content_latest, 1.0) + jnp.maximum(
        heat_content_latest - 1.0 - LATENT, 0.0
    )


def face_flux(c_one, c_two, a_one, a_two, t_one, t_two):
    return 2.0 * c_one * c_two / (c_one + c_two) * (a_one * a_two) * (t_two - t_one)


def advance(enthalpy_pad, bordered_diffusivity, bead_pad, birth_pad, inside, step):
    in_grid = inside > 0.5
    born_now = (
        in_grid & (birth_pad >= float(step * TICKS)) & (birth_pad < float((step + 1) * TICKS))
    )
    present_heat_content = jnp.where(born_now, bead_pad, enthalpy_pad)
    standing_share = jnp.clip(float(step + 1) - birth_pad / float(TICKS), 0.0, 1.0)
    active = jnp.where(in_grid, standing_share, 0.0)
    kelvin_grid_values = heat_content_into_kelvin(present_heat_content)
    heat_diffusivity_grid = bordered_diffusivity * (0.5 + 0.25 * kelvin_grid_values)
    c_mid = heat_diffusivity_grid[1:-1, 1:-1]
    a_mid = active[1:-1, 1:-1]
    central_kelvin_value = kelvin_grid_values[1:-1, 1:-1]
    net_flux = jnp.zeros(c_mid.shape, jnp.float32)
    cuts = (
        (slice(2, None), slice(1, -1)),
        (slice(None, -2), slice(1, -1)),
        (slice(1, -1), slice(2, None)),
        (slice(1, -1), slice(None, -2)),
    )
    for track_limit_index, lateral_limit_index in cuts:
        net_flux = net_flux + face_flux(
            c_mid,
            heat_diffusivity_grid[track_limit_index, lateral_limit_index],
            a_mid,
            active[track_limit_index, lateral_limit_index],
            central_kelvin_value,
            kelvin_grid_values[track_limit_index, lateral_limit_index],
        )
    z_flux = face_flux(
        c_mid[..., :-1],
        c_mid[..., 1:],
        a_mid[..., :-1],
        a_mid[..., 1:],
        central_kelvin_value[..., :-1],
        central_kelvin_value[..., 1:],
    )
    z_edge = jnp.zeros(z_flux.shape[:-1] + (1,), jnp.float32)
    net_flux = (
        net_flux + jnp.concatenate([z_flux, z_edge], -1) - jnp.concatenate([z_edge, z_flux], -1)
    )
    return present_heat_content[1:-1, 1:-1] + RATE * net_flux


def grid_inside(track_cells, lateral_cells, margin):
    track_global = (
        lax.axis_index("gx") * track_cells
        + jnp.arange(track_cells + 2 * margin, dtype=jnp.int32)
        - margin
    )
    lateral_global = (
        lax.axis_index("gy") * lateral_cells
        + jnp.arange(lateral_cells + 2 * margin, dtype=jnp.int32)
        - margin
    )
    track_inside = (track_global >= 0) & (track_global < lax.axis_size("gx") * track_cells)
    lateral_inside = (lateral_global >= 0) & (lateral_global < lax.axis_size("gy") * lateral_cells)
    return (track_inside[:, None] & lateral_inside[None, :]).astype(jnp.float32)[..., None]


def per_device(enthalpy, conductivity, bead_enthalpy, birth_time, send_rows, send_counts):
    rim_width = 1
    statics = jnp.stack([conductivity, bead_enthalpy, birth_time.astype(jnp.float32)])
    static_pad = padded(statics, (("gx", 1), ("gy", 2)), rim_width)
    inside = grid_inside(enthalpy.shape[0], enthalpy.shape[1], rim_width)
    bordered_diffusivity = jnp.where(inside > 0.5, static_pad[0], 1.0)
    bead_pad = static_pad[1]
    birth_pad = static_pad[2]
    present_heat_content = enthalpy
    for step in range(STEPS):
        widened = padded(present_heat_content, (("gx", 0), ("gy", 1)), 1)
        present_heat_content = advance(
            widened, bordered_diffusivity, bead_pad, birth_pad, inside, step
        )
    kelvin_grid_values = heat_content_into_kelvin(present_heat_content)
    layer_count_vertical = kelvin_grid_values.shape[-1]
    integration_point_matrix = kelvin_grid_values.reshape(-1, layer_count_vertical)
    send_list = send_rows[0, 0]
    send_num = send_counts[0, 0]
    slot_total = send_list.shape[1]
    picked = integration_point_matrix[send_list]
    slot_index = jnp.arange(slot_total, dtype=jnp.int32)
    keep_slot = slot_index[None, :] < send_num[:, None]
    outgoing = jnp.where(keep_slot[..., None], picked, 0.0)
    received = lax.all_to_all(outgoing, ("gx", "gy"), split_axis=0, concat_axis=0, tiled=True)
    return (present_heat_content, received.reshape(-1, layer_count_vertical))


def solution(mesh):
    in_specs = (
        P("gx", "gy", None),
        P("gx", "gy", None),
        P("gx", "gy", None),
        P("gx", "gy", None),
        P("gx", "gy", None, None),
        P("gx", "gy", None),
    )
    out_specs = (P("gx", "gy", None), P(("gx", "gy"), None))
    return jax.shard_map(
        per_device, mesh=mesh, in_specs=in_specs, out_specs=out_specs, check_vma=False
    )
```

profile of v0, /device:TPU:1, one launch (start us, length us, event | category | flops | bytes accessed | tf_op | source)
XLA Modules:
  0.0 243.2 jit_solution(8441462213558989810)
XLA Ops:
  0.7 2.7 %convert_bitcast_fusion = f32[1,64,128,128]{3,2,1,0:T(8,128)S(1)} fusion(s32[64,128,128]{2,1,0:T(8,128)} %param.9), kind=kLoop, calls=%fused_computation.117 | loop fusion | flops 1048576 | bytes 8388608 | tf_op jit(solution)/shard_map/stack | solution.py:99
  4.1 2.8 %copy-done.8 = f32[64,128,128]{2,1,0:T(8,128)S(1)} copy-done((f32[64,128,128]{2,1,0:T(8,128)S(1)}, f32[64,128,128]{2,1,0:T(8,128)}, u32[]{:S(2)}) %copy-start.8) | copy-done | bytes 4194328
  6.9 4.0 %collective-permute-start = (f32[3,1,128,128]{3,2,1,0:T(8,128)S(1)}, f32[3,1,128,128]{3,2,1,0:T(8,128)S(1)}, u32[]{:S(2)}, u32[]{:S(2)}) collective-permute-start(f32[3,1,128,128]{3,2,1,0:T(8,128)S(1)} %get-tuple-element.15), channel_id=1, source_target_pairs={{0,8},{8,16},{16,24},{24,32},{32,40},{40,48},{48,56},{56,64},{64,7... | collective-permute-start | bytes 589832 | tf_op jit(solution)/shard_map/ppermute | solution.py:19
  13.2 4.0 %collective-permute-start.4 = (f32[1,128,128]{2,1,0:T(8,128)S(1)}, f32[1,128,128]{2,1,0:T(8,128)S(1)}, u32[]{:S(2)}, u32[]{:S(2)}) collective-permute-start(f32[1,128,128]{2,1,0:T(8,128)S(1)} %get-tuple-element.28), channel_id=1, source_target_pairs={{0,8},{8,16},{16,24},{24,32},{32,40},{40,48},{48,56},{56,64},{64,7... | collective-permute-start | bytes 196616 | tf_op jit(solution)/shard_map/ppermute | solution.py:19
  18.6 2.8 %constant_dynamic-update-slice_fusion.1 = f32[66,128,128]{2,1,0:T(8,128)S(1)} fusion(f32[66,128,128]{2,1,0:T(8,128)S(1)} %constant_dynamic-update-slice_fusion.2, f32[64,128,128]{2,1,0:T(8,128)} %param.6), kind=kLoop, calls=%fused_computation.138 | loop fusion | bytes 8388608
  24.7 5.0 %collective-permute-start.2 = (f32[3,66,1,128]{3,2,1,0:T(1,128)S(1)}, f32[3,66,1,128]{3,2,1,0:T(1,128)S(1)}, u32[]{:S(2)}, u32[]{:S(2)}) collective-permute-start(f32[3,66,1,128]{3,2,1,0:T(1,128)S(1)} %get-tuple-element.13), channel_id=1, source_target_pairs={{0,1},{1,2},{2,3},{3,4},{4,5},{5,6},{6,7},{8,9},{9,10},{10,11},{11... | collective-permute-start | bytes 304136 | tf_op jit(solution)/shard_map/ppermute | solution.py:19
  29.7 1.9 collective-permute-start.3
  31.7 3.6 %collective-permute-start.6 = (f32[66,1,128]{2,1,0:T(1,128)S(1)}, f32[66,1,128]{2,1,0:T(1,128)S(1)}, u32[]{:S(2)}, u32[]{:S(2)}) collective-permute-start(f32[66,1,128]{2,1,0:T(1,128)S(1)} %get-tuple-element.21), channel_id=1, source_target_pairs={{0,1},{1,2},{2,3},{3,4},{4,5},{5,6},{6,7},{8,9},{9,10},{10,11},{11... | collective-permute-start | bytes 101384 | tf_op jit(solution)/shard_map/ppermute | solution.py:19
  35.3 1.9 collective-permute-start.7
  37.3 4.9 %pad_maximum_fusion = f32[3,66,130,128]{3,2,1,0:T(8,128)S(1)} fusion(f32[3,66,1,128]{3,2,1,0:T(1,128)S(1)} %collective-permute-done.3, f32[3,1,128,128]{3,2,1,0:T(8,128)S(1)} %collective-permute-done.1, f32[1,64,128,128]{3,2,1,0:T(8,128)S(1)} %copy-done.3, f32[1,64,128,128]{3,2,1,0:T(8,128)S(1)} %bitcast.74, f32[1,64,128,128]{3,2,1,0:T(8,128)S(1)} %bitcast.77, ...), kind=kLoop, calls=%fused_computation.1 | loop fusion | flops 19768320 | bytes 26357760 | tf_op jit(solution)/shard_map/concatenate | solution.py:23
  42.2 6.4 %add_multiply_fusion.2 = (f32[66,130,128]{2,1,0:T(8,128)S(1)}, f32[66,130,128]{2,1,0:T(8,128)S(1)}, f32[66,130,128]{2,1,0:T(8,128)}, f32[66,130,128]{2,1,0:T(8,128)S(1)}) fusion(f32[3,66,130,128]{3,2,1,0:T(8,128)S(1)} %pad_maximum_fusion, pred[66,130]{1,0:T(8,128)(4,1)S(1)} %convert_compare_fusion, f32[66,1,128]{2,1,0:T(1,128)S(1)} %collective-permute-done.7, ...), kind=kLoop, calls=%fused_computation.15 | loop fusion | flops 24161280 | bytes 35152260 | tf_op jit(solution)/shard_map/mul | solution.py:46
  50.7 5.6 %fusion.35 = f32[64,128,127]{2,1,0:T(8,128)} fusion(f32[66,130,128]{2,1,0:T(8,128)S(1)} %maximum_add_fusion.2, f32[66,130,128]{2,1,0:T(8,128)S(1)} %get-tuple-element.12, f32[66,130,128]{2,1,0:T(8,128)S(1)} %get-tuple-element.8), kind=kLoop, calls=%fused_computation.78 | loop fusion | flops 8323072 | bytes 29130752 | tf_op jit(solution)/shard_map/mul | solution.py:34
  56.4 14.6 %fusion.42 = f32[64,128,128]{2,1,0:T(8,128)} fusion(f32[66,130,128]{2,1,0:T(8,128)S(1)} %maximum_add_fusion.2, f32[66,130,128]{2,1,0:T(8,128)S(1)} %get-tuple-element.12, f32[66,130,128]{2,1,0:T(8,128)} %copy-done.6, f32[64,128,127]{2,1,0:T(8,128)} %fusion.35, f32[66,130,128]{2,1,0:T(8,128)S(1)} %get-tuple-element.8), kind=kLoop, calls=%fused_computation.87 | loop fusion | flops 37748736 | bytes 75464704 | tf_op jit(solution)/shard_map/add | solution.py:78
  71.8 4.0 %collective-permute-start.8 = (f32[1,128,128]{2,1,0:T(8,128)S(1)}, f32[1,128,128]{2,1,0:T(8,128)S(1)}, u32[]{:S(2)}, u32[]{:S(2)}) collective-permute-start(f32[1,128,128]{2,1,0:T(8,128)S(1)} %get-tuple-element.25), channel_id=1, source_target_pairs={{0,8},{8,16},{16,24},{24,32},{32,40},{40,48},{48,56},{56,64},{64,7... | collective-permute-start | bytes 196616 | tf_op jit(solution)/shard_map/ppermute | solution.py:19
  77.1 3.8 %collective-permute-done.9 = f32[1,128,128]{2,1,0:T(8,128)S(1)} collective-permute-done((f32[1,128,128]{2,1,0:T(8,128)S(1)}, f32[1,128,128]{2,1,0:T(8,128)S(1)}, u32[]{:S(2)}, u32[]{:S(2)}) %collective-permute-start.9) | collective-permute-done | bytes 65568 | tf_op jit(solution)/shard_map/ppermute | solution.py:22
  82.0 4.9 %collective-permute-start.10 = (f32[66,1,128]{2,1,0:T(1,128)S(1)}, f32[66,1,128]{2,1,0:T(1,128)S(1)}, u32[]{:S(2)}, u32[]{:S(2)}) collective-permute-start(f32[66,1,128]{2,1,0:T(1,128)S(1)} %get-tuple-element.19), channel_id=1, source_target_pairs={{0,1},{1,2},{2,3},{3,4},{4,5},{5,6},{6,7},{8,9},{9,10},{10,11},{11... | collective-permute-start | bytes 101384 | tf_op jit(solution)/shard_map/ppermute | solution.py:19
  87.0 2.1 collective-permute-start.11
  89.3 2.9 %collective-permute-done.11 = f32[66,1,128]{2,1,0:T(1,128)S(1)} collective-permute-done((f32[66,1,128]{2,1,0:T(1,128)S(1)}, f32[66,1,128]{2,1,0:T(1,128)S(1)}, u32[]{:S(2)}, u32[]{:S(2)}) %collective-permute-start.11) | collective-permute-done | bytes 33824 | tf_op jit(solution)/shard_map/ppermute | solution.py:22
  92.2 8.9 %add_multiply_fusion.1 = (f32[66,130,128]{2,1,0:T(8,128)S(1)}, f32[66,130,128]{2,1,0:T(8,128)S(1)}) fusion(f32[3,66,130,128]{3,2,1,0:T(8,128)} %copy-done.1, pred[66,130]{1,0:T(8,128)(4,1)S(1)} %convert_compare_fusion, f32[66,1,128]{2,1,0:T(1,128)S(1)} %collective-permute-done.11, f32[1,128,128]{2,1,0:T(8,128)S(1)} %collective-permute-done.9, ...), kind=kLoop, calls=%fused_computation.13 | loop fusion | flops 18670080 | bytes 26366340 | tf_op jit(solution)/shard_map/mul | solution.py:46
  101.7 1.7 copy-done.4
  105.0 5.6 %fusion.18 = f32[64,128,127]{2,1,0:T(8,128)} fusion(f32[66,130,128]{2,1,0:T(8,128)S(1)} %maximum_add_fusion.1, f32[66,130,128]{2,1,0:T(8,128)S(1)} %bitcast.70, f32[66,130,128]{2,1,0:T(8,128)S(1)} %get-tuple-element.6), kind=kLoop, calls=%fused_computation.51 | loop fusion | flops 8323072 | bytes 29130752 | tf_op jit(solution)/shard_map/mul | solution.py:34
  110.7 14.6 %fusion.25 = f32[64,128,128]{2,1,0:T(8,128)} fusion(f32[66,130,128]{2,1,0:T(8,128)S(1)} %maximum_add_fusion.1, f32[66,130,128]{2,1,0:T(8,128)S(1)} %bitcast.70, f32[66,130,128]{2,1,0:T(8,128)} %copy-done.4, f32[64,128,127]{2,1,0:T(8,128)} %fusion.18, f32[66,130,128]{2,1,0:T(8,128)S(1)} %get-tuple-element.6), kind=kLoop, calls=%fused_computation.60 | loop fusion | flops 37748736 | bytes 75464704 | tf_op jit(solution)/shard_map/add | solution.py:78
  126.3 5.7 %collective-permute-start.12 = (f32[1,128,128]{2,1,0:T(8,128)S(1)}, f32[1,128,128]{2,1,0:T(8,128)S(1)}, u32[]{:S(2)}, u32[]{:S(2)}) collective-permute-start(f32[1,128,128]{2,1,0:T(8,128)S(1)} %get-tuple-element.23), channel_id=1, source_target_pairs={{0,8},{8,16},{16,24},{24,32},{32,40},{40,48},{48,56},{56,64},{64,7... | collective-permute-start | bytes 196616 | tf_op jit(solution)/shard_map/ppermute | solution.py:19
  133.4 4.6 %collective-permute-done.13 = f32[1,128,128]{2,1,0:T(8,128)S(1)} collective-permute-done((f32[1,128,128]{2,1,0:T(8,128)S(1)}, f32[1,128,128]{2,1,0:T(8,128)S(1)}, u32[]{:S(2)}, u32[]{:S(2)}) %collective-permute-start.13) | collective-permute-done | bytes 65568 | tf_op jit(solution)/shard_map/ppermute | solution.py:22
  139.1 3.2 %collective-permute-start.14 = (f32[66,1,128]{2,1,0:T(1,128)S(1)}, f32[66,1,128]{2,1,0:T(1,128)S(1)}, u32[]{:S(2)}, u32[]{:S(2)}) collective-permute-start(f32[66,1,128]{2,1,0:T(1,128)S(1)} %get-tuple-element.17), channel_id=1, source_target_pairs={{0,1},{1,2},{2,3},{3,4},{4,5},{5,6},{6,7},{8,9},{9,10},{10,11},{11... | collective-permute-start | bytes 101384 | tf_op jit(solution)/shard_map/ppermute | solution.py:19
  142.3 2.1 collective-permute-start.15
  144.5 3.0 %collective-permute-done.15 = f32[66,1,128]{2,1,0:T(1,128)S(1)} collective-permute-done((f32[66,1,128]{2,1,0:T(1,128)S(1)}, f32[66,1,128]{2,1,0:T(1,128)S(1)}, u32[]{:S(2)}, u32[]{:S(2)}) %collective-permute-start.15) | collective-permute-done | bytes 33824 | tf_op jit(solution)/shard_map/ppermute | solution.py:22
  147.5 8.4 %add_multiply_fusion = (f32[66,130,128]{2,1,0:T(8,128)S(1)}, f32[66,130,128]{2,1,0:T(8,128)S(1)}, f32[66,130,128]{2,1,0:T(8,128)S(1)}) fusion(f32[3,66,130,128]{3,2,1,0:T(8,128)} %copy-done.1, pred[66,130]{1,0:T(8,128)(4,1)S(1)} %convert_compare_fusion, f32[66,1,128]{2,1,0:T(1,128)S(1)} %collective-permute-done.15, ...), kind=kLoop, calls=%fused_computation.11 | loop fusion | flops 23063040 | bytes 30759300 | tf_op jit(solution)/shard_map/mul | solution.py:46
  159.5 5.1 %fusion.1 = f32[64,128,127]{2,1,0:T(8,128)} fusion(f32[66,130,128]{2,1,0:T(8,128)S(1)} %maximum_add_fusion, f32[66,130,128]{2,1,0:T(8,128)S(1)} %get-tuple-element.10, f32[66,130,128]{2,1,0:T(8,128)S(1)} %get-tuple-element.4), kind=kLoop, calls=%fused_computation.24 | loop fusion | flops 8323072 | bytes 29130752 | tf_op jit(solution)/shard_map/mul | solution.py:34
  164.6 20.4 %maximum_add_fusion.3 = (f32[64,128,128]{2,1,0:T(8,128)}, f32[64,128,128]{2,1,0:T(8,128)}) fusion(f32[64,128,127]{2,1,0:T(8,128)} %fusion.1, f32[66,130,128]{2,1,0:T(8,128)S(1)} %maximum_add_fusion, f32[66,130,128]{2,1,0:T(8,128)} %copy-done, f32[66,130,128]{2,1,0:T(8,128)S(1)} %get-tuple-element.4, f32[66,130,128]{2,1,0:T(8,128)} %copy-done.5), kind=kLoop, calls=%fused_computation.104 | loop fusion | flops 41943040 | bytes 79659008 | tf_op jit(solution)/shard_map/add | solution.py:28
  185.0 13.0 %gather_fusion = f32[4096,128]{1,0:T(8,128)S(1)} fusion(f32[8192,128]{1,0:T(8,128)} %bitcast.71, s32[4096]{0:T(1024)S(1)} %broadcast_clamp_fusion), kind=kCustom, calls=%fused_computation | custom fusion | bytes 4210688 | tf_op jit(solution)/shard_map/gather | solution.py:117
  198.7 43.2 %all_to_all.5 = f32[128,32,128]{2,1,0:T(8,128)S(1)} all-to-all(f32[128,32,128]{2,1,0:T(8,128)S(1)} %broadcast_select_fusion), channel_id=1, replica_groups=mesh['gx'=16,'gy'=8] {'gx','gy'}, dimensions={0} | all-to-all | bytes 4194304 | tf_op jit(solution)/shard_map/all_to_all | solution.py:121
  (70 shorter events, 24.5 us)
Async XLA Ops:
  0.6 3.5 %copy-start.10 = (f32[64,128,128]{2,1,0:T(8,128)S(1)}, f32[64,128,128]{2,1,0:T(8,128)}, u32[]{:S(2)}) copy-start(f32[64,128,128]{2,1,0:T(8,128)} %param.7) | copy-start | bytes 12582916
  0.6 6.2 %copy-start.8 = (f32[64,128,128]{2,1,0:T(8,128)S(1)}, f32[64,128,128]{2,1,0:T(8,128)}, u32[]{:S(2)}) copy-start(f32[64,128,128]{2,1,0:T(8,128)} %param.8) | copy-start | bytes 12582916
  3.3 3.6 %copy-start.2 = (f32[1,64,128,128]{3,2,1,0:T(8,128)}, f32[1,64,128,128]{3,2,1,0:T(8,128)S(1)}, u32[]{:S(2)}) copy-start(f32[1,64,128,128]{3,2,1,0:T(8,128)S(1)} %convert_bitcast_fusion) | copy-start | bytes 12582916
  6.9 15.3 %collective-permute-start = (f32[3,1,128,128]{3,2,1,0:T(8,128)S(1)}, f32[3,1,128,128]{3,2,1,0:T(8,128)S(1)}, u32[]{:S(2)}, u32[]{:S(2)}) collective-permute-start(f32[3,1,128,128]{3,2,1,0:T(8,128)S(1)} %get-tuple-element.15), channel_id=1, source_target_pairs={{0,8},{8,16},{16,24},{24,32},{32,40},{40,48},{48,56},{56,64},{64,7... | collective-permute-start | bytes 589832 | tf_op jit(solution)/shard_map/ppermute | solution.py:19
  11.0 11.2 %collective-permute-start.1 = (f32[3,1,128,128]{3,2,1,0:T(8,128)S(1)}, f32[3,1,128,128]{3,2,1,0:T(8,128)S(1)}, u32[]{:S(2)}, u32[]{:S(2)}) collective-permute-start(f32[3,1,128,128]{3,2,1,0:T(8,128)S(1)} %get-tuple-element.16), channel_id=1, source_target_pairs={{8,0},{16,8},{24,16},{32,24},{40,32},{48,40},{56,48},{64,56},{72,6... | collective-permute-start | bytes 589832 | tf_op jit(solution)/shard_map/ppermute | solution.py:22
  13.2 5.4 %collective-permute-start.4 = (f32[1,128,128]{2,1,0:T(8,128)S(1)}, f32[1,128,128]{2,1,0:T(8,128)S(1)}, u32[]{:S(2)}, u32[]{:S(2)}) collective-permute-start(f32[1,128,128]{2,1,0:T(8,128)S(1)} %get-tuple-element.28), channel_id=1, source_target_pairs={{0,8},{8,16},{16,24},{24,32},{32,40},{40,48},{48,56},{56,64},{64,7... | collective-permute-start | bytes 196616 | tf_op jit(solution)/shard_map/ppermute | solution.py:19
  17.1 5.0 %collective-permute-start.5 = (f32[1,128,128]{2,1,0:T(8,128)S(1)}, f32[1,128,128]{2,1,0:T(8,128)S(1)}, u32[]{:S(2)}, u32[]{:S(2)}) collective-permute-start(f32[1,128,128]{2,1,0:T(8,128)S(1)} %get-tuple-element.27), channel_id=1, source_target_pairs={{8,0},{16,8},{24,16},{32,24},{40,32},{48,40},{56,48},{64,56},{72,6... | collective-permute-start | bytes 196616 | tf_op jit(solution)/shard_map/ppermute | solution.py:22
  18.6 3.6 %copy-start.3 = (f32[1,64,128,128]{3,2,1,0:T(8,128)S(1)}, f32[1,64,128,128]{3,2,1,0:T(8,128)}, u32[]{:S(2)}) copy-start(f32[1,64,128,128]{3,2,1,0:T(8,128)} %copy-done.2) | copy-start | bytes 12582916
  18.6 4.7 %copy-start.9 = (f32[64,128,128]{2,1,0:T(8,128)S(1)}, f32[64,128,128]{2,1,0:T(8,128)}, u32[]{:S(2)}) copy-start(f32[64,128,128]{2,1,0:T(8,128)} %param.8) | copy-start | bytes 12582916
  22.2 15.1 %copy-start.11 = (f32[64,128,128]{2,1,0:T(8,128)S(1)}, f32[64,128,128]{2,1,0:T(8,128)}, u32[]{:S(2)}) copy-start(f32[64,128,128]{2,1,0:T(8,128)} %param.7) | copy-start | bytes 12582916
  24.7 12.5 %collective-permute-start.2 = (f32[3,66,1,128]{3,2,1,0:T(1,128)S(1)}, f32[3,66,1,128]{3,2,1,0:T(1,128)S(1)}, u32[]{:S(2)}, u32[]{:S(2)}) collective-permute-start(f32[3,66,1,128]{3,2,1,0:T(1,128)S(1)} %get-tuple-element.13), channel_id=1, source_target_pairs={{0,1},{1,2},{2,3},{3,4},{4,5},{5,6},{6,7},{8,9},{9,10},{10,11},{11... | collective-permute-start | bytes 304136 | tf_op jit(solution)/shard_map/ppermute | solution.py:19
  29.7 7.6 %collective-permute-start.3 = (f32[3,66,1,128]{3,2,1,0:T(1,128)S(1)}, f32[3,66,1,128]{3,2,1,0:T(1,128)S(1)}, u32[]{:S(2)}, u32[]{:S(2)}) collective-permute-start(f32[3,66,1,128]{3,2,1,0:T(1,128)S(1)} %get-tuple-element.14), channel_id=1, source_target_pairs={{1,0},{2,1},{3,2},{4,3},{5,4},{6,5},{7,6},{9,8},{10,9},{11,10},{12... | collective-permute-start | bytes 304136 | tf_op jit(solution)/shard_map/ppermute | solution.py:22
  31.7 10.5 %collective-permute-start.6 = (f32[66,1,128]{2,1,0:T(1,128)S(1)}, f32[66,1,128]{2,1,0:T(1,128)S(1)}, u32[]{:S(2)}, u32[]{:S(2)}) collective-permute-start(f32[66,1,128]{2,1,0:T(1,128)S(1)} %get-tuple-element.21), channel_id=1, source_target_pairs={{0,1},{1,2},{2,3},{3,4},{4,5},{5,6},{6,7},{8,9},{9,10},{10,11},{11... | collective-permute-start | bytes 101384 | tf_op jit(solution)/shard_map/ppermute | solution.py:19
  35.3 6.9 %collective-permute-start.7 = (f32[66,1,128]{2,1,0:T(1,128)S(1)}, f32[66,1,128]{2,1,0:T(1,128)S(1)}, u32[]{:S(2)}, u32[]{:S(2)}) collective-permute-start(f32[66,1,128]{2,1,0:T(1,128)S(1)} %get-tuple-element.22), channel_id=1, source_target_pairs={{1,0},{2,1},{3,2},{4,3},{5,4},{6,5},{7,6},{9,8},{10,9},{11,10},{12... | collective-permute-start | bytes 101384 | tf_op jit(solution)/shard_map/ppermute | solution.py:22
  42.2 6.4 %copy-start.1 = (f32[3,66,130,128]{3,2,1,0:T(8,128)}, f32[3,66,130,128]{3,2,1,0:T(8,128)S(1)}, u32[]{:S(2)}) copy-start(f32[3,66,130,128]{3,2,1,0:T(8,128)S(1)} %pad_maximum_fusion) | copy-start | bytes 39536644
  48.6 2.1 copy-start.6
  70.9 18.2 %copy-start.12 = (s32[1,1,128,32]{2,3,1,0:T(8,128)S(1)}, s32[1,1,128,32]{2,3,1,0:T(8,128)}, u32[]{:S(2)}) copy-start(s32[1,1,128,32]{2,3,1,0:T(8,128)} %param.10) | copy-start | bytes 49156
  71.8 5.3 %collective-permute-start.8 = (f32[1,128,128]{2,1,0:T(8,128)S(1)}, f32[1,128,128]{2,1,0:T(8,128)S(1)}, u32[]{:S(2)}, u32[]{:S(2)}) collective-permute-start(f32[1,128,128]{2,1,0:T(8,128)S(1)} %get-tuple-element.25), channel_id=1, source_target_pairs={{0,8},{8,16},{16,24},{24,32},{32,40},{40,48},{48,56},{56,64},{64,7... | collective-permute-start | bytes 196616 | tf_op jit(solution)/shard_map/ppermute | solution.py:19
  75.8 5.1 %collective-permute-start.9 = (f32[1,128,128]{2,1,0:T(8,128)S(1)}, f32[1,128,128]{2,1,0:T(8,128)S(1)}, u32[]{:S(2)}, u32[]{:S(2)}) collective-permute-start(f32[1,128,128]{2,1,0:T(8,128)S(1)} %get-tuple-element.26), channel_id=1, source_target_pairs={{8,0},{16,8},{24,16},{32,24},{40,32},{48,40},{56,48},{64,56},{72,6... | collective-permute-start | bytes 196616 | tf_op jit(solution)/shard_map/ppermute | solution.py:22
  82.0 7.3 %collective-permute-start.10 = (f32[66,1,128]{2,1,0:T(1,128)S(1)}, f32[66,1,128]{2,1,0:T(1,128)S(1)}, u32[]{:S(2)}, u32[]{:S(2)}) collective-permute-start(f32[66,1,128]{2,1,0:T(1,128)S(1)} %get-tuple-element.19), channel_id=1, source_target_pairs={{0,1},{1,2},{2,3},{3,4},{4,5},{5,6},{6,7},{8,9},{9,10},{10,11},{11... | collective-permute-start | bytes 101384 | tf_op jit(solution)/shard_map/ppermute | solution.py:19
  87.0 5.2 %collective-permute-start.11 = (f32[66,1,128]{2,1,0:T(1,128)S(1)}, f32[66,1,128]{2,1,0:T(1,128)S(1)}, u32[]{:S(2)}, u32[]{:S(2)}) collective-permute-start(f32[66,1,128]{2,1,0:T(1,128)S(1)} %get-tuple-element.20), channel_id=1, source_target_pairs={{1,0},{2,1},{3,2},{4,3},{5,4},{6,5},{7,6},{9,8},{10,9},{11,10},{12... | collective-permute-start | bytes 101384 | tf_op jit(solution)/shard_map/ppermute | solution.py:22
  101.1 2.3 copy-start.4
  101.1 3.9 %slice-start = ((s8[4595712]{0:T(1024)(128)(4,1)}), s8[4194304]{0:T(1024)(128)(4,1)S(1)}, s32[]{:S(2)}) async-start(s8[4595712]{0:T(1024)(128)(4,1)} %bitcast.69), calls=%async_computation.1 | async-start | bytes 8388608
  101.1 3.9 %slice-start.1 = ((s8[4595712]{0:T(1024)(128)(4,1)}), s8[401408]{0:T(1024)(128)(4,1)S(1)}, s32[]{:S(2)}) async-start(s8[4595712]{0:T(1024)(128)(4,1)} %bitcast.69), calls=%async_computation.2 | async-start | bytes 802816
  125.3 19.1 %copy-start.13 = (s32[1,1,128]{2,1,0:T(1,128)S(1)}, s32[1,1,128]{2,1,0:T(1,128)}, u32[]{:S(2)}) copy-start(s32[1,1,128]{2,1,0:T(1,128)} %param.11) | copy-start | bytes 1540
  125.3 22.2 %copy-start.7 = (f32[64,128,128]{2,1,0:T(8,128)S(1)}, f32[64,128,128]{2,1,0:T(8,128)}, u32[]{:S(2)}) copy-start(f32[64,128,128]{2,1,0:T(8,128)} %fusion.25) | copy-start | bytes 12582916
  126.3 7.1 %collective-permute-start.12 = (f32[1,128,128]{2,1,0:T(8,128)S(1)}, f32[1,128,128]{2,1,0:T(8,128)S(1)}, u32[]{:S(2)}, u32[]{:S(2)}) collective-permute-start(f32[1,128,128]{2,1,0:T(8,128)S(1)} %get-tuple-element.23), channel_id=1, source_target_pairs={{0,8},{8,16},{16,24},{24,32},{32,40},{40,48},{48,56},{56,64},{64,7... | collective-permute-start | bytes 196616 | tf_op jit(solution)/shard_map/ppermute | solution.py:19
  132.0 5.9 %collective-permute-start.13 = (f32[1,128,128]{2,1,0:T(8,128)S(1)}, f32[1,128,128]{2,1,0:T(8,128)S(1)}, u32[]{:S(2)}, u32[]{:S(2)}) collective-permute-start(f32[1,128,128]{2,1,0:T(8,128)S(1)} %get-tuple-element.24), channel_id=1, source_target_pairs={{8,0},{16,8},{24,16},{32,24},{40,32},{48,40},{56,48},{64,56},{72,6... | collective-permute-start | bytes 196616 | tf_op jit(solution)/shard_map/ppermute | solution.py:22
  139.1 5.4 %collective-permute-start.14 = (f32[66,1,128]{2,1,0:T(1,128)S(1)}, f32[66,1,128]{2,1,0:T(1,128)S(1)}, u32[]{:S(2)}, u32[]{:S(2)}) collective-permute-start(f32[66,1,128]{2,1,0:T(1,128)S(1)} %get-tuple-element.17), channel_id=1, source_target_pairs={{0,1},{1,2},{2,3},{3,4},{4,5},{5,6},{6,7},{8,9},{9,10},{10,11},{11... | collective-permute-start | bytes 101384 | tf_op jit(solution)/shard_map/ppermute | solution.py:19
  142.3 5.2 %collective-permute-start.15 = (f32[66,1,128]{2,1,0:T(1,128)S(1)}, f32[66,1,128]{2,1,0:T(1,128)S(1)}, u32[]{:S(2)}, u32[]{:S(2)}) collective-permute-start(f32[66,1,128]{2,1,0:T(1,128)S(1)} %get-tuple-element.18), channel_id=1, source_target_pairs={{1,0},{2,1},{3,2},{4,3},{5,4},{6,5},{7,6},{9,8},{10,9},{11,10},{12... | collective-permute-start | bytes 101384 | tf_op jit(solution)/shard_map/ppermute | solution.py:22
  155.9 2.1 copy-start.5
  156.0 3.5 %copy-start = (f32[66,130,128]{2,1,0:T(8,128)}, f32[66,130,128]{2,1,0:T(8,128)S(1)}, u32[]{:S(2)}) copy-start(f32[66,130,128]{2,1,0:T(8,128)S(1)} %get-tuple-element.10) | copy-start | bytes 13178884
where the time goes:
time: 244 us; the launch traced here: 243 us
  other arithmetic  103 us (42%)
  starting transfers between devices  47.7 us (20%)
  blocking collectives  43.2 us (18%)
  local copies, waits for them, and re-layouts  32.6 us (13%)
  waiting for transfers between devices  15.1 us (6%)
    all_to_all x1, blocking collectives, per_device(): lax.all_to_all(outgoing, ('gx', 'gy'), split_axis=0, concat_axis=0, tiled...  43.2 us
    ppermute x8, starting transfers between devices, padded(): lax.ppermute(lax.slice_in_dim(block, block.shape[dim] - width, None, axis...  34.5 us
    add x2, other arithmetic, advance(): return present_heat_content[1:-1, 1:-1] + RATE * net_flux  29.2 us
    mul x3, other arithmetic, advance(): bordered_diffusivity * (0.5 + 0.25 * kelvin_grid_values)  23.7 us
    add x4, other arithmetic, heat_content_into_kelvin(): jnp.minimum(heat_content_latest, 1.0)  22.2 us
    unnamed x35, local copies, waits for them, and re-layouts  16.7 us
    mul x3, other arithmetic, face_flux(): 2.0 * c_one * c_two / (c_one + c_two) * (a_one * a_two) * (t_two - t_one)  16.4 us
    ppermute x8, waiting for transfers between devices, padded(): lax.ppermute(lax.slice_in_dim(block, 0, width, axis=dim), axis, backward)  15 us
  transfers between devices with their start and end apart: 16, of which 5 were waited for; matrix products, arithmetic and copies ran while one was open for 4% of the time, Pallas kernels for 0%

commit v1 on v0

v1 whole, which is shorter than its diff:
```python
import functools

import jax
import jax.numpy as jnp
from jax import lax
from jax.experimental import pallas as pl
from jax.experimental.pallas import tpu as pltpu
from jax.sharding import PartitionSpec as P

STEPS = 3
TICKS = 2000
LATENT = 0.5
SHARE = 0.2
TICK_SHARE = SHARE / TICKS

HALO = 3
EDGE = 8
CHUNKS = 4


def kelvin(h):
    return jnp.minimum(h, jnp.maximum(h - LATENT, 1.0))


def face(one, two):
    t_one, c_one, p_one = one
    t_two, c_two, p_two = two
    return p_one * p_two * pl.reciprocal(c_one + c_two, approx=True) * (t_two - t_one)


def window_kernel(
    track, lateral, index_ref, h_hbm, k_hbm, bead_hbm, birth_hbm, xlo_ref, xhi_ref, ylo_ref, yhi_ref,
    clo_ref, chi_ref, out_hbm, rows_ref, hs, ks, bs, bead_v, birth_v, ring_t, ring_c, ring_p, fx_s,
    fy_s, sem_in, sem_out,
):
    planes = track + 2 * HALO
    height = lateral + 2 * EDGE
    ring = height + 2 * EDGE
    piece = track // CHUNKS

    def copies(n):
        src = pl.ds(n * piece, piece)
        dst = pl.ds(HALO + n * piece, piece)
        return [
            pltpu.make_async_copy(h_hbm.at[src], hs.at[dst, pl.ds(EDGE, lateral)], sem_in.at[0, n]),
            pltpu.make_async_copy(k_hbm.at[src], ks.at[dst, pl.ds(EDGE, lateral)], sem_in.at[1, n]),
            pltpu.make_async_copy(bead_hbm.at[src], bead_v.at[src], sem_in.at[2, n]),
            pltpu.make_async_copy(birth_hbm.at[src], birth_v.at[src], sem_in.at[3, n]),
        ]

    for n in range(CHUNKS):
        for copy in copies(n):
            copy.start()

    def place(h, k, b, x, rows):
        inside = k > 0.0
        hs[x, rows, :] = h
        ks[x, rows, :] = jnp.where(inside, k, 1.0)
        bs[x, rows, :] = jnp.where(inside, b, 1.0)

    for ref, first in ((xlo_ref, 0), (xhi_ref, HALO + track)):
        for d in range(HALO):
            place(ref[d], ref[HALO + d], ref[2 * HALO + d], first + d, pl.ds(EDGE, lateral))
    for ref, first in ((ylo_ref, EDGE - HALO), (yhi_ref, EDGE + lateral)):
        @pl.loop(0, track)
        def _(x, ref=ref, first=first):
            place(ref[x, 0:HALO], ref[x, HALO:2 * HALO], ref[x, 2 * HALO:], x + HALO, pl.ds(first, HALO))
    for ref, first in ((clo_ref, 0), (chi_ref, HALO + track)):
        for d in range(HALO):
            for side, row in ((0, EDGE - HALO), (1, EDGE + lateral)):
                at = side * 3 * HALO
                place(
                    ref[d, at:at + HALO], ref[d, at + HALO:at + 2 * HALO], ref[d, at + 2 * HALO:at + 3 * HALO],
                    first + d, pl.ds(row, HALO),
                )

    for n in range(CHUNKS):
        for copy in copies(n):
            copy.wait()

        @pl.loop(n * piece, (n + 1) * piece)
        def _(x):
            birth = birth_v[x]
            rows = pl.ds(EDGE, lateral)
            born = (birth >= 0) & (birth < STEPS * TICKS)
            hs[x + HALO, rows, :] = jnp.where(born, bead_v[x], hs[x + HALO, rows, :])
            bs[x + HALO, rows, :] = birth.astype(jnp.float32) * TICK_SHARE

    def run_step(step, xa, xb, r0, r1, size):
        def point(x, r, n):
            rows = pl.ds(r, n)
            t = kelvin(hs[x, rows, :])
            c = ks[x, rows, :] * (2.0 + t)
            a = jnp.clip(SHARE * (step + 1) - bs[x, rows, :], 0.0, SHARE)
            return t, c, c * a

        def slot(x):
            return pl.multiple_of(lax.rem(x, 2) * ring + EDGE, EDGE)

        def put(at, values):
            for ref, value in zip((ring_t, ring_c, ring_p), values):
                ref[at, :] = value

        def get(at):
            return ring_t[at, :], ring_c[at, :], ring_p[at, :]

        starts = list(range(r0, r1, size))
        ends = [r for r in (r0 - EDGE, r1) if 0 <= r < height]
        for r in starts + ends:
            n = size if r in starts else EDGE
            before = point(xa - 1, r, n)
            now = point(xa, r, n)
            put(pl.ds(slot(jnp.int32(xa)) + r, n), now)
            fx_s[pl.ds(r, n), :] = face(before, now)

        @pl.loop(xa, xb)
        def _(x):
            here, there = slot(x), slot(x + 1)
            keep = lax.broadcasted_iota(jnp.int32, (size, 128), 1) < 127
            for r in ends:
                put(pl.ds(there + r, EDGE), point(x + 1, r, EDGE))
            if r0 > 0:
                at = here + r0 - EDGE
                fy_s[pl.ds(at, EDGE), :] = face(get(pl.ds(at, EDGE)), get(pl.ds(at + 1, EDGE)))
            for r in starts:
                cur = get(pl.ds(here + r, size))
                nxt = point(x + 1, r, size)
                put(pl.ds(there + r, size), nxt)
                fx = face(cur, nxt)
                fx_old = fx_s[pl.ds(r, size), :]
                fx_s[pl.ds(r, size), :] = fx
                fy = face(cur, get(pl.ds(here + r + 1, size)))
                fy_s[pl.ds(here + r, size), :] = fy
                fy_old = fy_s[pl.ds(here + r - 1, size), :]
                up = [pltpu.roll(v, 127, 1) for v in cur]
                up[2] = jnp.where(keep, up[2], 0.0)
                fz = face(cur, up)
                flux = (fx - fx_old) + (fy - fy_old) + (fz - pltpu.roll(fz, 1, 1))
                hs[x, pl.ds(r, size), :] = hs[x, pl.ds(r, size), :] + flux

    run_step(0, 1, planes - 1, 0, height, 24)
    run_step(1, 2, planes - 2, 0, height, 24)

    def out_copy(n):
        return pltpu.make_async_copy(
            hs.at[pl.ds(HALO + n * piece, piece), pl.ds(EDGE, lateral)],
            out_hbm.at[pl.ds(n * piece, piece)],
            sem_out.at[n],
        )

    run_step(2, HALO, HALO + track, EDGE, EDGE + lateral, 32)
    for n in range(CHUNKS):
        out_copy(n).start()

    hs[0, 0:EDGE, :] = jnp.zeros((EDGE, 128), jnp.float32)
    owners, slots = index_ref.shape
    flat = hs.reshape(planes * height, 128)

    @pl.loop(0, owners)
    def _(o):
        for k in range(slots):
            rows_ref[pl.ds(o * slots + k, 1), :] = kelvin(flat[pl.ds(index_ref[o, k], 1), :])

    for n in range(CHUNKS):
        out_copy(n).wait()


def window(index, h, k, bead, birth, halos):
    track, lateral, stack = h.shape
    planes, height = track + 2 * HALO, lateral + 2 * EDGE
    ring = height + 2 * EDGE
    owners, slots = index.shape
    anyspace = pl.BlockSpec(memory_space=pl.ANY)
    vmem = pl.BlockSpec(memory_space=pltpu.VMEM)
    grid_shape = (planes, height, stack)
    return pl.pallas_call(
        functools.partial(window_kernel, track, lateral),
        out_shape=(
            jax.ShapeDtypeStruct(h.shape, jnp.float32),
            jax.ShapeDtypeStruct((owners * slots, stack), jnp.float32),
        ),
        in_specs=[pl.BlockSpec(memory_space=pltpu.SMEM)] + [anyspace] * 4 + [vmem] * 6,
        out_specs=(anyspace, vmem),
        scratch_shapes=[
            pltpu.VMEM(grid_shape, jnp.float32),
            pltpu.VMEM(grid_shape, jnp.float32),
            pltpu.VMEM(grid_shape, jnp.float32),
            pltpu.VMEM(h.shape, jnp.float32),
            pltpu.VMEM(h.shape, jnp.int32),
            pltpu.VMEM((2 * ring, stack), jnp.float32),
            pltpu.VMEM((2 * ring, stack), jnp.float32),
            pltpu.VMEM((2 * ring, stack), jnp.float32),
            pltpu.VMEM((height, stack), jnp.float32),
            pltpu.VMEM((2 * ring, stack), jnp.float32),
            pltpu.SemaphoreType.DMA((4, CHUNKS)),
            pltpu.SemaphoreType.DMA((CHUNKS,)),
        ],
        compiler_params=pltpu.CompilerParams(vmem_limit_bytes=50 * 1024 * 1024),
    )(index, h, k, bead, birth, *halos)


def shift(axis, by):
    count = lax.axis_size(axis)
    return [(i, i + by) for i in range(count) if 0 <= i + by < count]


def per_device(enthalpy, conductivity, bead_enthalpy, birth_time, send_rows, send_counts):
    track, lateral, _ = enthalpy.shape

    def fields(cut):
        birth = birth_time[cut]
        born = (birth >= 0) & (birth < STEPS * TICKS)
        return (
            jnp.where(born, bead_enthalpy[cut], enthalpy[cut]),
            conductivity[cut],
            birth.astype(jnp.float32) * TICK_SHARE,
        )

    low, high = slice(0, HALO), slice(-HALO, None)
    xlo = lax.ppermute(jnp.concatenate(fields((high,)), 0), "gx", shift("gx", 1))
    xhi = lax.ppermute(jnp.concatenate(fields((low,)), 0), "gx", shift("gx", -1))
    ylo = lax.ppermute(jnp.concatenate(fields((slice(None), high)), 1), "gy", shift("gy", 1))
    yhi = lax.ppermute(jnp.concatenate(fields((slice(None), low)), 1), "gy", shift("gy", -1))
    clo = lax.ppermute(jnp.concatenate([ylo[-HALO:], yhi[-HALO:]], 1), "gx", shift("gx", 1))
    chi = lax.ppermute(jnp.concatenate([ylo[:HALO], yhi[:HALO]], 1), "gx", shift("gx", -1))

    rows, counts = send_rows[0, 0], send_counts[0, 0]
    slot = jnp.arange(rows.shape[1], dtype=jnp.int32)
    place = (rows // lateral + HALO) * (lateral + 2 * EDGE) + rows % lateral + EDGE
    index = jnp.where(slot[None, :] < counts[:, None], place, 0)
    end, outgoing = window(
        index, enthalpy, conductivity, bead_enthalpy, birth_time, (xlo, xhi, ylo, yhi, clo, chi)
    )
    outgoing = outgoing.reshape(rows.shape + outgoing.shape[1:])
    received = lax.all_to_all(outgoing, ("gx", "gy"), split_axis=0, concat_axis=0, tiled=True)
    return end, received.reshape(-1, received.shape[-1])


def solution(mesh):
    in_specs = (
        P("gx", "gy", None),
        P("gx", "gy", None),
        P("gx", "gy", None),
        P("gx", "gy", None),
        P("gx", "gy", None, None),
        P("gx", "gy", None),
    )
    out_specs = (P("gx", "gy", None), P(("gx", "gy"), None))
    return jax.shard_map(
        per_device, mesh=mesh, in_specs=in_specs, out_specs=out_specs, check_vma=False
    )
```

time: 244 us -> 139 us (0.57)
  other arithmetic: 103 us -> 5.35 us
  Pallas kernels: 0 us -> 62 us
  starting transfers between devices: 47.7 us -> 15.4 us
  local copies, waits for them, and re-layouts: 32.6 us -> 1.43 us
  waiting for transfers between devices: 15.1 us -> 10.6 us
    pallas_call x0 -> x1, Pallas kernels: none -> 62 us  [window(): pl.pallas_call(functools.partial(window_kernel, track, lateral), out_shap...]
    add x6 -> x0, other arithmetic: 51.4 us -> none  [the longest x2 29.2 us: advance(): return present_heat_content[1:-1, 1:-1] + RATE * net_flux]
    mul x6 -> x0, other arithmetic: 40 us -> none  [the longest x3 23.7 us: advance(): bordered_diffusivity * (0.5 + 0.25 * kelvin_grid_values)]
    ppermute x16 -> x6, starting transfers between devices: 47.7 us -> 15.4 us  [the longest x1 4.5 us: per_device(): lax.ppermute(jnp.concatenate(fields((slice(None), high)), 1), 'gy', shift...]
    unnamed x35 -> x6, local copies, waits for them, and re-layouts: 16.7 us -> 1.42 us
    gather x1 -> x0, local copies, waits for them, and re-layouts: 13 us -> none  [per_device(): picked = integration_point_matrix[send_list]]
    ppermute x16 -> x6, waiting for transfers between devices: 15.1 us -> 10.6 us  [the longest x1 4.18 us: per_device(): lax.ppermute(jnp.concatenate([ylo[:HALO], yhi[:HALO]], 1), 'gx', shift('g...]
    slice x4 -> x0, other arithmetic: 3.57 us -> none  [padded(): lax.slice_in_dim(block, block.shape[dim] - width, None, axis=dim)]
  transfers between devices with their start and end apart: 16 -> 6, of which waited for: 5 -> 3; matrix products, arithmetic and copies ran while one was open for 4% -> 2% of each run, Pallas kernels for 0% -> 0%
where the time goes in v1:
time: 139 us
  Pallas kernels  62 us (45%)
  blocking collectives  43.5 us (31%)
  starting transfers between devices  15.4 us (11%)
  waiting for transfers between devices  10.6 us (8%)
  other arithmetic  5.35 us (4%)
  local copies, waits for them, and re-layouts  1.43 us (1%)
    pallas_call x1, Pallas kernels, window(): pl.pallas_call(functools.partial(window_kernel, track, lateral), out_shap...  62 us
    all_to_all x1, blocking collectives, per_device(): lax.all_to_all(outgoing, ('gx', 'gy'), split_axis=0, concat_axis=0, tiled...  43.5 us
    ppermute x1, starting transfers between devices, per_device(): lax.ppermute(jnp.concatenate(fields((slice(None), high)), 1), 'gy', shift...  4.5 us
    ppermute x1, waiting for transfers between devices, per_device(): lax.ppermute(jnp.concatenate([ylo[:HALO], yhi[:HALO]], 1), 'gx', shift('g...  4.18 us
    ppermute x1, waiting for transfers between devices, per_device(): lax.ppermute(jnp.concatenate([ylo[-HALO:], yhi[-HALO:]], 1), 'gx', shift(...  3.63 us
    select_n x2, other arithmetic, fields(): jnp.where(born, bead_enthalpy[cut], enthalpy[cut])  3.31 us
    ppermute x1, starting transfers between devices, per_device(): lax.ppermute(jnp.concatenate(fields((high,)), 0), 'gx', shift('gx', 1))  3.24 us
    ppermute x1, starting transfers between devices, per_device(): lax.ppermute(jnp.concatenate([ylo[-HALO:], yhi[-HALO:]], 1), 'gx', shift(...  3.2 us
  transfers between devices with their start and end apart: 6, of which 3 were waited for; matrix products, arithmetic and copies ran while one was open for 2% of the time, Pallas kernels for 0%

profile of v1, /device:TPU:1, one launch (start us, length us, event | category | flops | bytes accessed | tf_op | source)
XLA Modules:
  0.0 139.1 jit_solution(805055175713440598)
XLA Ops:
  0.6 0.0 copy-start
  0.6 0.0 copy-start.1
  0.6 1.7 %slice_select_fusion.2 = (f32[64,3,128]{2,1,0:T(4,128)S(1)}, f32[64,3,128]{2,1,0:T(4,128)S(1)}, f32[64,3,128]{2,1,0:T(4,128)S(1)}, f32[64,3,128]{2,1,0:T(4,128)S...) fusion(f32[64,128,128]{2,1,0:T(8,128)} %h_hbm.1, f32[64,128,128]{2,1,0:T(8,128)} %bead_hbm.1, ...), kind=kLoop, calls=%fused_computation.9 | loop fusion | flops 294912 | bytes 1376256 | tf_op jit(solution)/shard_map/jit(_where)/select_n | solution.py:214
  2.4 0.9 pad_maximum_fusion.2
  3.3 4.5 %collective-permute-start.2 = (f32[64,9,128]{2,1,0:T(8,128)}, f32[64,9,128]{2,1,0:T(8,128)S(1)}, u32[]{:S(2)}, u32[]{:S(2)}) collective-permute-start(f32[64,9,128]{2,1,0:T(8,128)} %pad_maximum_fusion.2), channel_id=1, source_target_pairs={{0,1},{1,2},{2,3},{3,4},{4,5},{5,6},{6,7},{8,9},{9,10},{10,11},{11... | collective-permute-start | bytes 884744 | tf_op jit(solution)/shard_map/ppermute | solution.py:222
  7.8 0.9 pad_maximum_fusion.3
  8.8 1.9 %collective-permute-start.3 = (f32[64,9,128]{2,1,0:T(8,128)}, f32[64,9,128]{2,1,0:T(8,128)S(1)}, u32[]{:S(2)}, u32[]{:S(2)}) collective-permute-start(f32[64,9,128]{2,1,0:T(8,128)} %pad_maximum_fusion.3), channel_id=1, source_target_pairs={{1,0},{2,1},{3,2},{4,3},{5,4},{6,5},{7,6},{9,8},{10,9},{11,10},{12... | collective-permute-start | bytes 884744 | tf_op jit(solution)/shard_map/ppermute | solution.py:223
  10.7 1.6 %slice_select_fusion = (f32[3,128,128]{2,1,0:T(8,128)S(1)}, f32[3,128,128]{2,1,0:T(8,128)S(1)}, f32[3,128,128]{2,1,0:T(8,128)S(1)}, f32[3,128,128]{2,1,0:T(8,128...) fusion(f32[64,128,128]{2,1,0:T(8,128)} %h_hbm.1, f32[64,128,128]{2,1,0:T(8,128)} %bead_hbm.1, ...), kind=kLoop, calls=%fused_computation.5 | loop fusion | flops 589824 | bytes 2752512 | tf_op jit(solution)/shard_map/jit(_where)/select_n | solution.py:214
  12.3 3.2 %collective-permute-start = (f32[9,128,128]{2,1,0:T(8,128)S(1)}, f32[9,128,128]{2,1,0:T(8,128)S(1)}, u32[]{:S(2)}, u32[]{:S(2)}) collective-permute-start(f32[9,128,128]{2,1,0:T(8,128)S(1)} %pad_maximum_fusion), channel_id=1, source_target_pairs={{0,8},{8,16},{16,24},{24,32},{32,40},{40,48},{48,56},{56,64},{64,7... | collective-permute-start | bytes 1769480 | tf_op jit(solution)/shard_map/ppermute | solution.py:220
  15.6 1.3 collective-permute-start.1
  16.9 0.0 copy-done
  16.9 0.1 copy.8
  17.0 0.0 collective-permute-done.2.ylo_ref
  17.0 2.7 %collective-permute-done.3.yhi_ref = f32[64,9,128]{2,1,0:T(8,128)S(1)} collective-permute-done((f32[64,9,128]{2,1,0:T(8,128)}, f32[64,9,128]{2,1,0:T(8,128)S(1)}, u32[]{:S(2)}, u32[]{:S(2)}) %collective-permute-start.3) | collective-permute-done | bytes 294944 | tf_op jit(solution)/shard_map/ppermute | solution.py:223
  19.8 3.2 %collective-permute-start.4 = (f32[3,18,128]{2,1,0:T(8,128)S(1)}, f32[3,18,128]{2,1,0:T(8,128)S(1)}, u32[]{:S(2)}, u32[]{:S(2)}) collective-permute-start(f32[3,18,128]{2,1,0:T(8,128)S(1)} %pad_maximum_fusion.4), channel_id=1, source_target_pairs={{0,8},{8,16},{16,24},{24,32},{32,40},{40,48},{48,56},{56,64},{64,7... | collective-permute-start | bytes 82952 | tf_op jit(solution)/shard_map/ppermute | solution.py:224
  23.0 1.3 collective-permute-start.5
  24.3 0.0 copy-done.1
  24.3 0.1 fusion.4.index_ref
  24.4 3.6 %collective-permute-done.4.clo_ref = f32[3,18,128]{2,1,0:T(8,128)S(1)} collective-permute-done((f32[3,18,128]{2,1,0:T(8,128)S(1)}, f32[3,18,128]{2,1,0:T(8,128)S(1)}, u32[]{:S(2)}, u32[]{:S(2)}) %collective-permute-start.4) | collective-permute-done | bytes 27680 | tf_op jit(solution)/shard_map/ppermute | solution.py:224
  28.0 4.2 %collective-permute-done.5.chi_ref = f32[3,18,128]{2,1,0:T(8,128)S(1)} collective-permute-done((f32[3,18,128]{2,1,0:T(8,128)S(1)}, f32[3,18,128]{2,1,0:T(8,128)S(1)}, u32[]{:S(2)}, u32[]{:S(2)}) %collective-permute-start.5) | collective-permute-done | bytes 27680 | tf_op jit(solution)/shard_map/ppermute | solution.py:225
  32.2 0.0 collective-permute-done.xlo_ref
  32.2 0.0 collective-permute-done.1.xhi_ref
  32.2 62.0 %shard_map.77 = (f32[64,128,128]{2,1,0:T(8,128)}, f32[4096,128]{1,0:T(8,128)}) custom-call(s32[128,32]{1,0:T(8,128)S(1)} %fusion.4.index_ref, f32[64,128,128]{2,1,0:T(8,128)} %h_hbm.1, f32[64,128,128]{2,1,0:T(8,128)} %k_hbm.1, f32[64,128,128]{2,1,0:T(8,128)} %bead_hbm.1, s32[64,128,128]{2,1,0:T(8,128)} %birth_hbm.1, ...), custom_call_target="tpu_custom_call" | custom-call | tf_op jit(solution)/shard_map/pallas_call | solution.py:176
  94.3 43.5 %all_to_all.5 = f32[128,32,128]{2,1,0:T(8,128)S(1)} all-to-all(f32[128,32,128]{2,1,0:T(8,128)} %bitcast.24), channel_id=1, replica_groups=mesh['gx'=16,'gy'=8] {'gx','gy'}, dimensions={0} | all-to-all | bytes 4194304 | tf_op jit(solution)/shard_map/all_to_all | solution.py:235
  137.7 1.3 copy.10
  (6 shorter events, 0.1 us)
Async XLA Ops:
  0.6 16.3 %copy-start = (s32[1,1,128,32]{2,3,1,0:T(8,128)S(1)}, s32[1,1,128,32]{2,3,1,0:T(8,128)}, u32[]{:S(2)}) copy-start(s32[1,1,128,32]{2,3,1,0:T(8,128)} %param.10) | copy-start | bytes 49156
  0.6 23.7 %copy-start.1 = (s32[1,1,128]{2,1,0:T(1,128)S(1)}, s32[1,1,128]{2,1,0:T(1,128)}, u32[]{:S(2)}) copy-start(s32[1,1,128]{2,1,0:T(1,128)} %param.11) | copy-start | bytes 1540
  3.3 13.7 %collective-permute-start.2 = (f32[64,9,128]{2,1,0:T(8,128)}, f32[64,9,128]{2,1,0:T(8,128)S(1)}, u32[]{:S(2)}, u32[]{:S(2)}) collective-permute-start(f32[64,9,128]{2,1,0:T(8,128)} %pad_maximum_fusion.2), channel_id=1, source_target_pairs={{0,1},{1,2},{2,3},{3,4},{4,5},{5,6},{6,7},{8,9},{9,10},{10,11},{11... | collective-permute-start | bytes 884744 | tf_op jit(solution)/shard_map/ppermute | solution.py:222
  8.8 11.0 %collective-permute-start.3 = (f32[64,9,128]{2,1,0:T(8,128)}, f32[64,9,128]{2,1,0:T(8,128)S(1)}, u32[]{:S(2)}, u32[]{:S(2)}) collective-permute-start(f32[64,9,128]{2,1,0:T(8,128)} %pad_maximum_fusion.3), channel_id=1, source_target_pairs={{1,0},{2,1},{3,2},{4,3},{5,4},{6,5},{7,6},{9,8},{10,9},{11,10},{12... | collective-permute-start | bytes 884744 | tf_op jit(solution)/shard_map/ppermute | solution.py:223
  12.3 19.9 %collective-permute-start = (f32[9,128,128]{2,1,0:T(8,128)S(1)}, f32[9,128,128]{2,1,0:T(8,128)S(1)}, u32[]{:S(2)}, u32[]{:S(2)}) collective-permute-start(f32[9,128,128]{2,1,0:T(8,128)S(1)} %pad_maximum_fusion), channel_id=1, source_target_pairs={{0,8},{8,16},{16,24},{24,32},{32,40},{40,48},{48,56},{56,64},{64,7... | collective-permute-start | bytes 1769480 | tf_op jit(solution)/shard_map/ppermute | solution.py:220
  15.6 16.6 %collective-permute-start.1 = (f32[9,128,128]{2,1,0:T(8,128)S(1)}, f32[9,128,128]{2,1,0:T(8,128)S(1)}, u32[]{:S(2)}, u32[]{:S(2)}) collective-permute-start(f32[9,128,128]{2,1,0:T(8,128)S(1)} %pad_maximum_fusion.1), channel_id=1, source_target_pairs={{8,0},{16,8},{24,16},{32,24},{40,32},{48,40},{56,48},{64,56},{72,6... | collective-permute-start | bytes 1769480 | tf_op jit(solution)/shard_map/ppermute | solution.py:221
  19.8 8.3 %collective-permute-start.4 = (f32[3,18,128]{2,1,0:T(8,128)S(1)}, f32[3,18,128]{2,1,0:T(8,128)S(1)}, u32[]{:S(2)}, u32[]{:S(2)}) collective-permute-start(f32[3,18,128]{2,1,0:T(8,128)S(1)} %pad_maximum_fusion.4), channel_id=1, source_target_pairs={{0,8},{8,16},{16,24},{24,32},{32,40},{40,48},{48,56},{56,64},{64,7... | collective-permute-start | bytes 82952 | tf_op jit(solution)/shard_map/ppermute | solution.py:224
  23.0 9.2 %collective-permute-start.5 = (f32[3,18,128]{2,1,0:T(8,128)S(1)}, f32[3,18,128]{2,1,0:T(8,128)S(1)}, u32[]{:S(2)}, u32[]{:S(2)}) collective-permute-start(f32[3,18,128]{2,1,0:T(8,128)S(1)} %pad_maximum_fusion.5), channel_id=1, source_target_pairs={{8,0},{16,8},{24,16},{32,24},{40,32},{48,40},{56,48},{64,56},{72,6... | collective-permute-start | bytes 82952 | tf_op jit(solution)/shard_map/ppermute | solution.py:225

commit v2 on v1

v2 whole, which is shorter than its diff:
```python
import functools

import jax
import jax.numpy as jnp
from jax import lax
from jax.experimental import pallas as pl
from jax.experimental.pallas import tpu as pltpu
from jax.sharding import PartitionSpec as P

STEPS = 3
TICKS = 2000
LATENT = 0.5
SHARE = 0.2
TICK_SHARE = SHARE / TICKS

HALO = 3
EDGE = 8
LEAD = 4
LANES = 128
TILE = 8
OFFSET = 2.0
FAR = 1e-30
CHUNKS = 8
OUTS = 4
UNROLL = 2
PUN = 2


def kelvin(h):
    return jnp.minimum(h, jnp.maximum(h - LATENT, 1.0 + OFFSET))


def face(one, two):
    return one[2] * two[2] * pl.reciprocal(one[1] + two[1], approx=True) * (two[0] - one[0])


def window_kernel(
    track, lateral, index_ref, h_hbm, k_hbm, bead_hbm, birth_hbm, xlo_ref, xhi_ref, ylo_ref, yhi_ref,
    clo_ref, chi_ref, out_hbm, rows_ref, h_v, k_v, bead_v, birth_v, hs, hn, ks, kz, bs, bz, ring_a,
    ring_b, acc_s, sem_in, sem_out,
):
    planes = track + 2 * HALO
    height = lateral + 2 * EDGE
    span = (lateral + 2 * LEAD) // TILE
    inner = pl.ds(EDGE, lateral)

    def copies(n):
        piece = track // CHUNKS
        src = pl.ds(n * piece, piece)
        dst = pl.ds(HALO + n * piece, piece)
        pairs = ((h_hbm, h_v), (k_hbm, k_v), (bead_hbm, bead_v), (birth_hbm, birth_v))
        return [
            pltpu.make_async_copy(hbm.at[src], vmem.at[dst, inner], sem_in.at[i, n])
            for i, (hbm, vmem) in enumerate(pairs)
        ]

    for n in range(CHUNKS):
        for copy in copies(n):
            copy.start()

    def place(h, k, birth, x, rows):
        inside = k > 0.0
        h_v[x, rows, :] = h
        bead_v[x, rows, :] = h
        k_v[x, rows, :] = jnp.where(inside, k, 1.0)
        birth_v[x, rows, :] = jnp.where(inside, birth, 1e6).astype(jnp.int32)

    for ref, first in ((xlo_ref, 0), (xhi_ref, HALO + track)):
        @pl.loop(0, HALO)
        def _(d, ref=ref, first=first):
            place(ref[d], ref[HALO + d], ref[2 * HALO + d], first + d, inner)
    for ref, first in ((ylo_ref, EDGE - HALO), (yhi_ref, EDGE + lateral)):
        @pl.loop(0, track)
        def _(x, ref=ref, first=first):
            place(ref[x, 0:HALO], ref[x, HALO:2 * HALO], ref[x, 2 * HALO:], x + HALO, pl.ds(first, HALO))
    for ref, first in ((clo_ref, 0), (chi_ref, HALO + track)):
        for d in range(HALO):
            for side, row in ((0, EDGE - HALO), (1, EDGE + lateral)):
                at = side * 3 * HALO
                place(
                    ref[d, at:at + HALO], ref[d, at + HALO:at + 2 * HALO], ref[d, at + 2 * HALO:at + 3 * HALO],
                    first + d, pl.ds(row, HALO),
                )

    top = lax.broadcasted_iota(jnp.int32, (TILE, LANES), 1) == LANES - 1

    def natural(j):
        return pl.ds(EDGE - LEAD + j, TILE, stride=span)

    def tile(j):
        return pl.ds(j * TILE, TILE)

    def prepare(x):
        for j in range(span):
            at, to = natural(j), tile(j)
            birth = birth_v[x, at, :]
            k = k_v[x, at, :]
            born = (birth >= 0) & (birth < STEPS * TICKS)
            b = birth.astype(jnp.float32) * TICK_SHARE
            hs[x, to, :] = jnp.where(born, bead_v[x, at, :], h_v[x, at, :]) + OFFSET
            ks[x, to, :] = k
            kz[x, to, :] = jnp.where(top, FAR, pltpu.roll(k, LANES - 1, 1))
            bs[x, to, :] = b
            bz[x, to, :] = pltpu.roll(b, LANES - 1, 1)

    def prepare_all(lo, hi):
        @pl.loop(0, (hi - lo) // PUN)
        def _(i):
            for u in range(PUN):
                prepare(lo + i * PUN + u)
        for x in range(hi - (hi - lo) % PUN, hi):
            prepare(x)

    prepare_all(0, HALO)
    prepare_all(HALO + track, planes)
    for n in range(CHUNKS):
        for copy in copies(n):
            copy.wait()
        piece = track // CHUNKS
        prepare_all(HALO + n * piece, HALO + (n + 1) * piece)

    def run_step(step, src, store, cuts):
        def share(b):
            return jnp.clip(SHARE * (step + 1) - b, 0.0, SHARE)

        def point(x, j):
            at = tile(j)
            h = src[x, at, :]
            t = kelvin(h)
            return h, (t, pl.reciprocal(ks[x, at, :] * t, approx=True), share(bs[x, at, :]))

        def put(ring, j, values):
            for ref, value in zip(ring, values):
                ref[tile(j), :] = value

        def get(ring, j):
            return [ref[tile(j), :] for ref in ring]

        for j in range(span):
            before = point(cuts[0] - 1, j)[1]
            h, now = point(cuts[0], j)
            put(ring_a, j, now)
            acc_s[tile(j), :] = h - face(before, now)

        def plane(x, here, there):
            cur = get(here, 0)
            beyond = [pltpu.roll(v, TILE - 1, 0) for v in cur]
            fy_old = pltpu.roll(face(get(here, span - 1), beyond), 1, 0)
            for j in range(span):
                at = tile(j)
                ahead = get(here, j + 1) if j + 1 < span else beyond
                h, nxt = point(x + 1, j)
                put(there, j, nxt)
                fx = face(cur, nxt)
                total = acc_s[at, :] + fx
                acc_s[at, :] = h - fx
                fy = face(cur, ahead)
                t = pltpu.roll(cur[0], LANES - 1, 1)
                fz = face(cur, (t, pl.reciprocal(kz[x, at, :] * t, approx=True), share(bz[x, at, :])))
                total = total + ((fy - fy_old) + (fz - pltpu.roll(fz, 1, 1)))
                store(x, j, total)
                cur, fy_old = ahead, fy

        for n, (lo, hi) in enumerate(zip(cuts[:-1], cuts[1:])):
            unroll = [u for u in (UNROLL, 2) if (hi - lo) % u == 0][0]

            @pl.loop(0, (hi - lo) // unroll)
            def _(i):
                for u in range(unroll):
                    rings = (ring_a, ring_b) if u % 2 == 0 else (ring_b, ring_a)
                    plane(lo + unroll * i + u, *rings)

            if step == STEPS - 1:
                out_copy(n).start()

    def out_copy(n):
        piece = track // OUTS
        return pltpu.make_async_copy(
            h_v.at[pl.ds(HALO + n * piece, piece), inner], out_hbm.at[pl.ds(n * piece, piece)], sem_out.at[n]
        )

    def into(ref):
        def store(x, j, value):
            ref[x, tile(j), :] = value
        return store

    def finish(x, j, value):
        h_v[x, natural(j), :] = value - OFFSET

    run_step(0, hs, into(hn), (1, planes - 1))
    run_step(1, hn, into(hs), (2, planes - 2))
    run_step(2, hs, finish, [HALO + n * (track // OUTS) for n in range(OUTS + 1)])

    h_v[0, 0:EDGE, :] = jnp.zeros((EDGE, LANES), jnp.float32)
    owners, slots = index_ref.shape
    flat = h_v.reshape(planes * height, LANES)

    @pl.loop(0, owners)
    def _(o):
        for k in range(slots):
            h = flat[pl.ds(index_ref[o, k], 1), :]
            rows_ref[pl.ds(o * slots + k, 1), :] = jnp.minimum(h, jnp.maximum(h - LATENT, 1.0))

    for n in range(OUTS):
        out_copy(n).wait()


def window(index, h, k, bead, birth, halos):
    track, lateral, stack = h.shape
    planes, height = track + 2 * HALO, lateral + 2 * EDGE
    owners, slots = index.shape
    anyspace = pl.BlockSpec(memory_space=pl.ANY)
    vmem = pl.BlockSpec(memory_space=pltpu.VMEM)
    grid_shape = (planes, height, stack)
    tiles_shape = (planes, lateral + 2 * LEAD, stack)
    return pl.pallas_call(
        functools.partial(window_kernel, track, lateral),
        out_shape=(
            jax.ShapeDtypeStruct(h.shape, jnp.float32),
            jax.ShapeDtypeStruct((owners * slots, stack), jnp.float32),
        ),
        in_specs=[pl.BlockSpec(memory_space=pltpu.SMEM)] + [anyspace] * 4 + [vmem] * 6,
        out_specs=(anyspace, vmem),
        scratch_shapes=[
            pltpu.VMEM(grid_shape, jnp.float32),
            pltpu.VMEM(grid_shape, jnp.float32),
            pltpu.VMEM(grid_shape, jnp.float32),
            pltpu.VMEM(grid_shape, jnp.int32),
            pltpu.VMEM(tiles_shape, jnp.float32),
            pltpu.VMEM(tiles_shape, jnp.float32),
            pltpu.VMEM(tiles_shape, jnp.float32),
            pltpu.VMEM(tiles_shape, jnp.float32),
            pltpu.VMEM(tiles_shape, jnp.float32),
            pltpu.VMEM(tiles_shape, jnp.float32),
            [pltpu.VMEM(tiles_shape[1:], jnp.float32)] * 3,
            [pltpu.VMEM(tiles_shape[1:], jnp.float32)] * 3,
            pltpu.VMEM(tiles_shape[1:], jnp.float32),
            pltpu.SemaphoreType.DMA((4, CHUNKS)),
            pltpu.SemaphoreType.DMA((OUTS,)),
        ],
        compiler_params=pltpu.CompilerParams(vmem_limit_bytes=58 * 1024 * 1024),
    )(index, h, k, bead, birth, *halos)


def shift(axis, by):
    count = lax.axis_size(axis)
    return [(i, i + by) for i in range(count) if 0 <= i + by < count]


def per_device(enthalpy, conductivity, bead_enthalpy, birth_time, send_rows, send_counts):
    track, lateral, _ = enthalpy.shape

    def fields(cut):
        birth = birth_time[cut]
        born = (birth >= 0) & (birth < STEPS * TICKS)
        return (
            jnp.where(born, bead_enthalpy[cut], enthalpy[cut]),
            conductivity[cut],
            birth.astype(jnp.float32),
        )

    low, high = slice(0, HALO), slice(-HALO, None)
    xlo = lax.ppermute(jnp.concatenate(fields((high,)), 0), "gx", shift("gx", 1))
    xhi = lax.ppermute(jnp.concatenate(fields((low,)), 0), "gx", shift("gx", -1))
    ylo = lax.ppermute(jnp.concatenate(fields((slice(None), high)), 1), "gy", shift("gy", 1))
    yhi = lax.ppermute(jnp.concatenate(fields((slice(None), low)), 1), "gy", shift("gy", -1))
    clo = lax.ppermute(jnp.concatenate([ylo[-HALO:], yhi[-HALO:]], 1), "gx", shift("gx", 1))
    chi = lax.ppermute(jnp.concatenate([ylo[:HALO], yhi[:HALO]], 1), "gx", shift("gx", -1))

    rows, counts = send_rows[0, 0], send_counts[0, 0]
    slot = jnp.arange(rows.shape[1], dtype=jnp.int32)
    place = (rows // lateral + HALO) * (lateral + 2 * EDGE) + rows % lateral + EDGE
    index = jnp.where(slot[None, :] < counts[:, None], place, 0)
    end, outgoing = window(
        index, enthalpy, conductivity, bead_enthalpy, birth_time, (xlo, xhi, ylo, yhi, clo, chi)
    )
    outgoing = outgoing.reshape(rows.shape + outgoing.shape[1:])
    received = lax.all_to_all(outgoing, ("gx", "gy"), split_axis=0, concat_axis=0, tiled=True)
    return end, received.reshape(-1, received.shape[-1])


def solution(mesh):
    in_specs = (
        P("gx", "gy", None),
        P("gx", "gy", None),
        P("gx", "gy", None),
        P("gx", "gy", None),
        P("gx", "gy", None, None),
        P("gx", "gy", None),
    )
    out_specs = (P("gx", "gy", None), P(("gx", "gy"), None))
    return jax.shard_map(
        per_device, mesh=mesh, in_specs=in_specs, out_specs=out_specs, check_vma=False
    )
```

time: 139 us -> 118 us (0.85)
  Pallas kernels: 62 us -> 37 us
  other arithmetic: 5.35 us -> 8.06 us
  local copies, waits for them, and re-layouts: 1.43 us -> 3.09 us
    pallas_call x1, Pallas kernels: 62 us -> 37 us  [window(): pl.pallas_call(functools.partial(window_kernel, track, lateral), out_shap...]
    convert_element_type x0 -> x2, other arithmetic: none -> 2.13 us  [fields(): birth.astype(jnp.float32)]
    unnamed x6 -> x18, local copies, waits for them, and re-layouts: 1.42 us -> 3.08 us
  transfers between devices with their start and end apart: 6 -> 6, of which waited for: 3 -> 3; matrix products, arithmetic and copies ran while one was open for 2% -> 4% of each run, Pallas kernels for 0% -> 0%
where the time goes in v2:
time: 118 us
  blocking collectives  43.5 us (37%)
  Pallas kernels  37 us (31%)
  starting transfers between devices  15.7 us (13%)
  waiting for transfers between devices  9.62 us (8%)
  other arithmetic  8.06 us (7%)
  local copies, waits for them, and re-layouts  3.09 us (3%)
    all_to_all x1, blocking collectives, per_device(): lax.all_to_all(outgoing, ('gx', 'gy'), split_axis=0, concat_axis=0, tiled...  43.5 us
    pallas_call x1, Pallas kernels, window(): pl.pallas_call(functools.partial(window_kernel, track, lateral), out_shap...  37 us
    ppermute x1, starting transfers between devices, per_device(): lax.ppermute(jnp.concatenate(fields((slice(None), high)), 1), 'gy', shift...  4.5 us
    ppermute x1, waiting for transfers between devices, per_device(): lax.ppermute(jnp.concatenate([ylo[:HALO], yhi[:HALO]], 1), 'gx', shift('g...  4.18 us
    ppermute x1, waiting for transfers between devices, per_device(): lax.ppermute(jnp.concatenate([ylo[-HALO:], yhi[-HALO:]], 1), 'gx', shift(...  4.04 us
    ppermute x1, starting transfers between devices, per_device(): lax.ppermute(jnp.concatenate([ylo[-HALO:], yhi[-HALO:]], 1), 'gx', shift(...  3.5 us
    select_n x2, other arithmetic, fields(): jnp.where(born, bead_enthalpy[cut], enthalpy[cut])  3.25 us
    ppermute x1, starting transfers between devices, per_device(): lax.ppermute(jnp.concatenate(fields((high,)), 0), 'gx', shift('gx', 1))  3.24 us
  transfers between devices with their start and end apart: 6, of which 3 were waited for; matrix products, arithmetic and copies ran while one was open for 4% of the time, Pallas kernels for 0%

profile of v2, /device:TPU:1, one launch (start us, length us, event | category | flops | bytes accessed | tf_op | source)
XLA Modules:
  0.0 117.8 jit_solution(2945335397679148015)
XLA Ops:
  0.6 1.1 slice_convert_fusion.2
  1.7 0.0 copy-start.6
  1.7 1.7 %slice_select_fusion.2 = (f32[64,3,128]{2,1,0:T(4,128)S(1)}, f32[64,3,128]{2,1,0:T(4,128)S(1)}, f32[64,3,128]{2,1,0:T(4,128)S(1)}, f32[64,3,128]{2,1,0:T(4,128)S(1)}) fusion(f32[64,128,128]{2,1,0:T(8,128)} %h_hbm.1, f32[64,128,128]{2,1,0:T(8,128)} %bead_hbm.1, s32[64,128,128]{2,1,0:T(8,128)} %birth_hbm.1, f32[64,128,128]{2,1,0:T(8,128)} %k_hbm.1), kind=kLoop, calls=%fused_computation.8 | loop fusion | flops 196608 | bytes 1179648 | tf_op jit(solution)/shard_map/jit(_where)/select_n | solution.py:257
  3.4 0.0 copy-start.7
  3.4 0.9 pad_maximum_fusion.2
  4.4 4.5 %collective-permute-start.2 = (f32[64,9,128]{2,1,0:T(8,128)}, f32[64,9,128]{2,1,0:T(8,128)S(1)}, u32[]{:S(2)}, u32[]{:S(2)}) collective-permute-start(f32[64,9,128]{2,1,0:T(8,128)} %pad_maximum_fusion.2), channel_id=1, source_target_pairs={{0,1},{1,2},{2,3},{3,4},{4,5},{5,6},{6,7},{8,9},{9,10},{10,11},{11... | collective-permute-start | bytes 884744 | tf_op jit(solution)/shard_map/ppermute | solution.py:265
  8.9 0.9 pad_maximum_fusion.3
  9.8 1.9 %collective-permute-start.3 = (f32[64,9,128]{2,1,0:T(8,128)}, f32[64,9,128]{2,1,0:T(8,128)S(1)}, u32[]{:S(2)}, u32[]{:S(2)}) collective-permute-start(f32[64,9,128]{2,1,0:T(8,128)} %pad_maximum_fusion.3), channel_id=1, source_target_pairs={{1,0},{2,1},{3,2},{4,3},{5,4},{6,5},{7,6},{9,8},{10,9},{11,10},{12... | collective-permute-start | bytes 884744 | tf_op jit(solution)/shard_map/ppermute | solution.py:266
  11.7 1.6 %slice_select_fusion = (f32[3,128,128]{2,1,0:T(8,128)S(1)}, f32[3,128,128]{2,1,0:T(8,128)S(1)}, f32[3,128,128]{2,1,0:T(8,128)S(1)}, f32[3,128,128]{2,1,0:T(8,128)S(1)}) fusion(f32[64,128,128]{2,1,0:T(8,128)} %h_hbm.1, f32[64,128,128]{2,1,0:T(8,128)} %bead_hbm.1, s32[64,128,128]{2,1,0:T(8,128)} %birth_hbm.1, f32[64,128,128]{2,1,0:T(8,128)} %k_hbm.1), kind=kLoop, calls=%fused_computation.4 | loop fusion | flops 393216 | bytes 2359296 | tf_op jit(solution)/shard_map/jit(_where)/select_n | solution.py:257
  13.3 1.1 slice_convert_fusion
  14.4 3.2 %collective-permute-start = (f32[9,128,128]{2,1,0:T(8,128)S(1)}, f32[9,128,128]{2,1,0:T(8,128)S(1)}, u32[]{:S(2)}, u32[]{:S(2)}) collective-permute-start(f32[9,128,128]{2,1,0:T(8,128)S(1)} %pad_maximum_fusion), channel_id=1, source_target_pairs={{0,8},{8,16},{16,24},{24,32},{32,40},{40,48},{48,56},{56,64},{64,7... | collective-permute-start | bytes 1769480 | tf_op jit(solution)/shard_map/ppermute | solution.py:263
  17.7 1.3 %collective-permute-start.1 = (f32[9,128,128]{2,1,0:T(8,128)S(1)}, f32[9,128,128]{2,1,0:T(8,128)S(1)}, u32[]{:S(2)}, u32[]{:S(2)}) collective-permute-start(f32[9,128,128]{2,1,0:T(8,128)S(1)} %pad_maximum_fusion.1), channel_id=1, source_target_pairs={{8,0},{16,8},{24,16},{32,24},{40,32},{48,40},{56,48},{64,56},{72,6... | collective-permute-start | bytes 1769480 | tf_op jit(solution)/shard_map/ppermute | solution.py:264
  19.0 0.0 copy-done.6
  19.0 0.1 copy.8
  19.1 0.0 collective-permute-done.2.ylo_ref
  19.1 0.0 copy-start
  19.1 1.4 %collective-permute-done.3.yhi_ref = f32[64,9,128]{2,1,0:T(8,128)S(1)} collective-permute-done((f32[64,9,128]{2,1,0:T(8,128)}, f32[64,9,128]{2,1,0:T(8,128)S(1)}, u32[]{:S(2)}, u32[]{:S(2)}) %collective-permute-start.3) | collective-permute-done | bytes 294944 | tf_op jit(solution)/shard_map/ppermute | solution.py:266
  20.5 3.5 %collective-permute-start.4 = (f32[3,18,128]{2,1,0:T(8,128)S(1)}, f32[3,18,128]{2,1,0:T(8,128)S(1)}, u32[]{:S(2)}, u32[]{:S(2)}) collective-permute-start(f32[3,18,128]{2,1,0:T(8,128)S(1)} %pad_maximum_fusion.4), channel_id=1, source_target_pairs={{0,8},{8,16},{16,24},{24,32},{32,40},{40,48},{48,56},{56,64},{64,7... | collective-permute-start | bytes 82952 | tf_op jit(solution)/shard_map/ppermute | solution.py:267
  24.0 1.3 %collective-permute-start.5 = (f32[3,18,128]{2,1,0:T(8,128)S(1)}, f32[3,18,128]{2,1,0:T(8,128)S(1)}, u32[]{:S(2)}, u32[]{:S(2)}) collective-permute-start(f32[3,18,128]{2,1,0:T(8,128)S(1)} %pad_maximum_fusion.5), channel_id=1, source_target_pairs={{8,0},{16,8},{24,16},{32,24},{40,32},{48,40},{56,48},{64,56},{72,6... | collective-permute-start | bytes 82952 | tf_op jit(solution)/shard_map/ppermute | solution.py:268
  25.3 0.0 copy-done.7
  25.4 0.7 fusion.4.index_ref
  26.1 4.0 %collective-permute-done.4.clo_ref = f32[3,18,128]{2,1,0:T(8,128)S(1)} collective-permute-done((f32[3,18,128]{2,1,0:T(8,128)S(1)}, f32[3,18,128]{2,1,0:T(8,128)S(1)}, u32[]{:S(2)}, u32[]{:S(2)}) %collective-permute-start.4) | collective-permute-done | bytes 27680 | tf_op jit(solution)/shard_map/ppermute | solution.py:267
  30.1 4.2 %collective-permute-done.5.chi_ref = f32[3,18,128]{2,1,0:T(8,128)S(1)} collective-permute-done((f32[3,18,128]{2,1,0:T(8,128)S(1)}, f32[3,18,128]{2,1,0:T(8,128)S(1)}, u32[]{:S(2)}, u32[]{:S(2)}) %collective-permute-start.5) | collective-permute-done | bytes 27680 | tf_op jit(solution)/shard_map/ppermute | solution.py:268
  34.3 0.0 collective-permute-done.xlo_ref
  34.3 0.0 collective-permute-done.1.xhi_ref
  34.3 0.0 copy-done
  34.3 0.6 copy-done.5
  34.9 0.2 copy-done.2
  35.1 0.8 copy-done.3
  36.0 37.0 %shard_map.77 = (f32[64,128,128]{2,1,0:T(8,128)}, f32[4096,128]{1,0:T(8,128)}) custom-call(s32[128,32]{1,0:T(8,128)} %fusion.4.index_ref, f32[64,128,128]{2,1,0:T(8,128)} %h_hbm.1, f32[64,128,128]{2,1,0:T(8,128)} %k_hbm.1, f32[64,128,128]{2,1,0:T(8,128)} %bead_hbm.1, s32[64,128,128]{2,1,0:T(8,128)} %birth_hbm.1, f32[9,128,128]{2,1,0:T(8,128)} %copy-done.2, ...), custom_call_target="tpu_custom_call" | custom-call | tf_op jit(solution)/shard_map/pallas_call | solution.py:216
  73.0 43.5 %all_to_all.5 = f32[128,32,128]{2,1,0:T(8,128)S(1)} all-to-all(f32[128,32,128]{2,1,0:T(8,128)} %bitcast.24), channel_id=1, replica_groups=mesh['gx'=16,'gy'=8] {'gx','gy'}, dimensions={0} | all-to-all | bytes 4194304 | tf_op jit(solution)/shard_map/all_to_all | solution.py:278
  116.5 1.3 %copy.10 = f32[4096,128]{1,0:T(8,128)} copy(f32[4096,128]{1,0:T(8,128)S(1)} %bitcast.23) | data formatting | bytes 4194304
  (13 shorter events, 0.1 us)
Async XLA Ops:
  1.7 17.3 %copy-start.6 = (s32[1,1,128,32]{2,3,1,0:T(8,128)S(1)}, s32[1,1,128,32]{2,3,1,0:T(8,128)}, u32[]{:S(2)}) copy-start(s32[1,1,128,32]{2,3,1,0:T(8,128)} %param.10) | copy-start | bytes 49156
  3.4 21.9 %copy-start.7 = (s32[1,1,128]{2,1,0:T(1,128)S(1)}, s32[1,1,128]{2,1,0:T(1,128)}, u32[]{:S(2)}) copy-start(s32[1,1,128]{2,1,0:T(1,128)} %param.11) | copy-start | bytes 1540
  4.4 14.7 %collective-permute-start.2 = (f32[64,9,128]{2,1,0:T(8,128)}, f32[64,9,128]{2,1,0:T(8,128)S(1)}, u32[]{:S(2)}, u32[]{:S(2)}) collective-permute-start(f32[64,9,128]{2,1,0:T(8,128)} %pad_maximum_fusion.2), channel_id=1, source_target_pairs={{0,1},{1,2},{2,3},{3,4},{4,5},{5,6},{6,7},{8,9},{9,10},{10,11},{11... | collective-permute-start | bytes 884744 | tf_op jit(solution)/shard_map/ppermute | solution.py:265
  9.8 10.7 %collective-permute-start.3 = (f32[64,9,128]{2,1,0:T(8,128)}, f32[64,9,128]{2,1,0:T(8,128)S(1)}, u32[]{:S(2)}, u32[]{:S(2)}) collective-permute-start(f32[64,9,128]{2,1,0:T(8,128)} %pad_maximum_fusion.3), channel_id=1, source_target_pairs={{1,0},{2,1},{3,2},{4,3},{5,4},{6,5},{7,6},{9,8},{10,9},{11,10},{12... | collective-permute-start | bytes 884744 | tf_op jit(solution)/shard_map/ppermute | solution.py:266
  14.4 19.9 %collective-permute-start = (f32[9,128,128]{2,1,0:T(8,128)S(1)}, f32[9,128,128]{2,1,0:T(8,128)S(1)}, u32[]{:S(2)}, u32[]{:S(2)}) collective-permute-start(f32[9,128,128]{2,1,0:T(8,128)S(1)} %pad_maximum_fusion), channel_id=1, source_target_pairs={{0,8},{8,16},{16,24},{24,32},{32,40},{40,48},{48,56},{56,64},{64,7... | collective-permute-start | bytes 1769480 | tf_op jit(solution)/shard_map/ppermute | solution.py:263
  17.7 16.6 %collective-permute-start.1 = (f32[9,128,128]{2,1,0:T(8,128)S(1)}, f32[9,128,128]{2,1,0:T(8,128)S(1)}, u32[]{:S(2)}, u32[]{:S(2)}) collective-permute-start(f32[9,128,128]{2,1,0:T(8,128)S(1)} %pad_maximum_fusion.1), channel_id=1, source_target_pairs={{8,0},{16,8},{24,16},{32,24},{40,32},{48,40},{56,48},{64,56},{72,6... | collective-permute-start | bytes 1769480 | tf_op jit(solution)/shard_map/ppermute | solution.py:264
  19.1 15.2 %copy-start = (f32[64,9,128]{2,1,0:T(8,128)}, f32[64,9,128]{2,1,0:T(8,128)S(1)}, u32[]{:S(2)}) copy-start(f32[64,9,128]{2,1,0:T(8,128)S(1)} %collective-permute-done.2.ylo_ref) | copy-start | bytes 884740
  20.5 13.8 %copy-start.1 = (f32[64,9,128]{2,1,0:T(8,128)}, f32[64,9,128]{2,1,0:T(8,128)S(1)}, u32[]{:S(2)}) copy-start(f32[64,9,128]{2,1,0:T(8,128)S(1)} %collective-permute-done.3.yhi_ref) | copy-start | bytes 884740
  20.5 9.6 %collective-permute-start.4 = (f32[3,18,128]{2,1,0:T(8,128)S(1)}, f32[3,18,128]{2,1,0:T(8,128)S(1)}, u32[]{:S(2)}, u32[]{:S(2)}) collective-permute-start(f32[3,18,128]{2,1,0:T(8,128)S(1)} %pad_maximum_fusion.4), channel_id=1, source_target_pairs={{0,8},{8,16},{16,24},{24,32},{32,40},{40,48},{48,56},{56,64},{64,7... | collective-permute-start | bytes 82952 | tf_op jit(solution)/shard_map/ppermute | solution.py:267
  24.0 10.3 %collective-permute-start.5 = (f32[3,18,128]{2,1,0:T(8,128)S(1)}, f32[3,18,128]{2,1,0:T(8,128)S(1)}, u32[]{:S(2)}, u32[]{:S(2)}) collective-permute-start(f32[3,18,128]{2,1,0:T(8,128)S(1)} %pad_maximum_fusion.5), channel_id=1, source_target_pairs={{8,0},{16,8},{24,16},{32,24},{40,32},{48,40},{56,48},{64,56},{72,6... | collective-permute-start | bytes 82952 | tf_op jit(solution)/shard_map/ppermute | solution.py:268
  30.1 4.2 %copy-start.4 = (f32[3,18,128]{2,1,0:T(8,128)}, f32[3,18,128]{2,1,0:T(8,128)S(1)}, u32[]{:S(2)}) copy-start(f32[3,18,128]{2,1,0:T(8,128)S(1)} %collective-permute-done.4.clo_ref) | copy-start | bytes 82948
  34.3 0.6 copy-start.5
  34.3 0.8 copy-start.2
  35.1 0.8 copy-start.3

commit v3 on v2

v3 whole, which is shorter than its diff:
```python
import functools

import jax
import jax.numpy as jnp
from jax import lax
from jax.experimental import pallas as pl
from jax.experimental.pallas import tpu as pltpu
from jax.sharding import PartitionSpec as P

STEPS = 3
TICKS = 2000
LATENT = 0.5
SHARE = 0.2
TICK_SHARE = SHARE / TICKS

HALO = 3
EDGE = 8
LEAD = 4
LANES = 128
TILE = 8
OFFSET = 2.0
FAR = 1e-30
CHUNKS = 8
OUTS = 4
UNROLL = 4
PUN = 2
RIM = 3 * HALO
MIB = 1024 * 1024

ANY = pl.BlockSpec(memory_space=pl.ANY)
VMEM = pl.BlockSpec(memory_space=pltpu.VMEM)
SMEM = pl.BlockSpec(memory_space=pltpu.SMEM)


def kelvin(h):
    return jnp.minimum(h, jnp.maximum(h - LATENT, 1.0))


def lifted_kelvin(h):
    return jnp.minimum(h, jnp.maximum(h - LATENT, 1.0 + OFFSET))


def standing(h, bead, birth):
    return jnp.where((birth >= 0) & (birth < STEPS * TICKS), bead, h)


def face(one, two):
    return one[2] * two[2] * pl.reciprocal(one[1] + two[1], approx=True) * (two[0] - one[0])


def tile(j):
    return pl.ds(j * TILE, TILE)


class Slab:
    def __init__(self, raw, grids, rings, acc):
        self.raw = raw
        self.ha, self.hb, self.ks, self.kz, self.bs, self.bz = grids
        self.rings = rings
        self.acc = acc
        self.height = raw[0].shape[1]
        self.span = (self.height - 2 * (EDGE - LEAD)) // TILE

    def natural(self, j):
        return pl.ds(EDGE - LEAD + j, TILE, stride=self.span)

    def place(self, h, k, birth, x, rows):
        inside = k > 0.0
        values = (h, jnp.where(inside, k, 1.0), h, jnp.where(inside, birth, 1e6).astype(jnp.int32))
        for ref, value in zip(self.raw, values):
            ref[x, rows, :] = value

    def prepare(self, x):
        h_v, k_v, bead_v, birth_v = self.raw
        top = lax.broadcasted_iota(jnp.int32, (TILE, LANES), 1) == LANES - 1
        for j in range(self.span):
            at, to = self.natural(j), tile(j)
            birth, k = birth_v[x, at, :], k_v[x, at, :]
            b = birth.astype(jnp.float32) * TICK_SHARE
            self.ha[x, to, :] = standing(h_v[x, at, :], bead_v[x, at, :], birth) + OFFSET
            self.ks[x, to, :] = k
            self.kz[x, to, :] = jnp.where(top, FAR, pltpu.roll(k, LANES - 1, 1))
            self.bs[x, to, :] = b
            self.bz[x, to, :] = pltpu.roll(b, LANES - 1, 1)

    def prepare_all(self, lo, hi):
        @pl.loop(0, (hi - lo) // PUN)
        def _(i):
            for u in range(PUN):
                self.prepare(lo + i * PUN + u)

    def into(self, ref):
        def store(x, j, value):
            ref[x, tile(j), :] = value
        return store

    def run_step(self, step, src, store, base, cuts, after=None):
        span, acc, (ring_a, ring_b) = self.span, self.acc, self.rings

        def share(b):
            return jnp.clip(SHARE * (step + 1) - b, 0.0, SHARE)

        def point(x, j):
            at = tile(j)
            h = src[x, at, :]
            t = lifted_kelvin(h)
            return h, (t, pl.reciprocal(self.ks[x, at, :] * t, approx=True), share(self.bs[x, at, :]))

        def put(ring, j, values):
            for ref, value in zip(ring, values):
                ref[tile(j), :] = value

        def get(ring, j):
            return [ref[tile(j), :] for ref in ring]

        for j in range(span):
            before = point(base + cuts[0] - 1, j)[1]
            h, now = point(base + cuts[0], j)
            put(ring_a, j, now)
            acc[tile(j), :] = h - face(before, now)

        def plane(x, here, there):
            cur = get(here, 0)
            beyond = [pltpu.roll(v, TILE - 1, 0) for v in cur]
            fy_old = pltpu.roll(face(get(here, span - 1), beyond), 1, 0)
            for j in range(span):
                at = tile(j)
                ahead = get(here, j + 1) if j + 1 < span else beyond
                h, nxt = point(x + 1, j)
                put(there, j, nxt)
                fx = face(cur, nxt)
                total = acc[at, :] + fx
                acc[at, :] = h - fx
                fy = face(cur, ahead)
                t = pltpu.roll(cur[0], LANES - 1, 1)
                fz = face(
                    cur, (t, pl.reciprocal(self.kz[x, at, :] * t, approx=True), share(self.bz[x, at, :]))
                )
                store(x, j, total + ((fy - fy_old) + (fz - pltpu.roll(fz, 1, 1))))
                cur, fy_old = ahead, fy

        for n, (lo, hi) in enumerate(zip(cuts[:-1], cuts[1:])):
            unroll = UNROLL if (hi - lo) % UNROLL == 0 else 2

            @pl.loop(0, (hi - lo) // unroll)
            def _(i):
                for u in range(unroll):
                    rings = (ring_a, ring_b) if u % 2 == 0 else (ring_b, ring_a)
                    plane(base + lo + unroll * i + u, *rings)

            if (hi - lo) % 2:
                plane(base + hi - 1, ring_a, ring_b)
            if after is not None:
                after(n)


def slab_scratch(planes, lateral, stack):
    tiles = (lateral + 2 * LEAD, stack)
    raw = (planes, lateral + 2 * EDGE, stack)
    return [
        [pltpu.VMEM(raw, dtype) for dtype in (jnp.float32, jnp.float32, jnp.float32, jnp.int32)],
        [pltpu.VMEM((planes,) + tiles, jnp.float32)] * 6,
        [[pltpu.VMEM(tiles, jnp.float32)] * 3] * 2,
        pltpu.VMEM(tiles, jnp.float32),
    ]


def strip_kernel(
    h_hbm, k_hbm, bead_hbm, birth_hbm, xlo_ref, xhi_ref, ylo_ref, yhi_ref, xs, ys, sem
):
    track, lateral, _ = h_hbm.shape
    copies = []
    for i, hbm in enumerate((h_hbm, k_hbm, bead_hbm, birth_hbm)):
        for side in range(2):
            planes = pl.ds(side * (track - HALO), HALO)
            rows = pl.ds(side * (lateral - EDGE), EDGE)
            copies.append(pltpu.make_async_copy(hbm.at[planes], xs[i].at[side], sem.at[0, i, side]))
            copies.append(pltpu.make_async_copy(hbm.at[:, rows], ys[i].at[side], sem.at[1, i, side]))
    for copy in copies:
        copy.start()
    for copy in copies:
        copy.wait()
    for side, out in ((0, xlo_ref), (1, xhi_ref)):
        @pl.loop(0, HALO)
        def _(d, side=side, out=out):
            birth = xs[3][side, d]
            out[d] = standing(xs[0][side, d], xs[2][side, d], birth)
            out[HALO + d] = xs[1][side, d]
            out[2 * HALO + d] = birth.astype(jnp.float32)
    flat = [ref.reshape(2 * track * EDGE, LANES) for ref in ys]
    for side, out in ((0, ylo_ref), (1, yhi_ref)):
        for i in range(track // TILE):
            for d in range(HALO):
                row = (side * track + i * TILE) * EDGE + d + side * (EDGE - HALO)
                h, k, bead, birth = [ref[pl.ds(row, TILE, stride=EDGE), :] for ref in flat]
                out[d, tile(i), :] = standing(h, bead, birth)
                out[HALO + d, tile(i), :] = k
                out[2 * HALO + d, tile(i), :] = birth.astype(jnp.float32)


def strips(h, k, bead, birth):
    track, lateral, stack = h.shape
    types = (jnp.float32, jnp.float32, jnp.float32, jnp.int32)
    return pl.pallas_call(
        strip_kernel,
        out_shape=(
            jax.ShapeDtypeStruct((3 * HALO, lateral, stack), jnp.float32),
            jax.ShapeDtypeStruct((3 * HALO, lateral, stack), jnp.float32),
            jax.ShapeDtypeStruct((3 * HALO, track, stack), jnp.float32),
            jax.ShapeDtypeStruct((3 * HALO, track, stack), jnp.float32),
        ),
        in_specs=[ANY] * 4,
        out_specs=(VMEM,) * 4,
        scratch_shapes=[
            [pltpu.VMEM((2, HALO, lateral, stack), dtype) for dtype in types],
            [pltpu.VMEM((2, track, EDGE, stack), dtype) for dtype in types],
            pltpu.SemaphoreType.DMA((2, 4, 2)),
        ],
        compiler_params=pltpu.CompilerParams(vmem_limit_bytes=16 * MIB),
    )(h, k, bead, birth)


def inner_kernel(
    h_hbm, k_hbm, bead_hbm, birth_hbm, ylo_ref, yhi_ref, out_hbm, raw, grids, rings, acc, sem_in, sem_out
):
    track, lateral, _ = h_hbm.shape
    slab = Slab(raw, grids, rings, acc)
    inner = pl.ds(EDGE, lateral)
    piece = track // CHUNKS

    def copies(n):
        at = pl.ds(n * piece, piece)
        return [
            pltpu.make_async_copy(hbm.at[at], vmem.at[at, inner], sem_in.at[i, n])
            for i, (hbm, vmem) in enumerate(zip((h_hbm, k_hbm, bead_hbm, birth_hbm), raw))
        ]

    for n in range(CHUNKS):
        for copy in copies(n):
            copy.start()

    height = lateral + 2 * EDGE
    flat = [ref.reshape(track * height, LANES) for ref in raw]
    for ref, first in ((ylo_ref, EDGE - HALO), (yhi_ref, EDGE + lateral)):
        @pl.loop(0, track // TILE)
        def _(i, ref=ref, first=first):
            for d in range(HALO):
                h, k, birth = [ref[f * HALO + d, pl.ds(i * TILE, TILE), :] for f in range(3)]
                at = pl.ds(i * TILE * height + first + d, TILE, stride=height)
                inside = k > 0.0
                flat[0][at, :] = h
                flat[1][at, :] = jnp.where(inside, k, 1.0)
                flat[2][at, :] = h
                flat[3][at, :] = jnp.where(inside, birth, 1e6).astype(jnp.int32)

    for n in range(CHUNKS):
        for copy in copies(n):
            copy.wait()
        slab.prepare_all(n * piece, (n + 1) * piece)

    cuts = [HALO] + [n * (track // OUTS) + HALO for n in range(1, OUTS)] + [track - HALO]

    def out_copy(n):
        at = pl.ds(cuts[n], cuts[n + 1] - cuts[n])
        return pltpu.make_async_copy(raw[0].at[at, inner], out_hbm.at[at], sem_out.at[n])

    def finish(x, j, value):
        raw[0][x, slab.natural(j), :] = value - OFFSET

    slab.run_step(0, slab.ha, slab.into(slab.hb), 0, (1, track - 1))
    slab.run_step(1, slab.hb, slab.into(slab.ha), 0, (2, track - 2))
    slab.run_step(2, slab.ha, finish, 0, cuts, lambda n: out_copy(n).start())
    for n in range(OUTS):
        out_copy(n).wait()


def inner_planes(h, k, bead, birth, ylo, yhi):
    track, lateral, stack = h.shape
    return pl.pallas_call(
        inner_kernel,
        out_shape=jax.ShapeDtypeStruct(h.shape, jnp.float32),
        in_specs=[ANY] * 4 + [VMEM] * 2,
        out_specs=ANY,
        scratch_shapes=slab_scratch(track, lateral, stack) + [
            pltpu.SemaphoreType.DMA((4, CHUNKS)),
            pltpu.SemaphoreType.DMA((OUTS,)),
        ],
        compiler_params=pltpu.CompilerParams(vmem_limit_bytes=52 * MIB),
        cost_estimate=pl.CostEstimate(
            flops=200 * h.size, bytes_accessed=20 * h.size, transcendentals=15 * h.size
        ),
    )(h, k, bead, birth, ylo, yhi)


def rim_kernel(
    index_ref, h_hbm, k_hbm, bead_hbm, birth_hbm, part_hbm, xlo_ref, xhi_ref, ylo_ref, yhi_ref, clo_ref,
    chi_ref, out_hbm, rows_ref, raw, grids, rings, acc, whole, sem_in, sem_part, sem_out,
):
    track, lateral, _ = h_hbm.shape
    slab = Slab(raw, grids, rings, acc)
    inner = pl.ds(EDGE, lateral)
    own = RIM - HALO

    copies = []
    for i, (hbm, vmem) in enumerate(zip((h_hbm, k_hbm, bead_hbm, birth_hbm), raw)):
        for side in range(2):
            src = pl.ds(side * (track - own), own)
            dst = pl.ds(HALO + side * own, own)
            copies.append(pltpu.make_async_copy(hbm.at[src], vmem.at[dst, inner], sem_in.at[i, side]))
    for copy in copies:
        copy.start()
    middle = pl.ds(HALO, track - 2 * HALO)
    part = pltpu.make_async_copy(part_hbm.at[middle], whole.at[middle, inner], sem_part)
    part.start()

    for side, ref in ((0, xlo_ref), (1, xhi_ref)):
        @pl.loop(0, HALO)
        def _(d, side=side, ref=ref):
            slab.place(ref[d], ref[HALO + d], ref[2 * HALO + d], side * (RIM + own) + d, inner)
    for x in range(2 * RIM):
        beyond = x < HALO or x >= HALO + 2 * own
        for y in range(2):
            if beyond:
                ref, plane, first = (clo_ref, chi_ref)[x >= HALO], x % RIM - (own if x >= HALO else 0), y * RIM
            else:
                ref, plane, first = (ylo_ref, yhi_ref)[y], x - HALO + (track - 2 * own if x >= RIM else 0), 0
            for d in range(HALO):
                h, k, birth = [ref[first + f * HALO + d, pl.ds(plane, 1), :] for f in range(3)]
                slab.place(h, k, birth, x, pl.ds((EDGE - HALO, EDGE + lateral)[y] + d, 1))

    for copy in copies:
        copy.wait()
    slab.prepare_all(0, 2 * RIM)

    def finish(x, j, value):
        at = x - HALO + jnp.where(x >= RIM, track - 2 * own, 0)
        whole[at, slab.natural(j), :] = value - OFFSET

    @pl.loop(0, 2)
    def _(side):
        base = side * RIM
        slab.run_step(0, slab.ha, slab.into(slab.hb), base, (1, RIM - 1))
        slab.run_step(1, slab.hb, slab.into(slab.ha), base, (2, RIM - 2))
        slab.run_step(2, slab.ha, finish, base, (3, RIM - 3))

    outs = []
    for side in range(2):
        at = pl.ds(side * (track - HALO), HALO)
        outs.append(pltpu.make_async_copy(whole.at[at, inner], out_hbm.at[at], sem_out.at[side]))
    for copy in outs:
        copy.start()
    part.wait()

    whole[0, 0:EDGE, :] = jnp.zeros((EDGE, LANES), jnp.float32)
    owners, slots = index_ref.shape
    flat = whole.reshape(track * (lateral + 2 * EDGE), LANES)

    @pl.loop(0, owners)
    def _(o):
        for k in range(slots):
            rows_ref[pl.ds(o * slots + k, 1), :] = kelvin(flat[pl.ds(index_ref[o, k], 1), :])

    for copy in outs:
        copy.wait()


def rim_and_rows(index, h, k, bead, birth, part, halos):
    track, lateral, stack = h.shape
    owners, slots = index.shape
    return pl.pallas_call(
        rim_kernel,
        out_shape=(
            jax.ShapeDtypeStruct(h.shape, jnp.float32),
            jax.ShapeDtypeStruct((owners * slots, stack), jnp.float32),
        ),
        in_specs=[SMEM] + [ANY] * 5 + [VMEM] * 6,
        out_specs=(ANY, VMEM),
        input_output_aliases={5: 0},
        scratch_shapes=slab_scratch(2 * RIM, lateral, stack) + [
            pltpu.VMEM((track, lateral + 2 * EDGE, stack), jnp.float32),
            pltpu.SemaphoreType.DMA((4, 2)),
            pltpu.SemaphoreType.DMA,
            pltpu.SemaphoreType.DMA((2,)),
        ],
        compiler_params=pltpu.CompilerParams(vmem_limit_bytes=32 * MIB),
        cost_estimate=pl.CostEstimate(
            flops=50 * h.size, bytes_accessed=6 * h.size, transcendentals=4 * h.size
        ),
    )(index, h, k, bead, birth, part, *halos)


def shift(axis, by):
    count = lax.axis_size(axis)
    return [(i, i + by) for i in range(count) if 0 <= i + by < count]


def per_device(enthalpy, conductivity, bead_enthalpy, birth_time, send_rows, send_counts):
    lateral = enthalpy.shape[1]
    fields = (enthalpy, conductivity, bead_enthalpy, birth_time)

    to_low, to_high, to_left, to_right = strips(*fields)
    ylo = lax.ppermute(to_right, "gy", shift("gy", 1))
    yhi = lax.ppermute(to_left, "gy", shift("gy", -1))
    xlo = lax.ppermute(to_high, "gx", shift("gx", 1))
    xhi = lax.ppermute(to_low, "gx", shift("gx", -1))
    clo = lax.ppermute(jnp.concatenate([ylo[:, -HALO:], yhi[:, -HALO:]], 0), "gx", shift("gx", 1))
    chi = lax.ppermute(jnp.concatenate([ylo[:, :HALO], yhi[:, :HALO]], 0), "gx", shift("gx", -1))

    rows, counts = send_rows[0, 0], send_counts[0, 0]
    slot = jnp.arange(rows.shape[1], dtype=jnp.int32)
    place = rows // lateral * (lateral + 2 * EDGE) + rows % lateral + EDGE
    index = jnp.where(slot[None, :] < counts[:, None], place, 0)

    part = inner_planes(*fields, ylo, yhi)
    end, outgoing = rim_and_rows(index, *fields, part, (xlo, xhi, ylo, yhi, clo, chi))
    outgoing = outgoing.reshape(rows.shape + outgoing.shape[1:])
    received = lax.all_to_all(outgoing, ("gx", "gy"), split_axis=0, concat_axis=0, tiled=True)
    return end, received.reshape(-1, received.shape[-1])


def solution(mesh):
    in_specs = (
        P("gx", "gy", None),
        P("gx", "gy", None),
        P("gx", "gy", None),
        P("gx", "gy", None),
        P("gx", "gy", None, None),
        P("gx", "gy", None),
    )
    out_specs = (P("gx", "gy", None), P(("gx", "gy"), None))
    return jax.shard_map(
        per_device, mesh=mesh, in_specs=in_specs, out_specs=out_specs, check_vma=False
    )
```

time: 118 us -> 119 us (level)
  local copies, waits for them, and re-layouts: 3.09 us -> 15.2 us
  waiting for transfers between devices: 9.62 us -> 0.83 us
  other arithmetic: 8.06 us -> 0.95 us
  Pallas kernels: 37 us -> 40.5 us
    unnamed x18 -> x20, local copies, waits for them, and re-layouts: 3.08 us -> 15.2 us
    ppermute x6, waiting for transfers between devices: 9.62 us -> 0.83 us  [the longest x1 0.81 us: per_device(): yhi = lax.ppermute(to_left, 'gy', shift('gy', -1))]
    pallas_call x1 -> x3, Pallas kernels: 37 us -> 40.5 us  [the longest x1 26 us: inner_planes(): pl.pallas_call(inner_kernel, out_shape=jax.ShapeDtypeStruct(h.shape, jnp....]
    select_n x2 -> x0, other arithmetic: 3.25 us -> none  [fields(): jnp.where(born, bead_enthalpy[cut], enthalpy[cut])]
    convert_element_type x2 -> x0, other arithmetic: 2.13 us -> none  [fields(): birth.astype(jnp.float32)]
    concatenate x6 -> x2, other arithmetic: 1.96 us -> 0.02 us  [the longest x1 0.01 us: per_device(): jnp.concatenate([ylo[:, -HALO:], yhi[:, -HALO:]], 0)]
  transfers between devices with their start and end apart: 6 -> 6, of which waited for: 3 -> 1; matrix products, arithmetic and copies ran while one was open for 4% -> 1% of each run, Pallas kernels for 0% -> 22%
where the time goes in v3:
time: 119 us; the launch traced here: 118 us
  blocking collectives  44.1 us (37%)
  Pallas kernels  40.5 us (34%)
  starting transfers between devices  15.7 us (13%)
  local copies, waits for them, and re-layouts  15.2 us (13%)
    all_to_all x1, blocking collectives, per_device(): lax.all_to_all(outgoing, ('gx', 'gy'), split_axis=0, concat_axis=0, tiled...  44.1 us
    pallas_call x1, Pallas kernels, inner_planes(): pl.pallas_call(inner_kernel, out_shape=jax.ShapeDtypeStruct(h.shape, jnp....  26 us
    unnamed x20, local copies, waits for them, and re-layouts  15.2 us
    pallas_call x1, Pallas kernels, rim_and_rows(): pl.pallas_call(rim_kernel, out_shape=(jax.ShapeDtypeStruct(h.shape, jnp.f...  11.9 us
    ppermute x1, starting transfers between devices, per_device(): ylo = lax.ppermute(to_right, 'gy', shift('gy', 1))  4.51 us
    ppermute x1, starting transfers between devices, per_device(): lax.ppermute(jnp.concatenate([ylo[:, -HALO:], yhi[:, -HALO:]], 0), 'gx',...  3.5 us
    ppermute x1, starting transfers between devices, per_device(): xlo = lax.ppermute(to_high, 'gx', shift('gx', 1))  3.24 us
    pallas_call x1, Pallas kernels, strips(): pl.pallas_call(strip_kernel, out_shape=(jax.ShapeDtypeStruct((3 * HALO, l...  2.69 us
  transfers between devices with their start and end apart: 6, of which 1 were waited for; matrix products, arithmetic and copies ran while one was open for 1% of the time, Pallas kernels for 22%

profile of v3, /device:TPU:1, one launch (start us, length us, event | category | flops | bytes accessed | tf_op | source)
XLA Modules:
  0.0 118.2 jit_solution(13138850785742436257)
XLA Ops:
  0.6 0.0 copy-start
  0.6 2.2 %copy-done = f32[64,128,128]{2,1,0:T(8,128)S(1)} copy-done((f32[64,128,128]{2,1,0:T(8,128)S(1)}, f32[64,128,128]{2,1,0:T(8,128)}, u32[]{:S(2)}) %copy-start) | copy-done | bytes 4194328
  2.8 2.2 %copy-done.2 = f32[64,128,128]{2,1,0:T(8,128)S(1)} copy-done((f32[64,128,128]{2,1,0:T(8,128)S(1)}, f32[64,128,128]{2,1,0:T(8,128)}, u32[]{:S(2)}) %copy-start.2) | copy-done | bytes 4194328
  5.0 2.2 %copy-done.4 = f32[64,128,128]{2,1,0:T(8,128)S(1)} copy-done((f32[64,128,128]{2,1,0:T(8,128)S(1)}, f32[64,128,128]{2,1,0:T(8,128)}, u32[]{:S(2)}) %copy-start.4) | copy-done | bytes 4194328
  7.2 2.2 %copy-done.6 = s32[64,128,128]{2,1,0:T(8,128)S(1)} copy-done((s32[64,128,128]{2,1,0:T(8,128)S(1)}, s32[64,128,128]{2,1,0:T(8,128)}, u32[]{:S(2)}) %copy-start.6) | copy-done | bytes 4194328
  9.4 2.7 %shard_map.77 = (f32[9,128,128]{2,1,0:T(8,128)S(1)}, f32[9,128,128]{2,1,0:T(8,128)S(1)}, f32[9,64,128]{2,1,0:T(8,128)S(1)}, f32[9,64,128]{2,1,0:T(8,128)S(1)}) custom-call(f32[64,128,128]{2,1,0:T(8,128)S(1)} %copy-done, f32[64,128,128]{2,1,0:T(8,128)S(1)} %copy-done.2, f32[64,128,128]{2,1,0:T(8,128)S(1)} %copy-done.4, s32[64,128,128]{2,1,0:T(8,128)S(1)} %copy-done.6), custom_call_target="tpu_custom_call" | custom-call | tf_op jit(solution)/shard_map/pallas_call | solution.py:204
  12.1 4.5 %collective-permute-start = (f32[9,64,128]{2,1,0:T(8,128)S(1)}, f32[9,64,128]{2,1,0:T(8,128)S(1)}, u32[]{:S(2)}, u32[]{:S(2)}) collective-permute-start(f32[9,64,128]{2,1,0:T(8,128)S(1)} %get-tuple-element.8), channel_id=1, source_target_pairs={{0,1},{1,2},{2,3},{3,4},{4,5},{5,6},{6,7},{8,9},{9,10},{10,11},{11... | collective-permute-start | bytes 884744 | tf_op jit(solution)/shard_map/ppermute | solution.py:402
  16.6 1.9 %collective-permute-start.1 = (f32[9,64,128]{2,1,0:T(8,128)S(1)}, f32[9,64,128]{2,1,0:T(8,128)S(1)}, u32[]{:S(2)}, u32[]{:S(2)}) collective-permute-start(f32[9,64,128]{2,1,0:T(8,128)S(1)} %get-tuple-element.9), channel_id=1, source_target_pairs={{1,0},{2,1},{3,2},{4,3},{5,4},{6,5},{7,6},{9,8},{10,9},{11,10},{12... | collective-permute-start | bytes 884744 | tf_op jit(solution)/shard_map/ppermute | solution.py:403
  18.5 3.2 %collective-permute-start.2 = (f32[9,128,128]{2,1,0:T(8,128)S(1)}, f32[9,128,128]{2,1,0:T(8,128)S(1)}, u32[]{:S(2)}, u32[]{:S(2)}) collective-permute-start(f32[9,128,128]{2,1,0:T(8,128)S(1)} %get-tuple-element.10), channel_id=1, source_target_pairs={{0,8},{8,16},{16,24},{24,32},{32,40},{40,48},{48,56},{56,64},{64,7... | collective-permute-start | bytes 1769480 | tf_op jit(solution)/shard_map/ppermute | solution.py:404
  21.8 1.3 %collective-permute-start.3 = (f32[9,128,128]{2,1,0:T(8,128)S(1)}, f32[9,128,128]{2,1,0:T(8,128)S(1)}, u32[]{:S(2)}, u32[]{:S(2)}) collective-permute-start(f32[9,128,128]{2,1,0:T(8,128)S(1)} %get-tuple-element.11), channel_id=1, source_target_pairs={{8,0},{16,8},{24,16},{32,24},{40,32},{48,40},{56,48},{64,56},{72,6... | collective-permute-start | bytes 1769480 | tf_op jit(solution)/shard_map/ppermute | solution.py:405
  23.1 0.0 copy-done.8
  23.1 0.7 copy.9
  23.8 0.0 collective-permute-done.ylo_ref
  23.8 0.8 collective-permute-done.1.yhi_ref
  24.7 3.5 %collective-permute-start.4 = (f32[18,3,128]{2,1,0:T(4,128)S(1)}, f32[18,3,128]{2,1,0:T(4,128)S(1)}, u32[]{:S(2)}, u32[]{:S(2)}) collective-permute-start(f32[18,3,128]{2,1,0:T(4,128)S(1)} %pad_maximum_fusion), channel_id=1, source_target_pairs={{0,8},{8,16},{16,24},{24,32},{32,40},{40,48},{48,56},{56,64},{64,7... | collective-permute-start | bytes 82952 | tf_op jit(solution)/shard_map/ppermute | solution.py:406
  28.2 1.3 %collective-permute-start.5 = (f32[18,3,128]{2,1,0:T(4,128)S(1)}, f32[18,3,128]{2,1,0:T(4,128)S(1)}, u32[]{:S(2)}, u32[]{:S(2)}) collective-permute-start(f32[18,3,128]{2,1,0:T(4,128)S(1)} %pad_maximum_fusion.1), channel_id=1, source_target_pairs={{8,0},{16,8},{24,16},{32,24},{40,32},{48,40},{56,48},{64,56},{72,6... | collective-permute-start | bytes 82952 | tf_op jit(solution)/shard_map/ppermute | solution.py:407
  29.5 0.9 fusion.3.index_ref
  30.4 0.0 copy-start.1
  30.4 0.0 copy-start.3
  30.5 26.0 %shard_map.78.part_hbm = f32[64,128,128]{2,1,0:T(8,128)} custom-call(f32[64,128,128]{2,1,0:T(8,128)} %h_hbm.5, f32[64,128,128]{2,1,0:T(8,128)} %k_hbm.5, f32[64,128,128]{2,1,0:T(8,128)} %bead_hbm.5, s32[64,128,128]{2,1,0:T(8,128)} %birth_hbm.5, f32[9,64,128]{2,1,0:T(8,128)S(1)} %collective-permute-done.ylo_ref, f32[9,64,128]{2,1,0:T(8,128)S(1)} %collective-permute-done.1.yhi_ref), custom_call_target="tpu_custom_call" | custom-call | flops 209715200 | bytes 20971520 | tf_op jit(solution)/shard_map/pallas_call | solution.py:279
  56.4 0.0 collective-permute-done.4.clo_ref
  56.4 0.0 collective-permute-done.5.chi_ref
  56.5 0.0 collective-permute-done.2.xlo_ref
  56.5 0.0 collective-permute-done.3.xhi_ref
  56.5 0.0 copy-done.1
  56.5 0.0 copy-done.3
  56.5 0.0 copy-start.5
  56.5 2.2 %copy-done.5 = f32[64,128,128]{2,1,0:T(8,128)S(1)} copy-done((f32[64,128,128]{2,1,0:T(8,128)S(1)}, f32[64,128,128]{2,1,0:T(8,128)}, u32[]{:S(2)}) %copy-start.5) | copy-done | bytes 4194328
  58.7 2.2 %copy-done.7 = s32[64,128,128]{2,1,0:T(8,128)S(1)} copy-done((s32[64,128,128]{2,1,0:T(8,128)S(1)}, s32[64,128,128]{2,1,0:T(8,128)}, u32[]{:S(2)}) %copy-start.7) | copy-done | bytes 4194328
  60.9 11.9 %shard_map.79 = (f32[64,128,128]{2,1,0:T(8,128)}, f32[4096,128]{1,0:T(8,128)S(1)}) custom-call(s32[128,32]{1,0:T(8,128)S(1)} %fusion.3.index_ref, f32[64,128,128]{2,1,0:T(8,128)S(1)} %copy-done.1, f32[64,128,128]{2,1,0:T(8,128)S(1)} %copy-done.3, f32[64,128,128]{2,1,0:T(8,128)S(1)} %copy-done.5, ...), custom_call_target="tpu_custom_call", output_to_operand_aliasing={{0}: (5, {})} | custom-call | flops 52428800 | bytes 6291456 | tf_op jit(solution)/shard_map/pallas_call | solution.py:370
  72.7 44.1 %all_to_all.5 = f32[128,32,128]{2,1,0:T(8,128)S(1)} all-to-all(f32[128,32,128]{2,1,0:T(8,128)S(1)} %bitcast.23), channel_id=1, replica_groups=mesh['gx'=16,'gy'=8] {'gx','gy'}, dimensions={0} | all-to-all | bytes 4194304 | tf_op jit(solution)/shard_map/all_to_all | solution.py:417
  116.9 1.3 %copy.12 = f32[4096,128]{1,0:T(8,128)} copy(f32[4096,128]{1,0:T(8,128)S(1)} %bitcast.24) | data formatting | bytes 4194304
  (9 shorter events, 0.0 us)
Async XLA Ops:
  0.6 2.2 %copy-start = (f32[64,128,128]{2,1,0:T(8,128)S(1)}, f32[64,128,128]{2,1,0:T(8,128)}, u32[]{:S(2)}) copy-start(f32[64,128,128]{2,1,0:T(8,128)} %h_hbm.5) | copy-start | bytes 12582916
  2.8 2.2 %copy-start.2 = (f32[64,128,128]{2,1,0:T(8,128)S(1)}, f32[64,128,128]{2,1,0:T(8,128)}, u32[]{:S(2)}) copy-start(f32[64,128,128]{2,1,0:T(8,128)} %k_hbm.5) | copy-start | bytes 12582916
  5.0 2.2 %copy-start.4 = (f32[64,128,128]{2,1,0:T(8,128)S(1)}, f32[64,128,128]{2,1,0:T(8,128)}, u32[]{:S(2)}) copy-start(f32[64,128,128]{2,1,0:T(8,128)} %bead_hbm.5) | copy-start | bytes 12582916
  7.2 2.2 %copy-start.6 = (s32[64,128,128]{2,1,0:T(8,128)S(1)}, s32[64,128,128]{2,1,0:T(8,128)}, u32[]{:S(2)}) copy-start(s32[64,128,128]{2,1,0:T(8,128)} %birth_hbm.5) | copy-start | bytes 12582916
  9.4 13.7 %copy-start.8 = (s32[1,1,128,32]{2,3,1,0:T(8,128)S(1)}, s32[1,1,128,32]{2,3,1,0:T(8,128)}, u32[]{:S(2)}) copy-start(s32[1,1,128,32]{2,3,1,0:T(8,128)} %param.10) | copy-start | bytes 49156
  12.1 11.7 %collective-permute-start = (f32[9,64,128]{2,1,0:T(8,128)S(1)}, f32[9,64,128]{2,1,0:T(8,128)S(1)}, u32[]{:S(2)}, u32[]{:S(2)}) collective-permute-start(f32[9,64,128]{2,1,0:T(8,128)S(1)} %get-tuple-element.8), channel_id=1, source_target_pairs={{0,1},{1,2},{2,3},{3,4},{4,5},{5,6},{6,7},{8,9},{9,10},{10,11},{11... | collective-permute-start | bytes 884744 | tf_op jit(solution)/shard_map/ppermute | solution.py:402
  16.6 8.0 %collective-permute-start.1 = (f32[9,64,128]{2,1,0:T(8,128)S(1)}, f32[9,64,128]{2,1,0:T(8,128)S(1)}, u32[]{:S(2)}, u32[]{:S(2)}) collective-permute-start(f32[9,64,128]{2,1,0:T(8,128)S(1)} %get-tuple-element.9), channel_id=1, source_target_pairs={{1,0},{2,1},{3,2},{4,3},{5,4},{6,5},{7,6},{9,8},{10,9},{11,10},{12... | collective-permute-start | bytes 884744 | tf_op jit(solution)/shard_map/ppermute | solution.py:403
  18.5 37.9 %collective-permute-start.2 = (f32[9,128,128]{2,1,0:T(8,128)S(1)}, f32[9,128,128]{2,1,0:T(8,128)S(1)}, u32[]{:S(2)}, u32[]{:S(2)}) collective-permute-start(f32[9,128,128]{2,1,0:T(8,128)S(1)} %get-tuple-element.10), channel_id=1, source_target_pairs={{0,8},{8,16},{16,24},{24,32},{32,40},{40,48},{48,56},{56,64},{64,7... | collective-permute-start | bytes 1769480 | tf_op jit(solution)/shard_map/ppermute | solution.py:404
  21.8 34.7 %collective-permute-start.3 = (f32[9,128,128]{2,1,0:T(8,128)S(1)}, f32[9,128,128]{2,1,0:T(8,128)S(1)}, u32[]{:S(2)}, u32[]{:S(2)}) collective-permute-start(f32[9,128,128]{2,1,0:T(8,128)S(1)} %get-tuple-element.11), channel_id=1, source_target_pairs={{8,0},{16,8},{24,16},{32,24},{40,32},{48,40},{56,48},{64,56},{72,6... | collective-permute-start | bytes 1769480 | tf_op jit(solution)/shard_map/ppermute | solution.py:405
  24.7 31.8 %collective-permute-start.4 = (f32[18,3,128]{2,1,0:T(4,128)S(1)}, f32[18,3,128]{2,1,0:T(4,128)S(1)}, u32[]{:S(2)}, u32[]{:S(2)}) collective-permute-start(f32[18,3,128]{2,1,0:T(4,128)S(1)} %pad_maximum_fusion), channel_id=1, source_target_pairs={{0,8},{8,16},{16,24},{24,32},{32,40},{40,48},{48,56},{56,64},{64,7... | collective-permute-start | bytes 82952 | tf_op jit(solution)/shard_map/ppermute | solution.py:406
  28.2 28.2 %collective-permute-start.5 = (f32[18,3,128]{2,1,0:T(4,128)S(1)}, f32[18,3,128]{2,1,0:T(4,128)S(1)}, u32[]{:S(2)}, u32[]{:S(2)}) collective-permute-start(f32[18,3,128]{2,1,0:T(4,128)S(1)} %pad_maximum_fusion.1), channel_id=1, source_target_pairs={{8,0},{16,8},{24,16},{32,24},{40,32},{48,40},{56,48},{64,56},{72,6... | collective-permute-start | bytes 82952 | tf_op jit(solution)/shard_map/ppermute | solution.py:407
  30.4 26.0 %copy-start.1 = (f32[64,128,128]{2,1,0:T(8,128)S(1)}, f32[64,128,128]{2,1,0:T(8,128)}, u32[]{:S(2)}) copy-start(f32[64,128,128]{2,1,0:T(8,128)} %h_hbm.5) | copy-start | bytes 12582916
  30.4 26.0 %copy-start.3 = (f32[64,128,128]{2,1,0:T(8,128)S(1)}, f32[64,128,128]{2,1,0:T(8,128)}, u32[]{:S(2)}) copy-start(f32[64,128,128]{2,1,0:T(8,128)} %k_hbm.5) | copy-start | bytes 12582916
  56.5 2.2 %copy-start.5 = (f32[64,128,128]{2,1,0:T(8,128)S(1)}, f32[64,128,128]{2,1,0:T(8,128)}, u32[]{:S(2)}) copy-start(f32[64,128,128]{2,1,0:T(8,128)} %bead_hbm.5) | copy-start | bytes 12582916
  58.7 2.2 %copy-start.7 = (s32[64,128,128]{2,1,0:T(8,128)S(1)}, s32[64,128,128]{2,1,0:T(8,128)}, u32[]{:S(2)}) copy-start(s32[64,128,128]{2,1,0:T(8,128)} %birth_hbm.5) | copy-start | bytes 12582916

commit v4 on v3

--- a/solution.py
+++ b/solution.py
@@ -26,6 +26,7 @@
 PUN = 2
 RIM = 3 * HALO
 MIB = 1024 * 1024
+VMEM_ALL = 60 * MIB
 
 ANY = pl.BlockSpec(memory_space=pl.ANY)
 VMEM = pl.BlockSpec(memory_space=pltpu.VMEM)
@@ -184,9 +185,10 @@
         @pl.loop(0, HALO)
         def _(d, side=side, out=out):
             birth = xs[3][side, d]
-            out[d] = standing(xs[0][side, d], xs[2][side, d], birth)
-            out[HALO + d] = xs[1][side, d]
-            out[2 * HALO + d] = birth.astype(jnp.float32)
+            rows = pl.ds(0, lateral)
+            out[d, rows, :] = standing(xs[0][side, d], xs[2][side, d], birth)
+            out[HALO + d, rows, :] = xs[1][side, d]
+            out[2 * HALO + d, rows, :] = birth.astype(jnp.float32)
     flat = [ref.reshape(2 * track * EDGE, LANES) for ref in ys]
     for side, out in ((0, ylo_ref), (1, yhi_ref)):
         for i in range(track // TILE):
@@ -204,8 +206,8 @@
     return pl.pallas_call(
         strip_kernel,
         out_shape=(
-            jax.ShapeDtypeStruct((3 * HALO, lateral, stack), jnp.float32),
-            jax.ShapeDtypeStruct((3 * HALO, lateral, stack), jnp.float32),
+            jax.ShapeDtypeStruct((3 * HALO, lateral + EDGE, stack), jnp.float32),
+            jax.ShapeDtypeStruct((3 * HALO, lateral + EDGE, stack), jnp.float32),
             jax.ShapeDtypeStruct((3 * HALO, track, stack), jnp.float32),
             jax.ShapeDtypeStruct((3 * HALO, track, stack), jnp.float32),
         ),
@@ -216,7 +218,7 @@
             [pltpu.VMEM((2, track, EDGE, stack), dtype) for dtype in types],
             pltpu.SemaphoreType.DMA((2, 4, 2)),
         ],
-        compiler_params=pltpu.CompilerParams(vmem_limit_bytes=16 * MIB),
+        compiler_params=pltpu.CompilerParams(vmem_limit_bytes=VMEM_ALL),
     )(h, k, bead, birth)
 
 
@@ -285,7 +287,7 @@
             pltpu.SemaphoreType.DMA((4, CHUNKS)),
             pltpu.SemaphoreType.DMA((OUTS,)),
         ],
-        compiler_params=pltpu.CompilerParams(vmem_limit_bytes=52 * MIB),
+        compiler_params=pltpu.CompilerParams(vmem_limit_bytes=58 * MIB),
         cost_estimate=pl.CostEstimate(
             flops=200 * h.size, bytes_accessed=20 * h.size, transcendentals=15 * h.size
         ),
@@ -293,8 +295,8 @@
 
 
 def rim_kernel(
-    index_ref, h_hbm, k_hbm, bead_hbm, birth_hbm, part_hbm, xlo_ref, xhi_ref, ylo_ref, yhi_ref, clo_ref,
-    chi_ref, out_hbm, rows_ref, raw, grids, rings, acc, whole, sem_in, sem_part, sem_out,
+    index_ref, h_hbm, k_hbm, bead_hbm, birth_hbm, part_hbm, xlo_ref, xhi_ref, ylo_ref, yhi_ref,
+    out_hbm, rows_ref, raw, grids, rings, acc, whole, sem_in, sem_part, sem_out,
 ):
     track, lateral, _ = h_hbm.shape
     slab = Slab(raw, grids, rings, acc)
@@ -313,20 +315,20 @@
     part = pltpu.make_async_copy(part_hbm.at[middle], whole.at[middle, inner], sem_part)
     part.start()
 
+    below, above = pl.ds(EDGE - HALO, HALO), pl.ds(EDGE + lateral, HALO)
     for side, ref in ((0, xlo_ref), (1, xhi_ref)):
         @pl.loop(0, HALO)
         def _(d, side=side, ref=ref):
-            slab.place(ref[d], ref[HALO + d], ref[2 * HALO + d], side * (RIM + own) + d, inner)
-    for x in range(2 * RIM):
-        beyond = x < HALO or x >= HALO + 2 * own
-        for y in range(2):
-            if beyond:
-                ref, plane, first = (clo_ref, chi_ref)[x >= HALO], x % RIM - (own if x >= HALO else 0), y * RIM
-            else:
-                ref, plane, first = (ylo_ref, yhi_ref)[y], x - HALO + (track - 2 * own if x >= RIM else 0), 0
+            for first, n, rows in ((0, lateral, inner), (lateral, HALO, below), (lateral + HALO, HALO, above)):
+                slab.place(
+                    *[ref[f * HALO + d, pl.ds(first, n), :] for f in range(3)], side * (RIM + own) + d, rows
+                )
+    for x in range(HALO, HALO + 2 * own):
+        at = pl.ds(x - HALO + (track - 2 * own if x >= RIM else 0), 1)
+        for y, ref in enumerate((ylo_ref, yhi_ref)):
             for d in range(HALO):
-                h, k, birth = [ref[first + f * HALO + d, pl.ds(plane, 1), :] for f in range(3)]
-                slab.place(h, k, birth, x, pl.ds((EDGE - HALO, EDGE + lateral)[y] + d, 1))
+                row = pl.ds((EDGE - HALO, EDGE + lateral)[y] + d, 1)
+                slab.place(*[ref[f * HALO + d, at, :] for f in range(3)], x, row)
 
     for copy in copies:
         copy.wait()
@@ -373,7 +375,7 @@
             jax.ShapeDtypeStruct(h.shape, jnp.float32),
             jax.ShapeDtypeStruct((owners * slots, stack), jnp.float32),
         ),
-        in_specs=[SMEM] + [ANY] * 5 + [VMEM] * 6,
+        in_specs=[SMEM] + [ANY] * 5 + [VMEM] * 4,
         out_specs=(ANY, VMEM),
         input_output_aliases={5: 0},
         scratch_shapes=slab_scratch(2 * RIM, lateral, stack) + [
@@ -382,7 +384,7 @@
             pltpu.SemaphoreType.DMA,
             pltpu.SemaphoreType.DMA((2,)),
         ],
-        compiler_params=pltpu.CompilerParams(vmem_limit_bytes=32 * MIB),
+        compiler_params=pltpu.CompilerParams(vmem_limit_bytes=VMEM_ALL),
         cost_estimate=pl.CostEstimate(
             flops=50 * h.size, bytes_accessed=6 * h.size, transcendentals=4 * h.size
         ),
@@ -401,10 +403,14 @@
     to_low, to_high, to_left, to_right = strips(*fields)
     ylo = lax.ppermute(to_right, "gy", shift("gy", 1))
     yhi = lax.ppermute(to_left, "gy", shift("gy", -1))
-    xlo = lax.ppermute(to_high, "gx", shift("gx", 1))
-    xhi = lax.ppermute(to_low, "gx", shift("gx", -1))
-    clo = lax.ppermute(jnp.concatenate([ylo[:, -HALO:], yhi[:, -HALO:]], 0), "gx", shift("gx", 1))
-    chi = lax.ppermute(jnp.concatenate([ylo[:, :HALO], yhi[:, :HALO]], 0), "gx", shift("gx", -1))
+
+    def with_corners(strip, cut):
+        corners = [y[:, cut].reshape(3, HALO, HALO, -1).swapaxes(1, 2) for y in (ylo, yhi)]
+        corners = jnp.concatenate(corners, 2).reshape(3 * HALO, 2 * HALO, -1)
+        return lax.dynamic_update_slice(strip, corners, (0, lateral, 0))
+
+    xlo = lax.ppermute(with_corners(to_high, slice(-HALO, None)), "gx", shift("gx", 1))
+    xhi = lax.ppermute(with_corners(to_low, slice(0, HALO)), "gx", shift("gx", -1))
 
     rows, counts = send_rows[0, 0], send_counts[0, 0]
     slot = jnp.arange(rows.shape[1], dtype=jnp.int32)
@@ -412,7 +418,7 @@
     index = jnp.where(slot[None, :] < counts[:, None], place, 0)
 
     part = inner_planes(*fields, ylo, yhi)
-    end, outgoing = rim_and_rows(index, *fields, part, (xlo, xhi, ylo, yhi, clo, chi))
+    end, outgoing = rim_and_rows(index, *fields, part, (xlo, xhi, ylo, yhi))
     outgoing = outgoing.reshape(rows.shape + outgoing.shape[1:])
     received = lax.all_to_all(outgoing, ("gx", "gy"), split_axis=0, concat_axis=0, tiled=True)
     return end, received.reshape(-1, received.shape[-1])

time: 119 us -> 111 us (0.933)
  local copies, waits for them, and re-layouts: 15.2 us -> 5.96 us
  waiting for transfers between devices: 0.83 us -> 6.32 us
  starting transfers between devices: 15.7 us -> 10.9 us
  Pallas kernels: 40.5 us -> 45 us
  blocking collectives: 44.1 us -> 41.1 us
    unnamed x20 -> x14, local copies, waits for them, and re-layouts: 15.2 us -> 3.07 us
    ppermute x4 -> x2, starting transfers between devices: 9.32 us -> 4.51 us  [the longest x1 3.23 us: per_device(): lax.ppermute(with_corners(to_high, slice(-HALO, None)), 'gx', shift('gx',...]
    ppermute x1, waiting for transfers between devices: 0.81 us -> 4.28 us  [per_device(): yhi = lax.ppermute(to_left, 'gy', shift('gy', -1))]
    all_to_all x1, blocking collectives: 44.1 us -> 41.1 us  [per_device(): lax.all_to_all(outgoing, ('gx', 'gy'), split_axis=0, concat_axis=0, tiled...]
    dynamic_update_slice x0 -> x2, local copies, waits for them, and re-layouts: none -> 2.86 us  [with_corners(): return lax.dynamic_update_slice(strip, corners, (0, lateral, 0))]
    pallas_call x1, Pallas kernels: 11.9 us -> 14.5 us  [rim_and_rows(): pl.pallas_call(rim_kernel, out_shape=(jax.ShapeDtypeStruct(h.shape, jnp.f...]
    ppermute x1, waiting for transfers between devices: 0.01 us -> 2.03 us  [per_device(): ylo = lax.ppermute(to_right, 'gy', shift('gy', 1))]
  transfers between devices with their start and end apart: 6 -> 4, of which waited for: 1 -> 2; matrix products, arithmetic and copies ran while one was open for 1% -> 2% of each run, Pallas kernels for 22% -> 24%
where the time goes in v4:
time: 111 us
  Pallas kernels  45 us (41%)
  blocking collectives  41.1 us (37%)
  starting transfers between devices  10.9 us (10%)
  waiting for transfers between devices  6.32 us (6%)
  local copies, waits for them, and re-layouts  5.96 us (5%)
    all_to_all x1, blocking collectives, per_device(): lax.all_to_all(outgoing, ('gx', 'gy'), split_axis=0, concat_axis=0, tiled...  41.1 us
    pallas_call x1, Pallas kernels, inner_planes(): pl.pallas_call(inner_kernel, out_shape=jax.ShapeDtypeStruct(h.shape, jnp....  26.9 us
    pallas_call x1, Pallas kernels, rim_and_rows(): pl.pallas_call(rim_kernel, out_shape=(jax.ShapeDtypeStruct(h.shape, jnp.f...  14.5 us
    ppermute x1, starting transfers between devices, per_device(): ylo = lax.ppermute(to_right, 'gy', shift('gy', 1))  4.51 us
    ppermute x1, waiting for transfers between devices, per_device(): yhi = lax.ppermute(to_left, 'gy', shift('gy', -1))  4.28 us
    pallas_call x1, Pallas kernels, strips(): pl.pallas_call(strip_kernel, out_shape=(jax.ShapeDtypeStruct((3 * HALO, l...  3.57 us
    ppermute x1, starting transfers between devices, per_device(): lax.ppermute(with_corners(to_high, slice(-HALO, None)), 'gx', shift('gx',...  3.23 us
    unnamed x14, local copies, waits for them, and re-layouts  3.07 us
  transfers between devices with their start and end apart: 4, of which 2 were waited for; matrix products, arithmetic and copies ran while one was open for 2% of the time, Pallas kernels for 24%

profile of v4, /device:TPU:1, one launch (start us, length us, event | category | flops | bytes accessed | tf_op | source)
XLA Modules:
  0.0 110.8 jit_solution(16749247078323426447)
XLA Ops:
  0.6 0.0 copy-start.4
  0.6 0.0 copy-start.5
  0.6 3.6 %shard_map.77 = (f32[9,136,128]{2,1,0:T(8,128)}, f32[9,136,128]{2,1,0:T(8,128)}, f32[9,64,128]{2,1,0:T(8,128)}, f32[9,64,128]{2,1,0:T(8,128)}) custom-call(f32[64,128,128]{2,1,0:T(8,128)} %h_hbm.5, f32[64,128,128]{2,1,0:T(8,128)} %k_hbm.5, f32[64,128,128]{2,1,0:T(8,128)} %bead_hbm.5, s32[64,128,128]{2,1,0:T(8,128)} %birth_hbm.5), custom_call_target="tpu_custom_call" | custom-call | tf_op jit(solution)/shard_map/pallas_call | solution.py:206
  4.2 4.5 %collective-permute-start = (f32[9,64,128]{2,1,0:T(8,128)}, f32[9,64,128]{2,1,0:T(8,128)S(1)}, u32[]{:S(2)}, u32[]{:S(2)}) collective-permute-start(f32[9,64,128]{2,1,0:T(8,128)} %get-tuple-element.8), channel_id=1, source_target_pairs={{0,1},{1,2},{2,3},{3,4},{4,5},{5,6},{6,7},{8,9},{9,10},{10,11},{11... | collective-permute-start | bytes 884744 | tf_op jit(solution)/shard_map/ppermute | solution.py:404
  8.7 1.9 %collective-permute-start.1 = (f32[9,64,128]{2,1,0:T(8,128)}, f32[9,64,128]{2,1,0:T(8,128)S(1)}, u32[]{:S(2)}, u32[]{:S(2)}) collective-permute-start(f32[9,64,128]{2,1,0:T(8,128)} %get-tuple-element.9), channel_id=1, source_target_pairs={{1,0},{2,1},{3,2},{4,3},{5,4},{6,5},{7,6},{9,8},{10,9},{11,10},{12... | collective-permute-start | bytes 884744 | tf_op jit(solution)/shard_map/ppermute | solution.py:405
  10.7 2.0 %collective-permute-done.ylo_ref = f32[9,64,128]{2,1,0:T(8,128)S(1)} collective-permute-done((f32[9,64,128]{2,1,0:T(8,128)}, f32[9,64,128]{2,1,0:T(8,128)S(1)}, u32[]{:S(2)}, u32[]{:S(2)}) %collective-permute-start) | collective-permute-done | bytes 294944 | tf_op jit(solution)/shard_map/ppermute | solution.py:404
  12.7 0.0 copy-start.2
  12.7 4.3 %collective-permute-done.1.yhi_ref = f32[9,64,128]{2,1,0:T(8,128)S(1)} collective-permute-done((f32[9,64,128]{2,1,0:T(8,128)}, f32[9,64,128]{2,1,0:T(8,128)S(1)}, u32[]{:S(2)}, u32[]{:S(2)}) %collective-permute-start.1) | collective-permute-done | bytes 294944 | tf_op jit(solution)/shard_map/ppermute | solution.py:405
  17.0 0.0 copy-start.3
  17.1 1.4 %dynamic_update_slice.6 = f32[9,136,128]{2,1,0:T(8,128)} dynamic-update-slice(f32[9,136,128]{2,1,0:T(8,128)} %get-tuple-element.10, f32[9,6,128]{2,1,0:T(8,128)S(1)} %bitcast.40, s32[]{:T(128)} %constant.26.clone.1, s32[]{:T(128)} %constant.31.clone.1, s32[]{:T(128)} %constant.26.clone.1) | dynamic-update-slice | bytes 55300 | tf_op jit(solution)/shard_map/dynamic_update_slice | solution.py:410
  18.5 3.2 %collective-permute-start.2 = (f32[9,136,128]{2,1,0:T(8,128)}, f32[9,136,128]{2,1,0:T(8,128)S(1)}, u32[]{:S(2)}, u32[]{:S(2)}) collective-permute-start(f32[9,136,128]{2,1,0:T(8,128)} %dynamic_update_slice.6), channel_id=1, source_target_pairs={{0,8},{8,16},{16,24},{24,32},{32,40},{40,48},{48,56},{56,64},{64,7... | collective-permute-start | bytes 1880072 | tf_op jit(solution)/shard_map/ppermute | solution.py:412
  21.8 1.4 %dynamic_update_slice.7 = f32[9,136,128]{2,1,0:T(8,128)} dynamic-update-slice(f32[9,136,128]{2,1,0:T(8,128)} %get-tuple-element.11, f32[9,6,128]{2,1,0:T(8,128)S(1)} %bitcast.39, s32[]{:T(128)} %constant.26.clone.1, s32[]{:T(128)} %constant.31.clone.1, s32[]{:T(128)} %constant.26.clone.1) | dynamic-update-slice | bytes 55300 | tf_op jit(solution)/shard_map/dynamic_update_slice | solution.py:410
  23.2 1.3 %collective-permute-start.3 = (f32[9,136,128]{2,1,0:T(8,128)}, f32[9,136,128]{2,1,0:T(8,128)S(1)}, u32[]{:S(2)}, u32[]{:S(2)}) collective-permute-start(f32[9,136,128]{2,1,0:T(8,128)} %dynamic_update_slice.7), channel_id=1, source_target_pairs={{8,0},{16,8},{24,16},{32,24},{40,32},{48,40},{56,48},{64,56},{72,6... | collective-permute-start | bytes 1880072 | tf_op jit(solution)/shard_map/ppermute | solution.py:413
  24.5 0.0 copy-done.4
  24.5 0.1 copy.9
  24.6 0.0 copy-done.5
  24.6 0.7 fusion.3.index_ref
  25.3 0.0 copy-done.2
  25.3 0.0 copy-done.3
  25.3 26.9 %shard_map.78.part_hbm = f32[64,128,128]{2,1,0:T(8,128)} custom-call(f32[64,128,128]{2,1,0:T(8,128)} %h_hbm.5, f32[64,128,128]{2,1,0:T(8,128)} %k_hbm.5, f32[64,128,128]{2,1,0:T(8,128)} %bead_hbm.5, s32[64,128,128]{2,1,0:T(8,128)} %birth_hbm.5, f32[9,64,128]{2,1,0:T(8,128)} %copy-done.2, f32[9,64,128]{2,1,0:T(8,128)} %copy-done.3), custom_call_target="tpu_custom_call" | custom-call | flops 209715200 | bytes 20971520 | tf_op jit(solution)/shard_map/pallas_call | solution.py:281
  52.2 0.0 collective-permute-done.2.xlo_ref
  52.2 0.0 copy-start
  52.2 0.0 collective-permute-done.3.xhi_ref
  52.2 0.8 copy-done
  53.0 0.0 copy-start.1
  53.0 0.8 copy-done.1
  53.8 14.5 %shard_map.79 = (f32[64,128,128]{2,1,0:T(8,128)}, f32[4096,128]{1,0:T(8,128)}) custom-call(s32[128,32]{1,0:T(8,128)} %fusion.3.index_ref, f32[64,128,128]{2,1,0:T(8,128)} %h_hbm.5, f32[64,128,128]{2,1,0:T(8,128)} %k_hbm.5, f32[64,128,128]{2,1,0:T(8,128)} %bead_hbm.5, s32[64,128,128]{2,1,0:T(8,128)} %birth_hbm.5, ...), custom_call_target="tpu_custom_call", output_to_operand_aliasing={{0}: (5, {})} | custom-call | flops 52428800 | bytes 6291456 | tf_op jit(solution)/shard_map/pallas_call | solution.py:372
  68.4 41.1 %all_to_all.5 = f32[128,32,128]{2,1,0:T(8,128)S(1)} all-to-all(f32[128,32,128]{2,1,0:T(8,128)} %bitcast.38), channel_id=1, replica_groups=mesh['gx'=16,'gy'=8] {'gx','gy'}, dimensions={0} | all-to-all | bytes 4194304 | tf_op jit(solution)/shard_map/all_to_all | solution.py:423
  109.5 1.3 %copy.16 = f32[4096,128]{1,0:T(8,128)} copy(f32[4096,128]{1,0:T(8,128)S(1)} %bitcast.37) | data formatting | bytes 4194304
  (6 shorter events, 0.1 us)
Async XLA Ops:
  0.6 23.8 %copy-start.4 = (s32[1,1,128,32]{2,3,1,0:T(8,128)S(1)}, s32[1,1,128,32]{2,3,1,0:T(8,128)}, u32[]{:S(2)}) copy-start(s32[1,1,128,32]{2,3,1,0:T(8,128)} %param.10) | copy-start | bytes 49156
  0.6 23.9 %copy-start.5 = (s32[1,1,128]{2,1,0:T(1,128)S(1)}, s32[1,1,128]{2,1,0:T(1,128)}, u32[]{:S(2)}) copy-start(s32[1,1,128]{2,1,0:T(1,128)} %param.11) | copy-start | bytes 1540
  4.2 8.5 %collective-permute-start = (f32[9,64,128]{2,1,0:T(8,128)}, f32[9,64,128]{2,1,0:T(8,128)S(1)}, u32[]{:S(2)}, u32[]{:S(2)}) collective-permute-start(f32[9,64,128]{2,1,0:T(8,128)} %get-tuple-element.8), channel_id=1, source_target_pairs={{0,1},{1,2},{2,3},{3,4},{4,5},{5,6},{6,7},{8,9},{9,10},{10,11},{11... | collective-permute-start | bytes 884744 | tf_op jit(solution)/shard_map/ppermute | solution.py:404
  8.7 8.3 %collective-permute-start.1 = (f32[9,64,128]{2,1,0:T(8,128)}, f32[9,64,128]{2,1,0:T(8,128)S(1)}, u32[]{:S(2)}, u32[]{:S(2)}) collective-permute-start(f32[9,64,128]{2,1,0:T(8,128)} %get-tuple-element.9), channel_id=1, source_target_pairs={{1,0},{2,1},{3,2},{4,3},{5,4},{6,5},{7,6},{9,8},{10,9},{11,10},{12... | collective-permute-start | bytes 884744 | tf_op jit(solution)/shard_map/ppermute | solution.py:405
  12.7 12.6 %copy-start.2 = (f32[9,64,128]{2,1,0:T(8,128)}, f32[9,64,128]{2,1,0:T(8,128)S(1)}, u32[]{:S(2)}) copy-start(f32[9,64,128]{2,1,0:T(8,128)S(1)} %collective-permute-done.ylo_ref) | copy-start | bytes 884740
  17.0 8.3 %copy-start.3 = (f32[9,64,128]{2,1,0:T(8,128)}, f32[9,64,128]{2,1,0:T(8,128)S(1)}, u32[]{:S(2)}) copy-start(f32[9,64,128]{2,1,0:T(8,128)S(1)} %collective-permute-done.1.yhi_ref) | copy-start | bytes 884740
  18.5 33.7 %collective-permute-start.2 = (f32[9,136,128]{2,1,0:T(8,128)}, f32[9,136,128]{2,1,0:T(8,128)S(1)}, u32[]{:S(2)}, u32[]{:S(2)}) collective-permute-start(f32[9,136,128]{2,1,0:T(8,128)} %dynamic_update_slice.6), channel_id=1, source_target_pairs={{0,8},{8,16},{16,24},{24,32},{32,40},{40,48},{48,56},{56,64},{64,7... | collective-permute-start | bytes 1880072 | tf_op jit(solution)/shard_map/ppermute | solution.py:412
  23.2 29.0 %collective-permute-start.3 = (f32[9,136,128]{2,1,0:T(8,128)}, f32[9,136,128]{2,1,0:T(8,128)S(1)}, u32[]{:S(2)}, u32[]{:S(2)}) collective-permute-start(f32[9,136,128]{2,1,0:T(8,128)} %dynamic_update_slice.7), channel_id=1, source_target_pairs={{8,0},{16,8},{24,16},{32,24},{40,32},{48,40},{56,48},{64,56},{72,6... | collective-permute-start | bytes 1880072 | tf_op jit(solution)/shard_map/ppermute | solution.py:413
  52.2 0.8 copy-start
  53.0 0.8 copy-start.1

commit v5 on v4

--- a/solution.py
+++ b/solution.py
@@ -23,12 +23,13 @@
 CHUNKS = 8
 OUTS = 4
 UNROLL = 4
+ROLL_UP = 2
+ROLL_DOWN = 2
 PUN = 2
 RIM = 3 * HALO
-MIB = 1024 * 1024
-VMEM_ALL = 60 * MIB
-
-ANY = pl.BlockSpec(memory_space=pl.ANY)
+LIMIT = 60 * 1024 * 1024
+
+HBM = pl.BlockSpec(memory_space=pl.ANY)
 VMEM = pl.BlockSpec(memory_space=pltpu.VMEM)
 SMEM = pl.BlockSpec(memory_space=pltpu.SMEM)
 
@@ -95,7 +96,7 @@
             ref[x, tile(j), :] = value
         return store
 
-    def run_step(self, step, src, store, base, cuts, after=None):
+    def run_step(self, step, src, store, base, cuts, before=None, after=None):
         span, acc, (ring_a, ring_b) = self.span, self.acc, self.rings
 
         def share(b):
@@ -114,43 +115,69 @@
         def get(ring, j):
             return [ref[tile(j), :] for ref in ring]
 
+        if before is not None:
+            before(0)
         for j in range(span):
-            before = point(base + cuts[0] - 1, j)[1]
+            last = point(base + cuts[0] - 1, j)[1]
             h, now = point(base + cuts[0], j)
             put(ring_a, j, now)
-            acc[tile(j), :] = h - face(before, now)
-
-        def plane(x, here, there):
-            cur = get(here, 0)
-            beyond = [pltpu.roll(v, TILE - 1, 0) for v in cur]
-            fy_old = pltpu.roll(face(get(here, span - 1), beyond), 1, 0)
-            for j in range(span):
+            acc[tile(j), :] = h - face(last, now)
+
+        def planes(xs, rings):
+            slots = []
+
+            def load(x, here, there, j):
+                cur = get(here, j)
+                slot = dict(x=x, j=j, cur=cur, up=pltpu.roll(cur[0], LANES - 1, 1))
+                if j == 0:
+                    slot["beyond"] = [pltpu.roll(v, TILE - 1, 0) for v in cur]
+                    slot["fy_old"] = pltpu.roll(face(get(here, span - 1), slot["beyond"]), 1, 0)
+                slot["h"], slot["nxt"] = point(x + 1, j)
+                put(there, j, slot["nxt"])
+                return slot
+
+            def work(n):
+                slot = slots[n]
+                x, j, cur, t = slot["x"], slot["j"], slot["cur"], slot["up"]
                 at = tile(j)
-                ahead = get(here, j + 1) if j + 1 < span else beyond
-                h, nxt = point(x + 1, j)
-                put(there, j, nxt)
-                fx = face(cur, nxt)
+                fx = face(cur, slot["nxt"])
                 total = acc[at, :] + fx
-                acc[at, :] = h - fx
-                fy = face(cur, ahead)
-                t = pltpu.roll(cur[0], LANES - 1, 1)
+                acc[at, :] = slot["h"] - fx
+                last = j + 1 == span
+                fy = face(cur, slots[n - j]["beyond"] if last else slots[n + 1]["cur"])
+                if not last:
+                    slots[n + 1]["fy_old"] = fy
                 fz = face(
                     cur, (t, pl.reciprocal(self.kz[x, at, :] * t, approx=True), share(self.bz[x, at, :]))
                 )
-                store(x, j, total + ((fy - fy_old) + (fz - pltpu.roll(fz, 1, 1))))
-                cur, fy_old = ahead, fy
-
+                slot["total"] = total + ((fy - slot["fy_old"]) + fz)
+                slot["down"] = pltpu.roll(fz, 1, 1)
+
+            def done(n):
+                slot = slots[n]
+                store(slot["x"], slot["j"], slot["total"] - slot["down"])
+
+            todo = [(x, *pair, j) for x, pair in zip(xs, rings) for j in range(span)]
+            for n in range(len(todo) + ROLL_UP + ROLL_DOWN):
+                if n < len(todo):
+                    slots.append(load(*todo[n]))
+                if 0 <= n - ROLL_UP < len(todo):
+                    work(n - ROLL_UP)
+                if 0 <= n - ROLL_UP - ROLL_DOWN:
+                    done(n - ROLL_UP - ROLL_DOWN)
+
+        both = [(ring_a, ring_b), (ring_b, ring_a)]
         for n, (lo, hi) in enumerate(zip(cuts[:-1], cuts[1:])):
             unroll = UNROLL if (hi - lo) % UNROLL == 0 else 2
+            if n and before is not None:
+                before(n)
 
             @pl.loop(0, (hi - lo) // unroll)
             def _(i):
-                for u in range(unroll):
-                    rings = (ring_a, ring_b) if u % 2 == 0 else (ring_b, ring_a)
-                    plane(base + lo + unroll * i + u, *rings)
+                planes([base + lo + unroll * i + u for u in range(unroll)], both * (unroll // 2))
 
             if (hi - lo) % 2:
-                plane(base + hi - 1, ring_a, ring_b)
+                planes([base + hi - 1], both[:1])
             if after is not None:
                 after(n)
 
@@ -166,31 +193,18 @@
     ]
 
 
-def strip_kernel(
-    h_hbm, k_hbm, bead_hbm, birth_hbm, xlo_ref, xhi_ref, ylo_ref, yhi_ref, xs, ys, sem
-):
+def lateral_kernel(h_hbm, k_hbm, bead_hbm, birth_hbm, lo_ref, hi_ref, ys, sem):
     track, lateral, _ = h_hbm.shape
-    copies = []
-    for i, hbm in enumerate((h_hbm, k_hbm, bead_hbm, birth_hbm)):
-        for side in range(2):
-            planes = pl.ds(side * (track - HALO), HALO)
-            rows = pl.ds(side * (lateral - EDGE), EDGE)
-            copies.append(pltpu.make_async_copy(hbm.at[planes], xs[i].at[side], sem.at[0, i, side]))
-            copies.append(pltpu.make_async_copy(hbm.at[:, rows], ys[i].at[side], sem.at[1, i, side]))
+    copies = [
+        pltpu.make_async_copy(hbm.at[:, pl.ds(side * (lateral - EDGE), EDGE)], ys[i].at[side], sem.at[i, side])
+        for i, hbm in enumerate((h_hbm, k_hbm, bead_hbm, birth_hbm)) for side in range(2)
+    ]
     for copy in copies:
         copy.start()
     for copy in copies:
         copy.wait()
-    for side, out in ((0, xlo_ref), (1, xhi_ref)):
-        @pl.loop(0, HALO)
-        def _(d, side=side, out=out):
-            birth = xs[3][side, d]
-            rows = pl.ds(0, lateral)
-            out[d, rows, :] = standing(xs[0][side, d], xs[2][side, d], birth)
-            out[HALO + d, rows, :] = xs[1][side, d]
-            out[2 * HALO + d, rows, :] = birth.astype(jnp.float32)
     flat = [ref.reshape(2 * track * EDGE, LANES) for ref in ys]
-    for side, out in ((0, ylo_ref), (1, yhi_ref)):
+    for side, out in ((0, lo_ref), (1, hi_ref)):
         for i in range(track // TILE):
             for d in range(HALO):
                 row = (side * track + i * TILE) * EDGE + d + side * (EDGE - HALO)
@@ -200,26 +214,73 @@
                 out[2 * HALO + d, tile(i), :] = birth.astype(jnp.float32)
 
 
-def strips(h, k, bead, birth):
-    track, lateral, stack = h.shape
-    types = (jnp.float32, jnp.float32, jnp.float32, jnp.int32)
+def track_kernel(h_hbm, k_hbm, bead_hbm, birth_hbm, lo_ref, hi_ref, xs, sem):
+    track, lateral, _ = h_hbm.shape
+    copies = [
+        pltpu.make_async_copy(hbm.at[pl.ds(side * (track - HALO), HALO)], xs[i].at[side], sem.at[i, side])
+        for i, hbm in enumerate((h_hbm, k_hbm, bead_hbm, birth_hbm)) for side in range(2)
+    ]
+    for copy in copies:
+        copy.start()
+    for copy in copies:
+        copy.wait()
+    rows = pl.ds(0, lateral)
+    for side, out in ((0, lo_ref), (1, hi_ref)):
+        @pl.loop(0, HALO)
+        def _(d, side=side, out=out):
+            birth = xs[3][side, d]
+            out[d, rows, :] = standing(xs[0][side, d], xs[2][side, d], birth)
+            out[HALO + d, rows, :] = xs[1][side, d]
+            out[2 * HALO + d, rows, :] = birth.astype(jnp.float32)
+
+
+def strips(kernel, fields, length, held):
+    stack = fields[0].shape[2]
+    out = jax.ShapeDtypeStruct((3 * HALO, length, stack), jnp.float32)
     return pl.pallas_call(
-        strip_kernel,
-        out_shape=(
-            jax.ShapeDtypeStruct((3 * HALO, lateral + EDGE, stack), jnp.float32),
-            jax.ShapeDtypeStruct((3 * HALO, lateral + EDGE, stack), jnp.float32),
-            jax.ShapeDtypeStruct((3 * HALO, track, stack), jnp.float32),
-            jax.ShapeDtypeStruct((3 * HALO, track, stack), jnp.float32),
-        ),
-        in_specs=[ANY] * 4,
-        out_specs=(VMEM,) * 4,
+        kernel,
+        out_shape=(out, out),
+        in_specs=[HBM] * 4,
+        out_specs=(VMEM,) * 2,
         scratch_shapes=[
-            [pltpu.VMEM((2, HALO, lateral, stack), dtype) for dtype in types],
-            [pltpu.VMEM((2, track, EDGE, stack), dtype) for dtype in types],
-            pltpu.SemaphoreType.DMA((2, 4, 2)),
+            [pltpu.VMEM((2,) + held, field.dtype) for field in fields],
+            pltpu.SemaphoreType.DMA((4, 2)),
         ],
-        compiler_params=pltpu.CompilerParams(vmem_limit_bytes=VMEM_ALL),
-    )(h, k, bead, birth)
+        compiler_params=pltpu.CompilerParams(vmem_limit_bytes=LIMIT),
+    )(*fields)
+
+
+def corner_kernel(low_in, high_in, ylo_ref, yhi_ref, low_out, high_out, held, sem):
+    del low_in, high_in
+    track = ylo_ref.shape[1]
+    copies = []
+    for side, out in ((0, low_out), (1, high_out)):
+        for f in range(3):
+            for d in range(HALO):
+                at = pl.ds(side * (track - HALO) + d, 1)
+                for y, ref in enumerate((ylo_ref, yhi_ref)):
+                    for e in range(HALO):
+                        held[side, f * HALO + d, pl.ds(y * HALO + e, 1), :] = ref[f * HALO + e, at, :]
+        rows = pl.ds(out.shape[1] - EDGE, EDGE)
+        copies.append(pltpu.make_async_copy(held.at[side], out.at[:, rows], sem.at[side]))
+        copies[-1].start()
+    for copy in copies:
+        copy.wait()
+
+
+def corners(low, high, ylo, yhi):
+    return pl.pallas_call(
+        corner_kernel,
+        out_shape=(jax.ShapeDtypeStruct(low.shape, low.dtype),) * 2,
+        in_specs=[HBM] * 2 + [VMEM] * 2,
+        out_specs=(HBM,) * 2,
+        input_output_aliases={0: 0, 1: 1},
+        scratch_shapes=[
+            pltpu.VMEM((2, 3 * HALO, EDGE, LANES), jnp.float32),
+            pltpu.SemaphoreType.DMA((2,)),
+        ],
+        compiler_params=pltpu.CompilerParams(vmem_limit_bytes=LIMIT),
+    )(low, high, ylo, yhi)
 
 
 def inner_kernel(
@@ -255,7 +316,7 @@
                 flat[2][at, :] = h
                 flat[3][at, :] = jnp.where(inside, birth, 1e6).astype(jnp.int32)
 
-    for n in range(CHUNKS):
+    def arrive(n):
         for copy in copies(n):
             copy.wait()
         slab.prepare_all(n * piece, (n + 1) * piece)
@@ -269,9 +330,10 @@
     def finish(x, j, value):
         raw[0][x, slab.natural(j), :] = value - OFFSET
 
-    slab.run_step(0, slab.ha, slab.into(slab.hb), 0, (1, track - 1))
+    arrivals = [1] + [n * piece - 1 for n in range(1, CHUNKS + 1)]
+    slab.run_step(0, slab.ha, slab.into(slab.hb), 0, arrivals, before=arrive)
     slab.run_step(1, slab.hb, slab.into(slab.ha), 0, (2, track - 2))
-    slab.run_step(2, slab.ha, finish, 0, cuts, lambda n: out_copy(n).start())
+    slab.run_step(2, slab.ha, finish, 0, cuts, after=lambda n: out_copy(n).start())
     for n in range(OUTS):
         out_copy(n).wait()
 
@@ -281,13 +343,13 @@
     return pl.pallas_call(
         inner_kernel,
         out_shape=jax.ShapeDtypeStruct(h.shape, jnp.float32),
-        in_specs=[ANY] * 4 + [VMEM] * 2,
-        out_specs=ANY,
+        in_specs=[HBM] * 4 + [VMEM] * 2,
+        out_specs=HBM,
         scratch_shapes=slab_scratch(track, lateral, stack) + [
             pltpu.SemaphoreType.DMA((4, CHUNKS)),
             pltpu.SemaphoreType.DMA((OUTS,)),
         ],
-        compiler_params=pltpu.CompilerParams(vmem_limit_bytes=58 * MIB),
+        compiler_params=pltpu.CompilerParams(vmem_limit_bytes=LIMIT),
         cost_estimate=pl.CostEstimate(
             flops=200 * h.size, bytes_accessed=20 * h.size, transcendentals=15 * h.size
         ),
@@ -375,8 +437,8 @@
             jax.ShapeDtypeStruct(h.shape, jnp.float32),
             jax.ShapeDtypeStruct((owners * slots, stack), jnp.float32),
         ),
-        in_specs=[SMEM] + [ANY] * 5 + [VMEM] * 4,
-        out_specs=(ANY, VMEM),
+        in_specs=[SMEM] + [HBM] * 5 + [VMEM] * 4,
+        out_specs=(HBM, VMEM),
         input_output_aliases={5: 0},
         scratch_shapes=slab_scratch(2 * RIM, lateral, stack) + [
             pltpu.VMEM((track, lateral + 2 * EDGE, stack), jnp.float32),
@@ -384,7 +446,7 @@
             pltpu.SemaphoreType.DMA,
             pltpu.SemaphoreType.DMA((2,)),
         ],
-        compiler_params=pltpu.CompilerParams(vmem_limit_bytes=VMEM_ALL),
+        compiler_params=pltpu.CompilerParams(vmem_limit_bytes=LIMIT),
         cost_estimate=pl.CostEstimate(
             flops=50 * h.size, bytes_accessed=6 * h.size, transcendentals=4 * h.size
         ),
@@ -397,20 +459,17 @@
 
 
 def per_device(enthalpy, conductivity, bead_enthalpy, birth_time, send_rows, send_counts):
-    lateral = enthalpy.shape[1]
     fields = (enthalpy, conductivity, bead_enthalpy, birth_time)
 
-    to_low, to_high, to_left, to_right = strips(*fields)
+    track, lateral, stack = enthalpy.shape
+    to_left, to_right = strips(lateral_kernel, fields, track, (track, EDGE, stack))
+    to_low, to_high = strips(track_kernel, fields, lateral + EDGE, (HALO, lateral, stack))
     ylo = lax.ppermute(to_right, "gy", shift("gy", 1))
     yhi = lax.ppermute(to_left, "gy", shift("gy", -1))
 
-    def with_corners(strip, cut):
-        corners = [y[:, cut].reshape(3, HALO, HALO, -1).swapaxes(1, 2) for y in (ylo, yhi)]
-        corners = jnp.concatenate(corners, 2).reshape(3 * HALO, 2 * HALO, -1)
-        return lax.dynamic_update_slice(strip, corners, (0, lateral, 0))
-
-    xlo = lax.ppermute(with_corners(to_high, slice(-HALO, None)), "gx", shift("gx", 1))
-    xhi = lax.ppermute(with_corners(to_low, slice(0, HALO)), "gx", shift("gx", -1))
+    to_low, to_high = corners(to_low, to_high, ylo, yhi)
+    xlo = lax.ppermute(to_high, "gx", shift("gx", 1))
+    xhi = lax.ppermute(to_low, "gx", shift("gx", -1))
 
     rows, counts = send_rows[0, 0], send_counts[0, 0]
     slot = jnp.arange(rows.shape[1], dtype=jnp.int32)

time: 111 us -> 108 us (0.973)
  waiting for transfers between devices: 6.32 us -> 3.63 us
  local copies, waits for them, and re-layouts: 5.96 us -> 3.77 us
  Pallas kernels: 45 us -> 46.7 us
    pallas_call x1 -> x3, Pallas kernels: 3.57 us -> 6.89 us  [the longest x2 5.17 us: strips(): pl.pallas_call(kernel, out_shape=(out, out), in_specs=[HBM] * 4, out_spec...]
    dynamic_update_slice x2 -> x0, local copies, waits for them, and re-layouts: 2.86 us -> none  [with_corners(): return lax.dynamic_update_slice(strip, corners, (0, lateral, 0))]
    ppermute x1, waiting for transfers between devices: 2.03 us -> 0.01 us  [per_device(): ylo = lax.ppermute(to_right, 'gy', shift('gy', 1))]
    pallas_call x1, Pallas kernels: 26.9 us -> 25.5 us  [inner_planes(): pl.pallas_call(inner_kernel, out_shape=jax.ShapeDtypeStruct(h.shape, jnp....]
  transfers between devices with their start and end apart: 4 -> 4, of which waited for: 2 -> 1; matrix products, arithmetic and copies ran while one was open for 2% -> 1% of each run, Pallas kernels for 24% -> 26%
where the time goes in v5:
time: 108 us
  Pallas kernels  46.7 us (43%)
  blocking collectives  41.1 us (38%)
  starting transfers between devices  11 us (10%)
  local copies, waits for them, and re-layouts  3.77 us (3%)
  waiting for transfers between devices  3.63 us (3%)
    all_to_all x1, blocking collectives, per_device(): lax.all_to_all(outgoing, ('gx', 'gy'), split_axis=0, concat_axis=0, tiled...  41.1 us
    pallas_call x1, Pallas kernels, inner_planes(): pl.pallas_call(inner_kernel, out_shape=jax.ShapeDtypeStruct(h.shape, jnp....  25.5 us
    pallas_call x1, Pallas kernels, rim_and_rows(): pl.pallas_call(rim_kernel, out_shape=(jax.ShapeDtypeStruct(h.shape, jnp.f...  14.3 us
    pallas_call x2, Pallas kernels, strips(): pl.pallas_call(kernel, out_shape=(out, out), in_specs=[HBM] * 4, out_spec...  5.17 us
    ppermute x1, starting transfers between devices, per_device(): ylo = lax.ppermute(to_right, 'gy', shift('gy', 1))  4.51 us
    unnamed x14, local copies, waits for them, and re-layouts  3.77 us
    ppermute x1, waiting for transfers between devices, per_device(): yhi = lax.ppermute(to_left, 'gy', shift('gy', -1))  3.62 us
    ppermute x1, starting transfers between devices, per_device(): xlo = lax.ppermute(to_high, 'gx', shift('gx', 1))  3.24 us
  transfers between devices with their start and end apart: 4, of which 1 were waited for; matrix products, arithmetic and copies ran while one was open for 1% of the time, Pallas kernels for 26%

profile of v5, /device:TPU:1, one launch (start us, length us, event | category | flops | bytes accessed | tf_op | source)
XLA Modules:
  0.0 107.6 jit_solution(15286993939420899807)
XLA Ops:
  0.6 2.5 %shard_map.77 = (f32[9,64,128]{2,1,0:T(8,128)}, f32[9,64,128]{2,1,0:T(8,128)}) custom-call(f32[64,128,128]{2,1,0:T(8,128)} %h_hbm.7, f32[64,128,128]{2,1,0:T(8,128)} %k_hbm.7, f32[64,128,128]{2,1,0:T(8,128)} %bead_hbm.7, s32[64,128,128]{2,1,0:T(8,128)} %birth_hbm.7), custom_call_target="tpu_custom_call" | custom-call | tf_op jit(solution)/shard_map/pallas_call | solution.py:240
  3.1 4.5 %collective-permute-start = (f32[9,64,128]{2,1,0:T(8,128)}, f32[9,64,128]{2,1,0:T(8,128)S(1)}, u32[]{:S(2)}, u32[]{:S(2)}) collective-permute-start(f32[9,64,128]{2,1,0:T(8,128)} %get-tuple-element.10), channel_id=1, source_target_pairs={{0,1},{1,2},{2,3},{3,4},{4,5},{5,6},{6,7},{8,9},{9,10},{10,11},{11... | collective-permute-start | bytes 884744 | tf_op jit(solution)/shard_map/ppermute | solution.py:467
  7.6 0.0 copy-start.4
  7.7 0.0 copy-start.5
  7.7 1.9 %collective-permute-start.1 = (f32[9,64,128]{2,1,0:T(8,128)}, f32[9,64,128]{2,1,0:T(8,128)S(1)}, u32[]{:S(2)}, u32[]{:S(2)}) collective-permute-start(f32[9,64,128]{2,1,0:T(8,128)} %get-tuple-element.11), channel_id=1, source_target_pairs={{1,0},{2,1},{3,2},{4,3},{5,4},{6,5},{7,6},{9,8},{10,9},{11,10},{12... | collective-permute-start | bytes 884744 | tf_op jit(solution)/shard_map/ppermute | solution.py:468
  9.6 2.7 %shard_map.79 = (f32[9,136,128]{2,1,0:T(8,128)}, f32[9,136,128]{2,1,0:T(8,128)}) custom-call(f32[64,128,128]{2,1,0:T(8,128)} %h_hbm.7, f32[64,128,128]{2,1,0:T(8,128)} %k_hbm.7, f32[64,128,128]{2,1,0:T(8,128)} %bead_hbm.7, s32[64,128,128]{2,1,0:T(8,128)} %birth_hbm.7), custom_call_target="tpu_custom_call" | custom-call | tf_op jit(solution)/shard_map/pallas_call | solution.py:240
  12.3 0.0 collective-permute-done.ylo_ref
  12.3 0.0 copy-start
  12.3 3.6 %collective-permute-done.1.yhi_ref = f32[9,64,128]{2,1,0:T(8,128)S(1)} collective-permute-done((f32[9,64,128]{2,1,0:T(8,128)}, f32[9,64,128]{2,1,0:T(8,128)S(1)}, u32[]{:S(2)}, u32[]{:S(2)}) %collective-permute-start.1) | collective-permute-done | bytes 294944 | tf_op jit(solution)/shard_map/ppermute | solution.py:468
  15.9 0.0 copy-start.1
  15.9 0.0 copy-done
  15.9 0.7 copy-done.1
  16.6 1.7 %shard_map.80 = (f32[9,136,128]{2,1,0:T(8,128)}, f32[9,136,128]{2,1,0:T(8,128)}) custom-call(f32[9,136,128]{2,1,0:T(8,128)} %get-tuple-element.12.low_in, f32[9,136,128]{2,1,0:T(8,128)} %get-tuple-element.13.high_in, f32[9,64,128]{2,1,0:T(8,128)} %copy-done, f32[9,64,128]{2,1,0:T(8,128)} %copy-done.1), custom_call_target="tpu_custom_call", output_to_operand_aliasing={{0}: (0, {}), {1}: (1, {})} | custom-call | tf_op jit(solution)/shard_map/pallas_call | solution.py:272
  18.4 3.2 %collective-permute-start.2 = (f32[9,136,128]{2,1,0:T(8,128)}, f32[9,136,128]{2,1,0:T(8,128)S(1)}, u32[]{:S(2)}, u32[]{:S(2)}) collective-permute-start(f32[9,136,128]{2,1,0:T(8,128)} %get-tuple-element.14), channel_id=1, source_target_pairs={{0,8},{8,16},{16,24},{24,32},{32,40},{40,48},{48,56},{56,64},{64,7... | collective-permute-start | bytes 1880072 | tf_op jit(solution)/shard_map/ppermute | solution.py:471
  21.6 1.3 %collective-permute-start.3 = (f32[9,136,128]{2,1,0:T(8,128)}, f32[9,136,128]{2,1,0:T(8,128)S(1)}, u32[]{:S(2)}, u32[]{:S(2)}) collective-permute-start(f32[9,136,128]{2,1,0:T(8,128)} %get-tuple-element.15), channel_id=1, source_target_pairs={{8,0},{16,8},{24,16},{32,24},{40,32},{48,40},{56,48},{64,56},{72,6... | collective-permute-start | bytes 1880072 | tf_op jit(solution)/shard_map/ppermute | solution.py:472
  22.9 0.0 copy-done.4
  22.9 0.1 copy.11
  23.0 0.0 copy-done.5
  23.0 0.7 fusion.3.index_ref
  23.7 25.5 %shard_map.78.part_hbm = f32[64,128,128]{2,1,0:T(8,128)} custom-call(f32[64,128,128]{2,1,0:T(8,128)} %h_hbm.7, f32[64,128,128]{2,1,0:T(8,128)} %k_hbm.7, f32[64,128,128]{2,1,0:T(8,128)} %bead_hbm.7, s32[64,128,128]{2,1,0:T(8,128)} %birth_hbm.7, f32[9,64,128]{2,1,0:T(8,128)} %copy-done, f32[9,64,128]{2,1,0:T(8,128)} %copy-done.1), custom_call_target="tpu_custom_call" | custom-call | flops 209715200 | bytes 20971520 | tf_op jit(solution)/shard_map/pallas_call | solution.py:343
  49.2 0.0 collective-permute-done.2.xlo_ref
  49.3 0.0 copy-start.2
  49.3 0.0 collective-permute-done.3.xhi_ref
  49.3 0.8 copy-done.2
  50.1 0.0 copy-start.3
  50.1 0.8 copy-done.3
  50.9 14.3 %shard_map.81 = (f32[64,128,128]{2,1,0:T(8,128)}, f32[4096,128]{1,0:T(8,128)}) custom-call(s32[128,32]{1,0:T(8,128)} %fusion.3.index_ref, f32[64,128,128]{2,1,0:T(8,128)} %h_hbm.7, f32[64,128,128]{2,1,0:T(8,128)} %k_hbm.7, f32[64,128,128]{2,1,0:T(8,128)} %bead_hbm.7, s32[64,128,128]{2,1,0:T(8,128)} %birth_hbm.7, ...), custom_call_target="tpu_custom_call", output_to_operand_aliasing={{0}: (5, {})} | custom-call | flops 52428800 | bytes 6291456 | tf_op jit(solution)/shard_map/pallas_call | solution.py:434
  65.2 41.1 %all_to_all.5 = f32[128,32,128]{2,1,0:T(8,128)S(1)} all-to-all(f32[128,32,128]{2,1,0:T(8,128)} %bitcast.24), channel_id=1, replica_groups=mesh['gx'=16,'gy'=8] {'gx','gy'}, dimensions={0} | all-to-all | bytes 4194304 | tf_op jit(solution)/shard_map/all_to_all | solution.py:482
  106.3 1.3 %copy.16 = f32[4096,128]{1,0:T(8,128)} copy(f32[4096,128]{1,0:T(8,128)S(1)} %bitcast.23) | data formatting | bytes 4194304
Async XLA Ops:
  3.1 9.2 %collective-permute-start = (f32[9,64,128]{2,1,0:T(8,128)}, f32[9,64,128]{2,1,0:T(8,128)S(1)}, u32[]{:S(2)}, u32[]{:S(2)}) collective-permute-start(f32[9,64,128]{2,1,0:T(8,128)} %get-tuple-element.10), channel_id=1, source_target_pairs={{0,1},{1,2},{2,3},{3,4},{4,5},{5,6},{6,7},{8,9},{9,10},{10,11},{11... | collective-permute-start | bytes 884744 | tf_op jit(solution)/shard_map/ppermute | solution.py:467
  7.6 15.3 %copy-start.4 = (s32[1,1,128,32]{2,3,1,0:T(8,128)S(1)}, s32[1,1,128,32]{2,3,1,0:T(8,128)}, u32[]{:S(2)}) copy-start(s32[1,1,128,32]{2,3,1,0:T(8,128)} %param.10) | copy-start | bytes 49156
  7.7 15.4 %copy-start.5 = (s32[1,1,128]{2,1,0:T(1,128)S(1)}, s32[1,1,128]{2,1,0:T(1,128)}, u32[]{:S(2)}) copy-start(s32[1,1,128]{2,1,0:T(1,128)} %param.11) | copy-start | bytes 1540
  7.7 8.3 %collective-permute-start.1 = (f32[9,64,128]{2,1,0:T(8,128)}, f32[9,64,128]{2,1,0:T(8,128)S(1)}, u32[]{:S(2)}, u32[]{:S(2)}) collective-permute-start(f32[9,64,128]{2,1,0:T(8,128)} %get-tuple-element.11), channel_id=1, source_target_pairs={{1,0},{2,1},{3,2},{4,3},{5,4},{6,5},{7,6},{9,8},{10,9},{11,10},{12... | collective-permute-start | bytes 884744 | tf_op jit(solution)/shard_map/ppermute | solution.py:468
  12.3 3.6 %copy-start = (f32[9,64,128]{2,1,0:T(8,128)}, f32[9,64,128]{2,1,0:T(8,128)S(1)}, u32[]{:S(2)}) copy-start(f32[9,64,128]{2,1,0:T(8,128)S(1)} %collective-permute-done.ylo_ref) | copy-start | bytes 884740
  15.9 0.7 copy-start.1
  18.4 30.9 %collective-permute-start.2 = (f32[9,136,128]{2,1,0:T(8,128)}, f32[9,136,128]{2,1,0:T(8,128)S(1)}, u32[]{:S(2)}, u32[]{:S(2)}) collective-permute-start(f32[9,136,128]{2,1,0:T(8,128)} %get-tuple-element.14), channel_id=1, source_target_pairs={{0,8},{8,16},{16,24},{24,32},{32,40},{40,48},{48,56},{56,64},{64,7... | collective-permute-start | bytes 1880072 | tf_op jit(solution)/shard_map/ppermute | solution.py:471
  21.6 27.7 %collective-permute-start.3 = (f32[9,136,128]{2,1,0:T(8,128)}, f32[9,136,128]{2,1,0:T(8,128)S(1)}, u32[]{:S(2)}, u32[]{:S(2)}) collective-permute-start(f32[9,136,128]{2,1,0:T(8,128)} %get-tuple-element.15), channel_id=1, source_target_pairs={{8,0},{16,8},{24,16},{32,24},{40,32},{48,40},{56,48},{64,56},{72,6... | collective-permute-start | bytes 1880072 | tf_op jit(solution)/shard_map/ppermute | solution.py:472
  49.3 0.8 copy-start.2
  50.1 0.8 copy-start.3

commit v6 on v5

--- a/solution.py
+++ b/solution.py
@@ -27,7 +27,10 @@
 ROLL_DOWN = 2
 PUN = 2
 RIM = 3 * HALO
-LIMIT = 60 * 1024 * 1024
+HANDED = ((0, 2), (1, 2), (2, 2), (0, 4), (0, 4), (0, 4), (0, 4))
+MIB = 1024 * 1024
+RIM_LIMIT = 24 * MIB
+LIMIT = 60 * MIB
 
 HBM = pl.BlockSpec(memory_space=pl.ANY)
 VMEM = pl.BlockSpec(memory_space=pltpu.VMEM)
@@ -72,24 +75,24 @@
         for ref, value in zip(self.raw, values):
             ref[x, rows, :] = value
 
-    def prepare(self, x):
+    def prepare(self, x, to_x):
         h_v, k_v, bead_v, birth_v = self.raw
         top = lax.broadcasted_iota(jnp.int32, (TILE, LANES), 1) == LANES - 1
         for j in range(self.span):
             at, to = self.natural(j), tile(j)
             birth, k = birth_v[x, at, :], k_v[x, at, :]
             b = birth.astype(jnp.float32) * TICK_SHARE
-            self.ha[x, to, :] = standing(h_v[x, at, :], bead_v[x, at, :], birth) + OFFSET
-            self.ks[x, to, :] = k
-            self.kz[x, to, :] = jnp.where(top, FAR, pltpu.roll(k, LANES - 1, 1))
-            self.bs[x, to, :] = b
-            self.bz[x, to, :] = pltpu.roll(b, LANES - 1, 1)
+            self.ha[to_x, to, :] = standing(h_v[x, at, :], bead_v[x, at, :], birth) + OFFSET
+            self.ks[to_x, to, :] = k
+            self.kz[to_x, to, :] = jnp.where(top, FAR, pltpu.roll(k, LANES - 1, 1))
+            self.bs[to_x, to, :] = b
+            self.bz[to_x, to, :] = pltpu.roll(b, LANES - 1, 1)
 
     def prepare_all(self, lo, hi):
         @pl.loop(0, (hi - lo) // PUN)
         def _(i):
             for u in range(PUN):
-                self.prepare(lo + i * PUN + u)
+                self.prepare(lo + i * PUN + u, lo + i * PUN + u)
 
     def into(self, ref):
         def store(x, j, value):
@@ -168,6 +171,9 @@
 
         both = [(ring_a, ring_b), (ring_b, ring_a)]
         for n, (lo, hi) in enumerate(zip(cuts[:-1], cuts[1:])):
+            if hi - lo == HALO:
+                planes([base + x for x in range(lo, hi)], (both * HALO)[:HALO])
+                continue
             unroll = UNROLL if (hi - lo) % UNROLL == 0 else 2
             if n and before is not None:
                 before(n)
@@ -176,15 +182,13 @@
             def _(i):
                 planes([base + lo + unroll * i + u for u in range(unroll)], both * (unroll // 2))
 
-            if (hi - lo) % 2:
-                planes([base + hi - 1], both[:1])
             if after is not None:
                 after(n)
 
 
-def slab_scratch(planes, lateral, stack):
+def slab_scratch(raw_planes, planes, lateral, stack):
     tiles = (lateral + 2 * LEAD, stack)
-    raw = (planes, lateral + 2 * EDGE, stack)
+    raw = (raw_planes, lateral + 2 * EDGE, stack)
     return [
         [pltpu.VMEM(raw, dtype) for dtype in (jnp.float32, jnp.float32, jnp.float32, jnp.int32)],
         [pltpu.VMEM((planes,) + tiles, jnp.float32)] * 6,
@@ -279,13 +283,14 @@
             pltpu.VMEM((2, 3 * HALO, EDGE, LANES), jnp.float32),
             pltpu.SemaphoreType.DMA((2,)),
         ],
-        compiler_params=pltpu.CompilerParams(vmem_limit_bytes=LIMIT),
+        compiler_params=pltpu.CompilerParams(vmem_limit_bytes=8 * MIB),
     )(low, high, ylo, yhi)
 
 
 def inner_kernel(
-    h_hbm, k_hbm, bead_hbm, birth_hbm, ylo_ref, yhi_ref, out_hbm, raw, grids, rings, acc, sem_in, sem_out
+    h_hbm, k_hbm, bead_hbm, birth_hbm, ylo_ref, yhi_ref, out_hbm, *rest
 ):
+    handed, (raw, grids, rings, acc, sem_in, sem_out, sem_hand) = rest[:7], rest[7:]
     track, lateral, _ = h_hbm.shape
     slab = Slab(raw, grids, rings, acc)
     inner = pl.ds(EDGE, lateral)
@@ -331,46 +336,67 @@
         raw[0][x, slab.natural(j), :] = value - OFFSET
 
     arrivals = [1] + [n * piece - 1 for n in range(1, CHUNKS + 1)]
+    def hand(i):
+        ref, (first, count) = (slab.ha, slab.hb, slab.ha, *grids[2:])[i], HANDED[i]
+        return [
+            pltpu.make_async_copy(
+                ref.at[pl.ds((first, track - first - count)[side], count)], handed[i].at[side], sem_hand.at[i, side]
+            )
+            for side in range(2)
+        ]
+
     slab.run_step(0, slab.ha, slab.into(slab.hb), 0, arrivals, before=arrive)
+    for i in (0, 1, 3, 4, 5, 6):
+        for copy in hand(i):
+            copy.start()
     slab.run_step(1, slab.hb, slab.into(slab.ha), 0, (2, track - 2))
+    for copy in hand(2):
+        copy.start()
     slab.run_step(2, slab.ha, finish, 0, cuts, after=lambda n: out_copy(n).start())
     for n in range(OUTS):
         out_copy(n).wait()
+    for i in range(len(HANDED)):
+        for copy in hand(i):
+            copy.wait()
 
 
 def inner_planes(h, k, bead, birth, ylo, yhi):
     track, lateral, stack = h.shape
     return pl.pallas_call(
         inner_kernel,
-        out_shape=jax.ShapeDtypeStruct(h.shape, jnp.float32),
+        out_shape=(
+            jax.ShapeDtypeStruct(h.shape, jnp.float32),
+            *[jax.ShapeDtypeStruct((2, n, lateral + 2 * LEAD, stack), jnp.float32) for _, n in HANDED],
+        ),
         in_specs=[HBM] * 4 + [VMEM] * 2,
-        out_specs=HBM,
-        scratch_shapes=slab_scratch(track, lateral, stack) + [
+        out_specs=(HBM,) * (1 + len(HANDED)),
+        scratch_shapes=slab_scratch(track, track, lateral, stack) + [
             pltpu.SemaphoreType.DMA((4, CHUNKS)),
             pltpu.SemaphoreType.DMA((OUTS,)),
+            pltpu.SemaphoreType.DMA((len(HANDED), 2)),
         ],
-        compiler_params=pltpu.CompilerParams(vmem_limit_bytes=LIMIT),
+        compiler_params=pltpu.CompilerParams(vmem_limit_bytes=50 * MIB),
         cost_estimate=pl.CostEstimate(
             flops=200 * h.size, bytes_accessed=20 * h.size, transcendentals=15 * h.size
         ),
     )(h, k, bead, birth, ylo, yhi)
 
 
-def rim_kernel(
-    index_ref, h_hbm, k_hbm, bead_hbm, birth_hbm, part_hbm, xlo_ref, xhi_ref, ylo_ref, yhi_ref,
-    out_hbm, rows_ref, raw, grids, rings, acc, whole, sem_in, sem_part, sem_out,
-):
-    track, lateral, _ = h_hbm.shape
+def rim_kernel(index_ref, part_hbm, xlo_ref, xhi_ref, *rest):
+    handed, (out_hbm, rows_ref, raw, grids, rings, acc, whole, sem_in, sem_part, sem_out) = rest[:7], rest[7:]
+    track, lateral, _ = part_hbm.shape
     slab = Slab(raw, grids, rings, acc)
     inner = pl.ds(EDGE, lateral)
     own = RIM - HALO
 
     copies = []
-    for i, (hbm, vmem) in enumerate(zip((h_hbm, k_hbm, bead_hbm, birth_hbm), raw)):
+    for i, (first, count) in enumerate(HANDED):
+        ref = (slab.ha, slab.hb, slab.ha, *grids[2:])[i]
         for side in range(2):
-            src = pl.ds(side * (track - own), own)
-            dst = pl.ds(HALO + side * own, own)
-            copies.append(pltpu.make_async_copy(hbm.at[src], vmem.at[dst, inner], sem_in.at[i, side]))
+            dst = (HALO + first, RIM + own - first - count)[side]
+            copies.append(
+                pltpu.make_async_copy(handed[i].at[side], ref.at[pl.ds(dst, count)], sem_in.at[i, side])
+            )
     for copy in copies:
         copy.start()
     middle = pl.ds(HALO, track - 2 * HALO)
@@ -379,22 +405,14 @@
 
     below, above = pl.ds(EDGE - HALO, HALO), pl.ds(EDGE + lateral, HALO)
     for side, ref in ((0, xlo_ref), (1, xhi_ref)):
-        @pl.loop(0, HALO)
-        def _(d, side=side, ref=ref):
+        for d in range(HALO):
             for first, n, rows in ((0, lateral, inner), (lateral, HALO, below), (lateral + HALO, HALO, above)):
-                slab.place(
-                    *[ref[f * HALO + d, pl.ds(first, n), :] for f in range(3)], side * (RIM + own) + d, rows
-                )
-    for x in range(HALO, HALO + 2 * own):
-        at = pl.ds(x - HALO + (track - 2 * own if x >= RIM else 0), 1)
-        for y, ref in enumerate((ylo_ref, yhi_ref)):
-            for d in range(HALO):
-                row = pl.ds((EDGE - HALO, EDGE + lateral)[y] + d, 1)
-                slab.place(*[ref[f * HALO + d, at, :] for f in range(3)], x, row)
-
+                slab.place(*[ref[f * HALO + d, pl.ds(first, n), :] for f in range(3)], side * HALO + d, rows)
+    for side in range(2):
+        for d in range(HALO):
+            slab.prepare(side * HALO + d, side * (RIM + own) + d)
     for copy in copies:
         copy.wait()
-    slab.prepare_all(0, 2 * RIM)
 
     def finish(x, j, value):
         at = x - HALO + jnp.where(x >= RIM, track - 2 * own, 0)
@@ -402,10 +420,11 @@
 
     @pl.loop(0, 2)
     def _(side):
-        base = side * RIM
-        slab.run_step(0, slab.ha, slab.into(slab.hb), base, (1, RIM - 1))
-        slab.run_step(1, slab.hb, slab.into(slab.ha), base, (2, RIM - 2))
-        slab.run_step(2, slab.ha, finish, base, (3, RIM - 3))
+        stores = (slab.into(slab.hb), slab.into(slab.ha), finish)
+        for step, (src, store) in enumerate(zip((slab.ha, slab.hb, slab.ha), stores)):
+            first = 1 + step
+            last = 2 * RIM - first - HALO
+            slab.run_step(step, src, store, side * (last - first), (first, first + HALO))
 
     outs = []
     for side in range(2):
@@ -428,29 +447,29 @@
         copy.wait()
 
 
-def rim_and_rows(index, h, k, bead, birth, part, halos):
-    track, lateral, stack = h.shape
+def rim_and_rows(index, part, xlo, xhi, handed):
+    track, lateral, stack = part.shape
     owners, slots = index.shape
     return pl.pallas_call(
         rim_kernel,
         out_shape=(
-            jax.ShapeDtypeStruct(h.shape, jnp.float32),
+            jax.ShapeDtypeStruct(part.shape, jnp.float32),
             jax.ShapeDtypeStruct((owners * slots, stack), jnp.float32),
         ),
-        in_specs=[SMEM] + [HBM] * 5 + [VMEM] * 4,
+        in_specs=[SMEM, HBM] + [VMEM] * 2 + [HBM] * len(HANDED),
         out_specs=(HBM, VMEM),
-        input_output_aliases={5: 0},
-        scratch_shapes=slab_scratch(2 * RIM, lateral, stack) + [
+        input_output_aliases={1: 0},
+        scratch_shapes=slab_scratch(2 * HALO, 2 * RIM, lateral, stack) + [
             pltpu.VMEM((track, lateral + 2 * EDGE, stack), jnp.float32),
-            pltpu.SemaphoreType.DMA((4, 2)),
+            pltpu.SemaphoreType.DMA((len(HANDED), 2)),
             pltpu.SemaphoreType.DMA,
             pltpu.SemaphoreType.DMA((2,)),
         ],
-        compiler_params=pltpu.CompilerParams(vmem_limit_bytes=LIMIT),
+        compiler_params=pltpu.CompilerParams(vmem_limit_bytes=RIM_LIMIT),
         cost_estimate=pl.CostEstimate(
-            flops=50 * h.size, bytes_accessed=6 * h.size, transcendentals=4 * h.size
+            flops=30 * part.size, bytes_accessed=3 * part.size, transcendentals=3 * part.size
         ),
-    )(index, h, k, bead, birth, part, *halos)
+    )(index, part, xlo, xhi, *handed)
 
 
 def shift(axis, by):
@@ -476,8 +495,8 @@
     place = rows // lateral * (lateral + 2 * EDGE) + rows % lateral + EDGE
     index = jnp.where(slot[None, :] < counts[:, None], place, 0)
 
-    part = inner_planes(*fields, ylo, yhi)
-    end, outgoing = rim_and_rows(index, *fields, part, (xlo, xhi, ylo, yhi))
+    part, *handed = inner_planes(*fields, ylo, yhi)
+    end, outgoing = rim_and_rows(index, part, xlo, xhi, handed)
     outgoing = outgoing.reshape(rows.shape + outgoing.shape[1:])
     received = lax.all_to_all(outgoing, ("gx", "gy"), split_axis=0, concat_axis=0, tiled=True)
     return end, received.reshape(-1, received.shape[-1])

time: 108 us -> 100 us (0.926)
  Pallas kernels: 46.7 us -> 41.9 us
  local copies, waits for them, and re-layouts: 3.77 us -> 1.43 us
    pallas_call x2, Pallas kernels: 39.8 us -> 36.1 us  [the longest x1 26 us: inner_planes(): pl.pallas_call(inner_kernel, out_shape=(jax.ShapeDtypeStruct(h.shape, jnp...]
    unnamed x14 -> x6, local copies, waits for them, and re-layouts: 3.77 us -> 1.43 us
  transfers between devices with their start and end apart: 4 -> 4, of which waited for: 1 -> 1; matrix products, arithmetic and copies ran while one was open for 1% -> 0% of each run, Pallas kernels for 26% -> 29%
where the time goes in v6:
time: 100 us; the launch traced here: 99.7 us
  Pallas kernels  41.9 us (42%)
  blocking collectives  40.9 us (41%)
  starting transfers between devices  11 us (11%)
  waiting for transfers between devices  3.64 us (4%)
  local copies, waits for them, and re-layouts  1.43 us (1%)
    all_to_all x1, blocking collectives, per_device(): lax.all_to_all(outgoing, ('gx', 'gy'), split_axis=0, concat_axis=0, tiled...  40.9 us
    pallas_call x1, Pallas kernels, inner_planes(): pl.pallas_call(inner_kernel, out_shape=(jax.ShapeDtypeStruct(h.shape, jnp...  26 us
    pallas_call x1, Pallas kernels, rim_and_rows(): pl.pallas_call(rim_kernel, out_shape=(jax.ShapeDtypeStruct(part.shape, jn...  10.1 us
    pallas_call x2, Pallas kernels, strips(): pl.pallas_call(kernel, out_shape=(out, out), in_specs=[HBM] * 4, out_spec...  5.16 us
    ppermute x1, starting transfers between devices, per_device(): ylo = lax.ppermute(to_right, 'gy', shift('gy', 1))  4.51 us
    ppermute x1, waiting for transfers between devices, per_device(): yhi = lax.ppermute(to_left, 'gy', shift('gy', -1))  3.63 us
    ppermute x1, starting transfers between devices, per_device(): xlo = lax.ppermute(to_high, 'gx', shift('gx', 1))  3.24 us
  transfers between devices with their start and end apart: 4, of which 1 were waited for; matrix products, arithmetic and copies ran while one was open for 0% of the time, Pallas kernels for 29%

profile of v6, /device:TPU:1, one launch (start us, length us, event | category | flops | bytes accessed | tf_op | source)
XLA Modules:
  0.0 99.7 jit_solution(18153476933643069964)
XLA Ops:
  0.6 2.5 %shard_map.77 = (f32[9,64,128]{2,1,0:T(8,128)}, f32[9,64,128]{2,1,0:T(8,128)}) custom-call(f32[64,128,128]{2,1,0:T(8,128)} %h_hbm.5, f32[64,128,128]{2,1,0:T(8,128)} %k_hbm.5, f32[64,128,128]{2,1,0:T(8,128)} %bead_hbm.5, s32[64,128,128]{2,1,0:T(8,128)} %birth_hbm.5), custom_call_target="tpu_custom_call" | custom-call | tf_op jit(solution)/shard_map/pallas_call | solution.py:244
  3.1 4.5 %collective-permute-start = (f32[9,64,128]{2,1,0:T(8,128)}, f32[9,64,128]{2,1,0:T(8,128)S(1)}, u32[]{:S(2)}, u32[]{:S(2)}) collective-permute-start(f32[9,64,128]{2,1,0:T(8,128)} %get-tuple-element.18), channel_id=1, source_target_pairs={{0,1},{1,2},{2,3},{3,4},{4,5},{5,6},{6,7},{8,9},{9,10},{10,11},{11... | collective-permute-start | bytes 884744 | tf_op jit(solution)/shard_map/ppermute | solution.py:486
  7.6 0.0 copy-start
  7.6 0.0 copy-start.1
  7.7 1.9 %collective-permute-start.1 = (f32[9,64,128]{2,1,0:T(8,128)}, f32[9,64,128]{2,1,0:T(8,128)S(1)}, u32[]{:S(2)}, u32[]{:S(2)}) collective-permute-start(f32[9,64,128]{2,1,0:T(8,128)} %get-tuple-element.19), channel_id=1, source_target_pairs={{1,0},{2,1},{3,2},{4,3},{5,4},{6,5},{7,6},{9,8},{10,9},{11,10},{12... | collective-permute-start | bytes 884744 | tf_op jit(solution)/shard_map/ppermute | solution.py:487
  9.6 2.7 %shard_map.79 = (f32[9,136,128]{2,1,0:T(8,128)}, f32[9,136,128]{2,1,0:T(8,128)}) custom-call(f32[64,128,128]{2,1,0:T(8,128)} %h_hbm.5, f32[64,128,128]{2,1,0:T(8,128)} %k_hbm.5, f32[64,128,128]{2,1,0:T(8,128)} %bead_hbm.5, s32[64,128,128]{2,1,0:T(8,128)} %birth_hbm.5), custom_call_target="tpu_custom_call" | custom-call | tf_op jit(solution)/shard_map/pallas_call | solution.py:244
  12.3 0.0 collective-permute-done.ylo_ref
  12.3 3.6 %collective-permute-done.1.yhi_ref = f32[9,64,128]{2,1,0:T(8,128)S(1)} collective-permute-done((f32[9,64,128]{2,1,0:T(8,128)}, f32[9,64,128]{2,1,0:T(8,128)S(1)}, u32[]{:S(2)}, u32[]{:S(2)}) %collective-permute-start.1) | collective-permute-done | bytes 294944 | tf_op jit(solution)/shard_map/ppermute | solution.py:487
  15.9 0.7 shard_map.80
  16.6 3.2 %collective-permute-start.2 = (f32[9,136,128]{2,1,0:T(8,128)}, f32[9,136,128]{2,1,0:T(8,128)S(1)}, u32[]{:S(2)}, u32[]{:S(2)}) collective-permute-start(f32[9,136,128]{2,1,0:T(8,128)} %get-tuple-element.23), channel_id=1, source_target_pairs={{0,8},{8,16},{16,24},{24,32},{32,40},{40,48},{48,56},{56,64},{64,7... | collective-permute-start | bytes 1880072 | tf_op jit(solution)/shard_map/ppermute | solution.py:490
  19.8 1.3 %collective-permute-start.3 = (f32[9,136,128]{2,1,0:T(8,128)}, f32[9,136,128]{2,1,0:T(8,128)S(1)}, u32[]{:S(2)}, u32[]{:S(2)}) collective-permute-start(f32[9,136,128]{2,1,0:T(8,128)} %get-tuple-element.24), channel_id=1, source_target_pairs={{8,0},{16,8},{24,16},{32,24},{40,32},{48,40},{56,48},{64,56},{72,6... | collective-permute-start | bytes 1880072 | tf_op jit(solution)/shard_map/ppermute | solution.py:491
  21.1 0.0 copy-done
  21.1 0.1 copy.11
  21.2 0.0 copy-done.1
  21.3 0.1 fusion.3.index_ref
  21.3 26.0 %shard_map.78 = (f32[64,128,128]{2,1,0:T(8,128)}, f32[2,2,136,128]{3,2,1,0:T(8,128)S(1)}, f32[2,2,136,128]{3,2,1,0:T(8,128)S(1)}, f32[2,2,136,128]{3,2,1,0:T(8,1...) custom-call(f32[64,128,128]{2,1,0:T(8,128)} %h_hbm.5, ...), custom_call_target="tpu_custom_call" | custom-call | flops 209715200 | bytes 20971520 | tf_op jit(solution)/shard_map/pallas_call | solution.py:365
  47.3 0.0 collective-permute-done.2.xlo_ref
  47.4 0.0 collective-permute-done.3.xhi_ref
  47.4 10.1 %shard_map.81 = (f32[64,128,128]{2,1,0:T(8,128)}, f32[4096,128]{1,0:T(8,128)S(1)}) custom-call(s32[128,32]{1,0:T(8,128)S(1)} %fusion.3.index_ref, f32[64,128,128]{2,1,0:T(8,128)} %get-tuple-element.20.part_hbm, f32[9,136,128]{2,1,0:T(8,128)S(1)} %collective-permute-done.2.xlo_ref, ...), custom_call_target="tpu_custom_call", output_to_operand_aliasing={{0}: (1, {})} | custom-call | flops 31457280 | bytes 3145728 | tf_op jit(solution)/shard_map/pallas_call | solution.py:453
  57.5 40.9 %all_to_all.5 = f32[128,32,128]{2,1,0:T(8,128)S(1)} all-to-all(f32[128,32,128]{2,1,0:T(8,128)S(1)} %bitcast.23), channel_id=1, replica_groups=mesh['gx'=16,'gy'=8] {'gx','gy'}, dimensions={0} | all-to-all | bytes 4194304 | tf_op jit(solution)/shard_map/all_to_all | solution.py:501
  98.4 1.3 %copy.16 = f32[4096,128]{1,0:T(8,128)} copy(f32[4096,128]{1,0:T(8,128)S(1)} %bitcast.24) | data formatting | bytes 4194304
Async XLA Ops:
  3.1 9.2 %collective-permute-start = (f32[9,64,128]{2,1,0:T(8,128)}, f32[9,64,128]{2,1,0:T(8,128)S(1)}, u32[]{:S(2)}, u32[]{:S(2)}) collective-permute-start(f32[9,64,128]{2,1,0:T(8,128)} %get-tuple-element.18), channel_id=1, source_target_pairs={{0,1},{1,2},{2,3},{3,4},{4,5},{5,6},{6,7},{8,9},{9,10},{10,11},{11... | collective-permute-start | bytes 884744 | tf_op jit(solution)/shard_map/ppermute | solution.py:486
  7.6 13.5 %copy-start = (s32[1,1,128,32]{2,3,1,0:T(8,128)S(1)}, s32[1,1,128,32]{2,3,1,0:T(8,128)}, u32[]{:S(2)}) copy-start(s32[1,1,128,32]{2,3,1,0:T(8,128)} %param.10) | copy-start | bytes 49156
  7.6 13.6 %copy-start.1 = (s32[1,1,128]{2,1,0:T(1,128)S(1)}, s32[1,1,128]{2,1,0:T(1,128)}, u32[]{:S(2)}) copy-start(s32[1,1,128]{2,1,0:T(1,128)} %param.11) | copy-start | bytes 1540
  7.7 8.3 %collective-permute-start.1 = (f32[9,64,128]{2,1,0:T(8,128)}, f32[9,64,128]{2,1,0:T(8,128)S(1)}, u32[]{:S(2)}, u32[]{:S(2)}) collective-permute-start(f32[9,64,128]{2,1,0:T(8,128)} %get-tuple-element.19), channel_id=1, source_target_pairs={{1,0},{2,1},{3,2},{4,3},{5,4},{6,5},{7,6},{9,8},{10,9},{11,10},{12... | collective-permute-start | bytes 884744 | tf_op jit(solution)/shard_map/ppermute | solution.py:487
  16.6 30.8 %collective-permute-start.2 = (f32[9,136,128]{2,1,0:T(8,128)}, f32[9,136,128]{2,1,0:T(8,128)S(1)}, u32[]{:S(2)}, u32[]{:S(2)}) collective-permute-start(f32[9,136,128]{2,1,0:T(8,128)} %get-tuple-element.23), channel_id=1, source_target_pairs={{0,8},{8,16},{16,24},{24,32},{32,40},{40,48},{48,56},{56,64},{64,7... | collective-permute-start | bytes 1880072 | tf_op jit(solution)/shard_map/ppermute | solution.py:490
  19.8 27.5 %collective-permute-start.3 = (f32[9,136,128]{2,1,0:T(8,128)}, f32[9,136,128]{2,1,0:T(8,128)S(1)}, u32[]{:S(2)}, u32[]{:S(2)}) collective-permute-start(f32[9,136,128]{2,1,0:T(8,128)} %get-tuple-element.24), channel_id=1, source_target_pairs={{8,0},{16,8},{24,16},{32,24},{40,32},{48,40},{56,48},{64,56},{72,6... | collective-permute-start | bytes 1880072 | tf_op jit(solution)/shard_map/ppermute | solution.py:491

commit v7 on v6

--- a/solution.py
+++ b/solution.py
@@ -25,7 +25,7 @@
 UNROLL = 4
 ROLL_UP = 2
 ROLL_DOWN = 2
-PUN = 2
+PUN = 8
 RIM = 3 * HALO
 HANDED = ((0, 2), (1, 2), (2, 2), (0, 4), (0, 4), (0, 4), (0, 4))
 MIB = 1024 * 1024
@@ -186,14 +186,15 @@
                 after(n)
 
 
-def slab_scratch(raw_planes, planes, lateral, stack):
+def slab_scratch(raw_planes, planes, lateral, stack, sides=None):
     tiles = (lateral + 2 * LEAD, stack)
     raw = (raw_planes, lateral + 2 * EDGE, stack)
+    rings, acc = [[pltpu.VMEM(tiles, jnp.float32)] * 3] * 2, pltpu.VMEM(tiles, jnp.float32)
     return [
         [pltpu.VMEM(raw, dtype) for dtype in (jnp.float32, jnp.float32, jnp.float32, jnp.int32)],
         [pltpu.VMEM((planes,) + tiles, jnp.float32)] * 6,
-        [[pltpu.VMEM(tiles, jnp.float32)] * 3] * 2,
-        pltpu.VMEM(tiles, jnp.float32),
+        [rings] * sides if sides else rings,
+        [acc] * sides if sides else acc,
     ]
 
 
@@ -385,7 +386,7 @@
 def rim_kernel(index_ref, part_hbm, xlo_ref, xhi_ref, *rest):
     handed, (out_hbm, rows_ref, raw, grids, rings, acc, whole, sem_in, sem_part, sem_out) = rest[:7], rest[7:]
     track, lateral, _ = part_hbm.shape
-    slab = Slab(raw, grids, rings, acc)
+    slab = Slab(raw, grids, None, None)
     inner = pl.ds(EDGE, lateral)
     own = RIM - HALO
 
@@ -415,16 +416,15 @@
         copy.wait()
 
     def finish(x, j, value):
-        at = x - HALO + jnp.where(x >= RIM, track - 2 * own, 0)
+        at = x - HALO + (track - 2 * own if x >= RIM else 0)
         whole[at, slab.natural(j), :] = value - OFFSET
 
-    @pl.loop(0, 2)
-    def _(side):
-        stores = (slab.into(slab.hb), slab.into(slab.ha), finish)
-        for step, (src, store) in enumerate(zip((slab.ha, slab.hb, slab.ha), stores)):
-            first = 1 + step
-            last = 2 * RIM - first - HALO
-            slab.run_step(step, src, store, side * (last - first), (first, first + HALO))
+    sides = [Slab(raw, grids, rings[side], acc[side]) for side in range(2)]
+    stores = (slab.into(slab.hb), slab.into(slab.ha), finish)
+    for step, (src, store) in enumerate(zip((slab.ha, slab.hb, slab.ha), stores)):
+        for side in range(2):
+            first = (1 + step, 2 * RIM - 1 - step - HALO)[side]
+            sides[side].run_step(step, src, store, 0, (first, first + HALO))
 
     outs = []
     for side in range(2):
@@ -438,10 +438,11 @@
     owners, slots = index_ref.shape
     flat = whole.reshape(track * (lateral + 2 * EDGE), LANES)
 
-    @pl.loop(0, owners)
-    def _(o):
-        for k in range(slots):
-            rows_ref[pl.ds(o * slots + k, 1), :] = kelvin(flat[pl.ds(index_ref[o, k], 1), :])
+    @pl.loop(0, owners // 2)
+    def _(i):
+        for o in (2 * i, 2 * i + 1):
+            for k in range(slots):
+                rows_ref[pl.ds(o * slots + k, 1), :] = kelvin(flat[pl.ds(index_ref[o, k], 1), :])
 
     for copy in outs:
         copy.wait()
@@ -459,7 +460,7 @@
         in_specs=[SMEM, HBM] + [VMEM] * 2 + [HBM] * len(HANDED),
         out_specs=(HBM, VMEM),
         input_output_aliases={1: 0},
-        scratch_shapes=slab_scratch(2 * HALO, 2 * RIM, lateral, stack) + [
+        scratch_shapes=slab_scratch(2 * HALO, 2 * RIM, lateral, stack, 2) + [
             pltpu.VMEM((track, lateral + 2 * EDGE, stack), jnp.float32),
             pltpu.SemaphoreType.DMA((len(HANDED), 2)),
             pltpu.SemaphoreType.DMA,

time: 100 us -> 98 us (0.980)
  Pallas kernels: 41.9 us -> 39.9 us
    pallas_call x1, Pallas kernels: 26 us -> 24.5 us  [inner_planes(): pl.pallas_call(inner_kernel, out_shape=(jax.ShapeDtypeStruct(h.shape, jnp...]
  transfers between devices with their start and end apart: 4 -> 4, of which waited for: 1 -> 1; matrix products, arithmetic and copies ran while one was open for 0% -> 0% of each run, Pallas kernels for 29% -> 28%
where the time goes in v7:
time: 98 us; the launch traced here: 97.7 us
  blocking collectives  40.9 us (42%)
  Pallas kernels  39.9 us (41%)
  starting transfers between devices  11 us (11%)
  waiting for transfers between devices  3.64 us (4%)
  local copies, waits for them, and re-layouts  1.43 us (1%)
    all_to_all x1, blocking collectives, per_device(): lax.all_to_all(outgoing, ('gx', 'gy'), split_axis=0, concat_axis=0, tiled...  40.9 us
    pallas_call x1, Pallas kernels, inner_planes(): pl.pallas_call(inner_kernel, out_shape=(jax.ShapeDtypeStruct(h.shape, jnp...  24.5 us
    pallas_call x1, Pallas kernels, rim_and_rows(): pl.pallas_call(rim_kernel, out_shape=(jax.ShapeDtypeStruct(part.shape, jn...  9.65 us
    pallas_call x2, Pallas kernels, strips(): pl.pallas_call(kernel, out_shape=(out, out), in_specs=[HBM] * 4, out_spec...  5.16 us
    ppermute x1, starting transfers between devices, per_device(): ylo = lax.ppermute(to_right, 'gy', shift('gy', 1))  4.51 us
    ppermute x1, waiting for transfers between devices, per_device(): yhi = lax.ppermute(to_left, 'gy', shift('gy', -1))  3.63 us
    ppermute x1, starting transfers between devices, per_device(): xlo = lax.ppermute(to_high, 'gx', shift('gx', 1))  3.24 us
  transfers between devices with their start and end apart: 4, of which 1 were waited for; matrix products, arithmetic and copies ran while one was open for 0% of the time, Pallas kernels for 28%

profile of v7, /device:TPU:1, one launch (start us, length us, event | category | flops | bytes accessed | tf_op | source)
XLA Modules:
  0.0 97.7 jit_solution(4647157865896055865)
XLA Ops:
  0.6 2.5 %shard_map.77 = (f32[9,64,128]{2,1,0:T(8,128)}, f32[9,64,128]{2,1,0:T(8,128)}) custom-call(f32[64,128,128]{2,1,0:T(8,128)} %h_hbm.5, f32[64,128,128]{2,1,0:T(8,128)} %k_hbm.5, f32[64,128,128]{2,1,0:T(8,128)} %bead_hbm.5, s32[64,128,128]{2,1,0:T(8,128)} %birth_hbm.5), custom_call_target="tpu_custom_call" | custom-call | tf_op jit(solution)/shard_map/pallas_call | solution.py:245
  3.1 4.5 %collective-permute-start = (f32[9,64,128]{2,1,0:T(8,128)}, f32[9,64,128]{2,1,0:T(8,128)S(1)}, u32[]{:S(2)}, u32[]{:S(2)}) collective-permute-start(f32[9,64,128]{2,1,0:T(8,128)} %get-tuple-element.18), channel_id=1, source_target_pairs={{0,1},{1,2},{2,3},{3,4},{4,5},{5,6},{6,7},{8,9},{9,10},{10,11},{11... | collective-permute-start | bytes 884744 | tf_op jit(solution)/shard_map/ppermute | solution.py:487
  7.6 0.0 copy-start
  7.6 0.0 copy-start.1
  7.7 1.9 %collective-permute-start.1 = (f32[9,64,128]{2,1,0:T(8,128)}, f32[9,64,128]{2,1,0:T(8,128)S(1)}, u32[]{:S(2)}, u32[]{:S(2)}) collective-permute-start(f32[9,64,128]{2,1,0:T(8,128)} %get-tuple-element.19), channel_id=1, source_target_pairs={{1,0},{2,1},{3,2},{4,3},{5,4},{6,5},{7,6},{9,8},{10,9},{11,10},{12... | collective-permute-start | bytes 884744 | tf_op jit(solution)/shard_map/ppermute | solution.py:488
  9.6 2.7 %shard_map.79 = (f32[9,136,128]{2,1,0:T(8,128)}, f32[9,136,128]{2,1,0:T(8,128)}) custom-call(f32[64,128,128]{2,1,0:T(8,128)} %h_hbm.5, f32[64,128,128]{2,1,0:T(8,128)} %k_hbm.5, f32[64,128,128]{2,1,0:T(8,128)} %bead_hbm.5, s32[64,128,128]{2,1,0:T(8,128)} %birth_hbm.5), custom_call_target="tpu_custom_call" | custom-call | tf_op jit(solution)/shard_map/pallas_call | solution.py:245
  12.3 0.0 collective-permute-done.ylo_ref
  12.3 3.6 %collective-permute-done.1.yhi_ref = f32[9,64,128]{2,1,0:T(8,128)S(1)} collective-permute-done((f32[9,64,128]{2,1,0:T(8,128)}, f32[9,64,128]{2,1,0:T(8,128)S(1)}, u32[]{:S(2)}, u32[]{:S(2)}) %collective-permute-start.1) | collective-permute-done | bytes 294944 | tf_op jit(solution)/shard_map/ppermute | solution.py:488
  15.9 0.7 shard_map.80
  16.6 3.2 %collective-permute-start.2 = (f32[9,136,128]{2,1,0:T(8,128)}, f32[9,136,128]{2,1,0:T(8,128)S(1)}, u32[]{:S(2)}, u32[]{:S(2)}) collective-permute-start(f32[9,136,128]{2,1,0:T(8,128)} %get-tuple-element.23), channel_id=1, source_target_pairs={{0,8},{8,16},{16,24},{24,32},{32,40},{40,48},{48,56},{56,64},{64,7... | collective-permute-start | bytes 1880072 | tf_op jit(solution)/shard_map/ppermute | solution.py:491
  19.8 1.3 %collective-permute-start.3 = (f32[9,136,128]{2,1,0:T(8,128)}, f32[9,136,128]{2,1,0:T(8,128)S(1)}, u32[]{:S(2)}, u32[]{:S(2)}) collective-permute-start(f32[9,136,128]{2,1,0:T(8,128)} %get-tuple-element.24), channel_id=1, source_target_pairs={{8,0},{16,8},{24,16},{32,24},{40,32},{48,40},{56,48},{64,56},{72,6... | collective-permute-start | bytes 1880072 | tf_op jit(solution)/shard_map/ppermute | solution.py:492
  21.1 0.0 copy-done
  21.1 0.1 copy.11
  21.2 0.0 copy-done.1
  21.3 0.1 fusion.3.index_ref
  21.3 24.5 %shard_map.78 = (f32[64,128,128]{2,1,0:T(8,128)}, f32[2,2,136,128]{3,2,1,0:T(8,128)S(1)}, f32[2,2,136,128]{3,2,1,0:T(8,128)S(1)}, f32[2,2,136,128]{3,2,1,0:T(8,1...) custom-call(f32[64,128,128]{2,1,0:T(8,128)} %h_hbm.5, ...), custom_call_target="tpu_custom_call" | custom-call | flops 209715200 | bytes 20971520 | tf_op jit(solution)/shard_map/pallas_call | solution.py:366
  45.8 0.0 collective-permute-done.2.xlo_ref
  45.8 0.0 collective-permute-done.3.xhi_ref
  45.8 9.6 %shard_map.81 = (f32[64,128,128]{2,1,0:T(8,128)}, f32[4096,128]{1,0:T(8,128)S(1)}) custom-call(s32[128,32]{1,0:T(8,128)S(1)} %fusion.3.index_ref, f32[64,128,128]{2,1,0:T(8,128)} %get-tuple-element.20.part_hbm, f32[9,136,128]{2,1,0:T(8,128)S(1)} %collective-permute-done.2.xlo_ref, ...), custom_call_target="tpu_custom_call", output_to_operand_aliasing={{0}: (1, {})} | custom-call | flops 31457280 | bytes 3145728 | tf_op jit(solution)/shard_map/pallas_call | solution.py:454
  55.5 40.9 %all_to_all.5 = f32[128,32,128]{2,1,0:T(8,128)S(1)} all-to-all(f32[128,32,128]{2,1,0:T(8,128)S(1)} %bitcast.23), channel_id=1, replica_groups=mesh['gx'=16,'gy'=8] {'gx','gy'}, dimensions={0} | all-to-all | bytes 4194304 | tf_op jit(solution)/shard_map/all_to_all | solution.py:502
  96.4 1.3 %copy.16 = f32[4096,128]{1,0:T(8,128)} copy(f32[4096,128]{1,0:T(8,128)S(1)} %bitcast.24) | data formatting | bytes 4194304
Async XLA Ops:
  3.1 9.2 %collective-permute-start = (f32[9,64,128]{2,1,0:T(8,128)}, f32[9,64,128]{2,1,0:T(8,128)S(1)}, u32[]{:S(2)}, u32[]{:S(2)}) collective-permute-start(f32[9,64,128]{2,1,0:T(8,128)} %get-tuple-element.18), channel_id=1, source_target_pairs={{0,1},{1,2},{2,3},{3,4},{4,5},{5,6},{6,7},{8,9},{9,10},{10,11},{11... | collective-permute-start | bytes 884744 | tf_op jit(solution)/shard_map/ppermute | solution.py:487
  7.6 13.5 %copy-start = (s32[1,1,128,32]{2,3,1,0:T(8,128)S(1)}, s32[1,1,128,32]{2,3,1,0:T(8,128)}, u32[]{:S(2)}) copy-start(s32[1,1,128,32]{2,3,1,0:T(8,128)} %param.10) | copy-start | bytes 49156
  7.6 13.6 %copy-start.1 = (s32[1,1,128]{2,1,0:T(1,128)S(1)}, s32[1,1,128]{2,1,0:T(1,128)}, u32[]{:S(2)}) copy-start(s32[1,1,128]{2,1,0:T(1,128)} %param.11) | copy-start | bytes 1540
  7.7 8.3 %collective-permute-start.1 = (f32[9,64,128]{2,1,0:T(8,128)}, f32[9,64,128]{2,1,0:T(8,128)S(1)}, u32[]{:S(2)}, u32[]{:S(2)}) collective-permute-start(f32[9,64,128]{2,1,0:T(8,128)} %get-tuple-element.19), channel_id=1, source_target_pairs={{1,0},{2,1},{3,2},{4,3},{5,4},{6,5},{7,6},{9,8},{10,9},{11,10},{12... | collective-permute-start | bytes 884744 | tf_op jit(solution)/shard_map/ppermute | solution.py:488
  16.6 29.2 %collective-permute-start.2 = (f32[9,136,128]{2,1,0:T(8,128)}, f32[9,136,128]{2,1,0:T(8,128)S(1)}, u32[]{:S(2)}, u32[]{:S(2)}) collective-permute-start(f32[9,136,128]{2,1,0:T(8,128)} %get-tuple-element.23), channel_id=1, source_target_pairs={{0,8},{8,16},{16,24},{24,32},{32,40},{40,48},{48,56},{56,64},{64,7... | collective-permute-start | bytes 1880072 | tf_op jit(solution)/shard_map/ppermute | solution.py:491
  19.8 26.0 %collective-permute-start.3 = (f32[9,136,128]{2,1,0:T(8,128)}, f32[9,136,128]{2,1,0:T(8,128)S(1)}, u32[]{:S(2)}, u32[]{:S(2)}) collective-permute-start(f32[9,136,128]{2,1,0:T(8,128)} %get-tuple-element.24), channel_id=1, source_target_pairs={{8,0},{16,8},{24,16},{32,24},{40,32},{48,40},{56,48},{64,56},{72,6... | collective-permute-start | bytes 1880072 | tf_op jit(solution)/shard_map/ppermute | solution.py:492
